TPU v7x, 512 devices: a whole 4x8x8 slice. The times are simulated.
512 devices in a mesh: gx: 32 (over z, x), gy: 16 (over y, core).
Axes of the slice: x: 4, y: 8, z: 8, core: 2. Of those that a mesh axis runs over, the one named last changes fastest.
Arguments:
- nest_state: float32 [4, 48, 192, 6144], P(None, None, 'gx', 'gy'), may hold values from -6 to 6
- stiffness: float32 [48, 192, 6144], P(None, 'gx', 'gy'), may hold values from 0.5 to 2
- parent: float32 [4, 48, 64, 2048], P(None, None, 'gx', 'gy'), may hold values from -6 to 6
- inverse_table: float32 [48, 48], replicated, may hold values from -0.12 to 0.52, as said below
- offsets: int32 [2], replicated, may hold values from -1 to 1
Outputs:
- new_state: float32 [4, 48, 192, 6144], P(None, None, 'gx', 'gy')
- parent_new: float32 [4, 48, 64, 2048], P(None, None, 'gx', 'gy')
Inputs may be any that keep to these rules, and one draw needn't show every extreme that they name: `inverse_table`: close to 0.4 times the identity.
All inputs are finite; a program needn't handle non-finite values.
Results may differ from a plain program's by a relative error of at most 0.0001.
Values sent between devices are 32-bit elements; how exact they have to be, the bound alone decides.
No kernel may reach another device: no remote copies, remote signals or barrier semaphores. Data moves between devices by JAX's collectives and lax.ppermute only.
A program may use at most 128 MiB of HBM per device.

v0:
```python
import jax
import jax.numpy as jnp
from jax import lax
from jax.sharding import PartitionSpec as P

RATIO = 3
SUBSTEPS = 2


GRAD_COEF = 0.25
DIV_COEF = 0.25
COUPLE_COEF = 0.25
LIFT_COEF = 0.5


def padded_2(block, sides, width):
    for axis, dim in sides:
        count = lax.axis_size(axis)
        forward = [(i, i + 1) for i in range(count - 1)]
        backward = [(target, source) for source, target in forward]
        low = lax.ppermute(
            lax.slice_in_dim(block, block.shape[dim] - width, None, axis=dim), axis, forward
        )
        high = lax.ppermute(lax.slice_in_dim(block, 0, width, axis=dim), axis, backward)
        block = jnp.concatenate([low, block, high], axis=dim)
    return block


def level_up(field):
    return jnp.concatenate([field[1:], jnp.zeros_like(field[:1])], 0)


def level_down(field):
    return jnp.concatenate([jnp.zeros_like(field[:1]), field[:-1]], 0)


def vertical_solve(inverse, right_side, stiffness):
    flattened = right_side.reshape(right_side.shape[0], -1)
    first_sweep = jnp.dot(inverse, flattened, precision=lax.Precision.HIGHEST).reshape(
        right_side.shape
    )
    applied = (1.0 + stiffness) * first_sweep - 0.25 * (
        level_up(first_sweep) + level_down(first_sweep)
    )
    leftover = (right_side - applied).reshape(flattened.shape)
    second_sweep = jnp.dot(inverse, leftover, precision=lax.Precision.HIGHEST).reshape(
        right_side.shape
    )
    return first_sweep + second_sweep


def smooth_pair(field):
    along_x = 0.25 * field[..., :-2, :] + 0.5 * field[..., 1:-1, :] + 0.25 * field[..., 2:, :]
    return 0.25 * along_x[..., :-2] + 0.5 * along_x[..., 1:-1] + 0.25 * along_x[..., 2:]


def acoustic(current, pres_pad, edge_zone, stiffness, inverse):
    u_wind, v_wind, w_wind, pressure = (current[0], current[1], current[2], current[3])
    u_next = jnp.where(
        edge_zone, u_wind, u_wind - GRAD_COEF * (pres_pad[:, 2:, 1:-1] - pres_pad[:, :-2, 1:-1])
    )
    v_next = jnp.where(
        edge_zone, v_wind, v_wind - GRAD_COEF * (pres_pad[:, 1:-1, 2:] - pres_pad[:, 1:-1, :-2])
    )
    winds = padded_2(jnp.stack([u_next, v_next]), (("gx", 2), ("gy", 3)), 1)
    divergence = (
        winds[0, :, 2:, 1:-1]
        - winds[0, :, :-2, 1:-1]
        + (winds[1, :, 1:-1, 2:] - winds[1, :, 1:-1, :-2])
    )
    right_side = (
        pressure - DIV_COEF * divergence - COUPLE_COEF * (level_up(w_wind) - level_down(w_wind))
    )
    solved = vertical_solve(inverse, right_side, stiffness)
    p_next = jnp.where(edge_zone, pressure, solved)
    w_next = jnp.where(edge_zone, w_wind, w_wind - LIFT_COEF * (level_up(p_next) - p_next))
    return jnp.stack([u_next, v_next, w_next, p_next])


def boundary_field(coarse, coarse_depth, offsets, tile_x, tile_y, start_x, start_y, nest_x, nest_y):
    coarse_x = tile_x // RATIO + 2 * coarse_depth
    coarse_y = tile_y // RATIO + 2 * coarse_depth
    first_x = start_x // RATIO - coarse_depth
    first_y = start_y // RATIO - coarse_depth
    clip_x = jnp.clip(first_x + jnp.arange(coarse_x), 0, nest_x // RATIO - 1) - first_x
    clip_y = jnp.clip(first_y + jnp.arange(coarse_y), 0, nest_y // RATIO - 1) - first_y
    fixed = jnp.take(jnp.take(coarse, clip_x, axis=2), clip_y, axis=3)
    fine = jnp.repeat(jnp.repeat(fixed, RATIO, axis=2), RATIO, axis=3)
    zero_start = jnp.zeros((), jnp.int32)
    begin_x = RATIO * coarse_depth + RATIO * offsets[0]
    begin_y = RATIO * coarse_depth + RATIO * offsets[1]
    return lax.dynamic_slice(
        fine, (zero_start, zero_start, begin_x, begin_y), (4, coarse.shape[1], tile_x, tile_y)
    )


def edge_mask(start_x, start_y, size_x, size_y, extension, nest_x, nest_y):
    global_x = start_x - extension + jnp.arange(size_x)
    global_y = start_y - extension + jnp.arange(size_y)
    return ((global_x < RATIO) | (global_x >= nest_x - RATIO))[:, None] | (
        (global_y < RATIO) | (global_y >= nest_y - RATIO)
    )[None, :]


def per_device(nest_state, stiffness, parent, inverse_table, offsets):
    levels = nest_state.shape[1]
    tile_x, tile_y = (nest_state.shape[2], nest_state.shape[3])
    nest_x = tile_x * lax.axis_size("gx")
    nest_y = tile_y * lax.axis_size("gy")
    start_x = lax.axis_index("gx") * tile_x
    start_y = lax.axis_index("gy") * tile_y
    move_x = RATIO * offsets[0]
    move_y = RATIO * offsets[1]
    coarse_depth = (2 * RATIO - 1) // RATIO
    coarse = padded_2(parent, (("gx", 2), ("gy", 3)), coarse_depth)
    boundary = boundary_field(
        coarse, coarse_depth, offsets, tile_x, tile_y, start_x, start_y, nest_x, nest_y
    )
    zero_start = jnp.zeros((), jnp.int32)
    begin_x = RATIO + move_x
    begin_y = RATIO + move_y
    padded = padded_2(nest_state, (("gx", 2), ("gy", 3)), RATIO)
    moved = lax.dynamic_slice(
        padded, (zero_start, zero_start, begin_x, begin_y), (4, levels, tile_x, tile_y)
    )
    edge_zone = edge_mask(start_x, start_y, tile_x, tile_y, 0, nest_x, nest_y)
    current = jnp.where(edge_zone, boundary, moved)
    for substep in range(SUBSTEPS):
        pres_pad = padded_2(current[3], (("gx", 1), ("gy", 2)), 1)
        current = acoustic(current, pres_pad, edge_zone, stiffness, inverse_table)
    parent_x = tile_x // RATIO
    parent_y = tile_y // RATIO
    total_x = nest_x // RATIO
    total_y = nest_y // RATIO
    blocks = current.reshape(4, levels, parent_x, RATIO, parent_y, RATIO).mean(axis=(3, 5))
    block_x = start_x // RATIO + jnp.arange(parent_x)
    block_y = start_y // RATIO + jnp.arange(parent_y)
    interior = (
        ((block_x >= 1) & (block_x <= total_x - 2))[:, None]
        & ((block_y >= 1) & (block_y <= total_y - 2))[None, :]
    ).astype(jnp.float32)
    weight_pad = padded_2(blocks * interior, (("gx", 2), ("gy", 3)), 2)
    wide_x = start_x // RATIO - 2 + jnp.arange(parent_x + 4)
    wide_y = start_y // RATIO - 2 + jnp.arange(parent_y + 4)
    inner_pad = (
        ((wide_x >= 1) & (wide_x <= total_x - 2))[:, None]
        & ((wide_y >= 1) & (wide_y <= total_y - 2))[None, :]
    ).astype(jnp.float32)
    window_x = 1 - offsets[0]
    window_y = 1 - offsets[1]
    weight_win = lax.dynamic_slice(
        weight_pad,
        (zero_start, zero_start, window_x, window_y),
        (4, levels, parent_x + 2, parent_y + 2),
    )
    inner_win = lax.dynamic_slice(inner_pad, (window_x, window_y), (parent_x + 2, parent_y + 2))
    numerator = smooth_pair(weight_win)
    denominator = smooth_pair(inner_win)
    centre = inner_win[1:-1, 1:-1] > 0
    parent_new = jnp.where(centre, numerator / jnp.where(centre, denominator, 1.0), parent)
    return (current, parent_new)


def solution(mesh):
    return jax.shard_map(
        per_device,
        mesh=mesh,
        in_specs=(
            P(None, None, "gx", "gy"),
            P(None, "gx", "gy"),
            P(None, None, "gx", "gy"),
            P(),
            P(),
        ),
        out_specs=(P(None, None, "gx", "gy"), P(None, None, "gx", "gy")),
        check_vma=False,
    )
```

profile of v0, /device:TPU:223, one launch (start us, length us, event | category | flops | bytes accessed | tf_op | source)
XLA Modules:
  0.0 260.1 jit_solution(1427839275863061449)
XLA Ops:
  1.9 5.1 %collective-permute-start = (f32[4,48,1,128]{3,1,2,0:T(8,128)S(1)}, f32[4,48,1,128]{3,1,2,0:T(8,128)S(1)}, u32[]{:S(2)}, u32[]{:S(2)}) collective-permute-start(f32[4,48,1,128]{3,1,2,0:T(8,128)S(1)} %copy.466), channel_id=1, source_target_pairs={{0,16},{16,32},{32,48},{48,64},{64,80},{80,96},{96,112},{112,128},... | collective-permute-start | bytes 294920 | tf_op jit(solution)/shard_map/ppermute | solution.py:21
  7.0 2.1 collective-permute-start.1
  9.1 2.8 %fusion.54 = (f32[4,48,3,384]{3,1,2,0:T(8,128)}, f32[4,48,3,384]{3,1,2,0:T(8,128)}) fusion(f32[4,48,6,384]{3,1,2,0:T(8,128)} %param.5), kind=kLoop, calls=%fused_computation.192 | loop fusion | bytes 3538944 | tf_op jit(solution)/shard_map/slice | solution.py:24
  11.9 6.7 %collective-permute-start.4 = (f32[4,48,3,384]{3,1,2,0:T(8,128)}, f32[4,48,3,384]{3,1,2,0:T(8,128)}, u32[]{:S(2)}, u32[]{:S(2)}) collective-permute-start(f32[4,48,3,384]{3,1,2,0:T(8,128)} %get-tuple-element.25), channel_id=1, source_target_pairs={{0,16},{16,32},{32,48},{48,64},{64,80},{80,96},{96,112},{112,128},... | collective-permute-start | bytes 2654216 | tf_op jit(solution)/shard_map/ppermute | solution.py:21
  18.6 1.9 collective-permute-start.5
  21.6 5.8 %collective-permute-start.2 = (f32[4,48,4,1]{3,1,2,0:T(8,128)S(1)}, f32[4,48,4,1]{3,1,2,0:T(8,128)S(1)}, u32[]{:S(2)}, u32[]{:S(2)}) collective-permute-start(f32[4,48,4,1]{3,1,2,0:T(8,128)S(1)} %get-tuple-element.58), channel_id=1, source_target_pairs={{0,1},{1,2},{2,3},{3,4},{4,5},{5,6},{6,7},{7,8},{8,9},{9,10},{10,1... | collective-permute-start | bytes 9224 | tf_op jit(solution)/shard_map/ppermute | solution.py:21
  27.5 1.9 collective-permute-start.3
  33.3 4.8 %collective-permute-done.3 = f32[4,48,4,1]{3,1,2,0:T(8,128)S(1)} collective-permute-done((f32[4,48,4,1]{3,1,2,0:T(8,128)S(1)}, f32[4,48,4,1]{3,1,2,0:T(8,128)S(1)}, u32[]{:S(2)}, u32[]{:S(2)}) %collective-permute-start.3) | collective-permute-done | bytes 3104 | tf_op jit(solution)/shard_map/ppermute | solution.py:24
  47.2 6.7 %collective-permute-start.6 = (f32[4,48,12,3]{1,0,3,2:T(4,128)S(1)}, f32[4,48,12,3]{1,0,3,2:T(4,128)S(1)}, u32[]{:S(2)}, u32[]{:S(2)}) collective-permute-start(f32[4,48,12,3]{1,0,3,2:T(4,128)S(1)} %copy.417), channel_id=1, source_target_pairs={{0,1},{1,2},{2,3},{3,4},{4,5},{5,6},{6,7},{7,8},{8,9},{9,10},{10,1... | collective-permute-start | bytes 82952 | tf_op jit(solution)/shard_map/ppermute | solution.py:21
  54.4 1.9 collective-permute-start.7
  56.8 5.0 %broadcast_in_dim.63 = f32[4,48,12,130,3]{1,0,4,3,2:T(4,128)} broadcast(f32[4,48,12,130]{1,0,3,2:T(4,128)S(1)} %bitcast.139), dimensions={0,1,2,3} | broadcast | bytes 4792320 | tf_op jit(solution)/shard_map/broadcast_in_dim | solution.py:88
  61.7 4.9 %constant_dynamic-slice_fusion = f32[4,48,6,384]{1,0,3,2:T(4,128)} fusion(f32[4,48,12,390]{1,0,3,2:T(4,128)} %bitcast.124, s32[]{:T(128)S(6)} %select_n.119, s32[]{:T(128)S(6)} %select_n.120), kind=kLoop, calls=%fused_computation.164 | loop fusion | bytes 3538952 | tf_op jit(solution)/shard_map/dynamic_slice | solution.py:92
  66.6 5.8 %copy.416 = f32[4,48,6,384]{3,1,2,0:T(8,128)} copy(f32[4,48,6,384]{1,0,3,2:T(4,128)} %constant_dynamic-slice_fusion) | data formatting | bytes 3538944
  72.9 2.4 copy.368
  75.3 3.3 %fusion.2 = f32[4,48,6,384]{3,1,2,0:T(8,128)S(1)} fusion(f32[4,48,6,384]{3,1,2,0:T(8,128)} %copy.416, s32[]{:T(128)S(6)} %select_n.119, s32[]{:T(128)S(6)} %select_n.120, f32[4,48,12,3]{3,1,2,0:T(8,128)S(1)} %copy.367, f32[4,48,12,384]{3,1,2,0:T(8,128)} %copy-done.3, f32[4,48,12,3]{3,1,2,0:T(8,128)} %copy.368, pred[6,384]{1,0:T(8,128)(4,1)S(1)} %broadcast_or_fusion), kind=kLoop, calls=%fused_computation.8 | loop fusion | flops 1327104 | bytes 7135496 | tf_op jit(solution)/shard_map/jit(_where)/select_n | solution.py:127
  78.6 2.5 collective-permute-start.9
  81.1 2.8 %collective-permute-start.8 = (f32[48,1,384]{2,0,1:T(8,128)S(1)}, f32[48,1,384]{2,0,1:T(8,128)S(1)}, u32[]{:S(2)}, u32[]{:S(2)}) collective-permute-start(f32[48,1,384]{2,0,1:T(8,128)S(1)} %get-tuple-element.56), channel_id=1, source_target_pairs={{16,0},{32,16},{48,32},{64,48},{80,64},{96,80},{112,96},{128,112},... | collective-permute-start | bytes 221192 | tf_op jit(solution)/shard_map/ppermute | solution.py:24
  84.5 5.4 %collective-permute-done.8 = f32[48,1,384]{2,0,1:T(8,128)S(1)} collective-permute-done((f32[48,1,384]{2,0,1:T(8,128)S(1)}, f32[48,1,384]{2,0,1:T(8,128)S(1)}, u32[]{:S(2)}, u32[]{:S(2)}) %collective-permute-start.8) | collective-permute-done | bytes 73760 | tf_op jit(solution)/shard_map/ppermute | solution.py:24
  90.2 3.0 %collective-permute-start.10 = (f32[48,8,1]{2,1,0:T(8,128)S(1)}, f32[48,8,1]{2,1,0:T(8,128)S(1)}, u32[]{:S(2)}, u32[]{:S(2)}) collective-permute-start(f32[48,8,1]{2,1,0:T(8,128)S(1)} %get-tuple-element.46), channel_id=1, source_target_pairs={{1,0},{2,1},{3,2},{4,3},{5,4},{6,5},{7,6},{8,7},{9,8},{10,9},{11,1... | collective-permute-start | bytes 4616 | tf_op jit(solution)/shard_map/ppermute | solution.py:24
  93.2 4.3 %collective-permute-start.11 = (f32[48,8,1]{2,1,0:T(8,128)S(1)}, f32[48,8,1]{2,1,0:T(8,128)S(1)}, u32[]{:S(2)}, u32[]{:S(2)}) collective-permute-start(f32[48,8,1]{2,1,0:T(8,128)S(1)} %get-tuple-element.47), channel_id=1, source_target_pairs={{0,1},{1,2},{2,3},{3,4},{4,5},{5,6},{6,7},{7,8},{8,9},{9,10},{10,1... | collective-permute-start | bytes 4616 | tf_op jit(solution)/shard_map/ppermute | solution.py:21
  101.6 1.9 collective-permute-start.13
  103.5 3.5 %collective-permute-start.12 = (f32[2,48,1,384]{3,1,2,0:T(8,128)S(1)}, f32[2,48,1,384]{3,1,2,0:T(8,128)S(1)}, u32[]{:S(2)}, u32[]{:S(2)}) collective-permute-start(f32[2,48,1,384]{3,1,2,0:T(8,128)S(1)} %get-tuple-element.38), channel_id=1, source_target_pairs={{16,0},{32,16},{48,32},{64,48},{80,64},{96,80},{112,96},{128,112},... | collective-permute-start | bytes 442376 | tf_op jit(solution)/shard_map/ppermute | solution.py:24
  109.0 5.1 %collective-permute-done.12 = f32[2,48,1,384]{3,1,2,0:T(8,128)S(1)} collective-permute-done((f32[2,48,1,384]{3,1,2,0:T(8,128)S(1)}, f32[2,48,1,384]{3,1,2,0:T(8,128)S(1)}, u32[]{:S(2)}, u32[]{:S(2)}) %collective-permute-start.12) | collective-permute-done | bytes 147488 | tf_op jit(solution)/shard_map/ppermute | solution.py:24
  114.7 2.8 %collective-permute-start.14 = (f32[2,48,8,1]{3,2,1,0:T(8,128)S(1)}, f32[2,48,8,1]{3,2,1,0:T(8,128)S(1)}, u32[]{:S(2)}, u32[]{:S(2)}) collective-permute-start(f32[2,48,8,1]{3,2,1,0:T(8,128)S(1)} %get-tuple-element.34), channel_id=1, source_target_pairs={{1,0},{2,1},{3,2},{4,3},{5,4},{6,5},{7,6},{8,7},{9,8},{10,9},{11,1... | collective-permute-start | bytes 9224 | tf_op jit(solution)/shard_map/ppermute | solution.py:24
  117.5 4.5 %collective-permute-start.15 = (f32[2,48,8,1]{3,2,1,0:T(8,128)S(1)}, f32[2,48,8,1]{3,2,1,0:T(8,128)S(1)}, u32[]{:S(2)}, u32[]{:S(2)}) collective-permute-start(f32[2,48,8,1]{3,2,1,0:T(8,128)S(1)} %get-tuple-element.35), channel_id=1, source_target_pairs={{0,1},{1,2},{2,3},{3,4},{4,5},{5,6},{6,7},{7,8},{8,9},{9,10},{10,1... | collective-permute-start | bytes 9224 | tf_op jit(solution)/shard_map/ppermute | solution.py:21
  122.0 3.5 %collective-permute-done.14 = f32[2,48,8,1]{3,2,1,0:T(8,128)S(1)} collective-permute-done((f32[2,48,8,1]{3,2,1,0:T(8,128)S(1)}, f32[2,48,8,1]{3,2,1,0:T(8,128)S(1)}, u32[]{:S(2)}, u32[]{:S(2)}) %collective-permute-start.14) | collective-permute-done | bytes 3104 | tf_op jit(solution)/shard_map/ppermute | solution.py:24
  135.5 1.9 collective-permute-start.17
  137.4 3.4 %collective-permute-start.16 = (f32[48,1,384]{2,0,1:T(8,128)S(1)}, f32[48,1,384]{2,0,1:T(8,128)S(1)}, u32[]{:S(2)}, u32[]{:S(2)}) collective-permute-start(f32[48,1,384]{2,0,1:T(8,128)S(1)} %get-tuple-element.52), channel_id=1, source_target_pairs={{16,0},{32,16},{48,32},{64,48},{80,64},{96,80},{112,96},{128,112},... | collective-permute-start | bytes 221192 | tf_op jit(solution)/shard_map/ppermute | solution.py:24
  141.5 5.2 %collective-permute-done.16 = f32[48,1,384]{2,0,1:T(8,128)S(1)} collective-permute-done((f32[48,1,384]{2,0,1:T(8,128)S(1)}, f32[48,1,384]{2,0,1:T(8,128)S(1)}, u32[]{:S(2)}, u32[]{:S(2)}) %collective-permute-start.16) | collective-permute-done | bytes 73760 | tf_op jit(solution)/shard_map/ppermute | solution.py:24
  147.0 2.7 %collective-permute-start.18 = (f32[48,8,1]{2,1,0:T(8,128)S(1)}, f32[48,8,1]{2,1,0:T(8,128)S(1)}, u32[]{:S(2)}, u32[]{:S(2)}) collective-permute-start(f32[48,8,1]{2,1,0:T(8,128)S(1)} %get-tuple-element.42), channel_id=1, source_target_pairs={{1,0},{2,1},{3,2},{4,3},{5,4},{6,5},{7,6},{8,7},{9,8},{10,9},{11,1... | collective-permute-start | bytes 4616 | tf_op jit(solution)/shard_map/ppermute | solution.py:24
  149.7 5.3 %collective-permute-start.19 = (f32[48,8,1]{2,1,0:T(8,128)S(1)}, f32[48,8,1]{2,1,0:T(8,128)S(1)}, u32[]{:S(2)}, u32[]{:S(2)}) collective-permute-start(f32[48,8,1]{2,1,0:T(8,128)S(1)} %get-tuple-element.43), channel_id=1, source_target_pairs={{0,1},{1,2},{2,3},{3,4},{4,5},{5,6},{6,7},{7,8},{8,9},{9,10},{10,1... | collective-permute-start | bytes 4616 | tf_op jit(solution)/shard_map/ppermute | solution.py:21
  162.6 3.4 %collective-permute-start.20 = (f32[2,48,1,384]{3,1,2,0:T(8,128)}, f32[2,48,1,384]{3,1,2,0:T(8,128)}, u32[]{:S(2)}, u32[]{:S(2)}) collective-permute-start(f32[2,48,1,384]{3,1,2,0:T(8,128)} %get-tuple-element.36), channel_id=1, source_target_pairs={{16,0},{32,16},{48,32},{64,48},{80,64},{96,80},{112,96},{128,112},... | collective-permute-start | bytes 442376 | tf_op jit(solution)/shard_map/ppermute | solution.py:24
  170.0 3.3 %collective-permute-done.20 = f32[2,48,1,384]{3,1,2,0:T(8,128)} collective-permute-done((f32[2,48,1,384]{3,1,2,0:T(8,128)}, f32[2,48,1,384]{3,1,2,0:T(8,128)}, u32[]{:S(2)}, u32[]{:S(2)}) %collective-permute-start.20) | collective-permute-done | bytes 147488 | tf_op jit(solution)/shard_map/ppermute | solution.py:24
  175.7 2.2 collective-permute-start.22
  178.0 5.5 %collective-permute-start.23 = (f32[2,48,8,1]{3,2,1,0:T(8,128)}, f32[2,48,8,1]{3,2,1,0:T(8,128)}, u32[]{:S(2)}, u32[]{:S(2)}) collective-permute-start(f32[2,48,8,1]{3,2,1,0:T(8,128)} %get-tuple-element.31), channel_id=1, source_target_pairs={{0,1},{1,2},{2,3},{3,4},{4,5},{5,6},{6,7},{7,8},{8,9},{9,10},{10,1... | collective-permute-start | bytes 9224 | tf_op jit(solution)/shard_map/ppermute | solution.py:21
  187.2 2.9 %stack.45 = f32[1,48,2,3,128,3]{1,5,4,3,2,0:T(4,128)} reshape(f32[48,6,384]{0,2,1:T(8,128)} %copy.405) | data formatting | bytes 884736 | tf_op jit(solution)/shard_map/stack | solution.py:77
  190.1 2.8 %stack.46 = f32[1,48,2,3,128,3]{1,5,4,3,2,0:T(4,128)} reshape(f32[48,6,384]{0,2,1:T(8,128)} %copy.406) | data formatting | bytes 884736 | tf_op jit(solution)/shard_map/stack | solution.py:77
  193.0 2.5 pad_maximum_fusion.7
  213.7 2.0 copy_select_fusion
  215.7 3.3 %copy.408 = f32[1,48,6,384]{1,0,3,2:T(1,128)S(1)} copy(f32[1,48,6,384]{3,1,2,0:T(8,128)} %copy_select_fusion) | data formatting | bytes 884736 | tf_op jit(solution)/shard_map/jit(_where)/select_n | solution.py:75
  220.5 6.2 %maximum_reduce_fusion = f32[4,48,2,128]{1,3,2,0:T(8,128)S(1)} fusion(f32[1,48,2,3,128,3]{1,5,4,3,2,0:T(4,128)S(1)} %copy.409, f32[1,48,2,3,128,3]{1,5,4,3,2,0:T(4,128)} %stack.47, f32[1,48,2,3,128,3]{1,5,4,3,2,0:T(4,128)S(1)} %copy-done.13, f32[1,48,2,3,128,3]{1,5,4,3,2,0:T(4,128)S(1)} %copy-done.12), kind=kLoop, calls=%fused_computation.2 | loop fusion | flops 1720320 | bytes 1966080 | tf_op jit(solution)/shard_map/reduce_sum | solution.py:135
  226.8 2.4 collective-permute-start.24
  229.2 3.0 %collective-permute-start.25 = (f32[4,48,2,128]{1,3,2,0:T(8,128)S(1)}, f32[4,48,2,128]{1,3,2,0:T(8,128)S(1)}, u32[]{:S(2)}, u32[]{:S(2)}) collective-permute-start(f32[4,48,2,128]{1,3,2,0:T(8,128)S(1)} %broadcast_multiply_fusion), channel_id=1, source_target_pairs={{16,0},{32,16},{48,32},{64,48},{80,64},{96,80},{112,96},{128,112},... | collective-permute-start | bytes 589832 | tf_op jit(solution)/shard_map/ppermute | solution.py:24
  232.3 8.1 %collective-permute-done.24 = f32[4,48,2,128]{1,3,2,0:T(8,128)S(1)} collective-permute-done((f32[4,48,2,128]{1,3,2,0:T(8,128)S(1)}, f32[4,48,2,128]{1,3,2,0:T(8,128)S(1)}, u32[]{:S(2)}, u32[]{:S(2)}) %collective-permute-start.24) | collective-permute-done | bytes 196640 | tf_op jit(solution)/shard_map/ppermute | solution.py:21
  240.4 5.0 %collective-permute-done.25 = f32[4,48,2,128]{1,3,2,0:T(8,128)S(1)} collective-permute-done((f32[4,48,2,128]{1,3,2,0:T(8,128)S(1)}, f32[4,48,2,128]{1,3,2,0:T(8,128)S(1)}, u32[]{:S(2)}, u32[]{:S(2)}) %collective-permute-start.25) | collective-permute-done | bytes 196640 | tf_op jit(solution)/shard_map/ppermute | solution.py:24
  245.4 5.3 %collective-permute-start.26 = (f32[4,48,6,2]{1,2,3,0:T(8,128)S(1)}, f32[4,48,6,2]{1,2,3,0:T(8,128)S(1)}, u32[]{:S(2)}, u32[]{:S(2)}) collective-permute-start(f32[4,48,6,2]{1,2,3,0:T(8,128)S(1)} %copy.410), channel_id=1, source_target_pairs={{0,1},{1,2},{2,3},{3,4},{4,5},{5,6},{6,7},{7,8},{8,9},{9,10},{10,1... | collective-permute-start | bytes 27656 | tf_op jit(solution)/shard_map/ppermute | solution.py:21
  250.7 1.9 collective-permute-start.27
  254.0 3.1 %collective-permute-done.27 = f32[4,48,6,2]{1,2,3,0:T(8,128)S(1)} collective-permute-done((f32[4,48,6,2]{1,2,3,0:T(8,128)S(1)}, f32[4,48,6,2]{1,2,3,0:T(8,128)S(1)}, u32[]{:S(2)}, u32[]{:S(2)}) %collective-permute-start.27) | collective-permute-done | bytes 9248 | tf_op jit(solution)/shard_map/ppermute | solution.py:24
  (188 shorter events, 72.6 us)
Async XLA Ops:
  0.6 127.6 %copy-start = (f32[48,48]{1,0:T(8,128)S(1)}, f32[48,48]{1,0:T(8,128)}, u32[]{:S(2)}) copy-start(f32[48,48]{1,0:T(8,128)} %param.8) | copy-start | bytes 27652
  1.9 19.5 %collective-permute-start = (f32[4,48,1,128]{3,1,2,0:T(8,128)S(1)}, f32[4,48,1,128]{3,1,2,0:T(8,128)S(1)}, u32[]{:S(2)}, u32[]{:S(2)}) collective-permute-start(f32[4,48,1,128]{3,1,2,0:T(8,128)S(1)} %copy.466), channel_id=1, source_target_pairs={{0,16},{16,32},{32,48},{48,64},{64,80},{80,96},{96,112},{112,128},... | collective-permute-start | bytes 294920 | tf_op jit(solution)/shard_map/ppermute | solution.py:21
  7.0 13.7 %copy-start.24 = (s32[2]{0:T(128)S(1)}, s32[2]{0:T(128)}, u32[]{:S(2)}) copy-start(s32[2]{0:T(128)} %param.9) | copy-start | bytes 28
  7.0 14.4 %copy-start.18 = (f32[4,48,2,128]{3,2,1,0:T(2,128)S(1)}, f32[4,48,2,128]{3,2,1,0:T(2,128)}, u32[]{:S(2)}) copy-start(f32[4,48,2,128]{3,2,1,0:T(2,128)} %param.7) | copy-start | bytes 589828
  7.0 14.4 %collective-permute-start.1 = (f32[4,48,1,128]{3,1,2,0:T(8,128)S(1)}, f32[4,48,1,128]{3,1,2,0:T(8,128)S(1)}, u32[]{:S(2)}, u32[]{:S(2)}) collective-permute-start(f32[4,48,1,128]{3,1,2,0:T(8,128)S(1)} %copy.467), channel_id=1, source_target_pairs={{16,0},{32,16},{48,32},{64,48},{80,64},{96,80},{112,96},{128,112},... | collective-permute-start | bytes 294920 | tf_op jit(solution)/shard_map/ppermute | solution.py:24
  11.9 30.1 %collective-permute-start.4 = (f32[4,48,3,384]{3,1,2,0:T(8,128)}, f32[4,48,3,384]{3,1,2,0:T(8,128)}, u32[]{:S(2)}, u32[]{:S(2)}) collective-permute-start(f32[4,48,3,384]{3,1,2,0:T(8,128)} %get-tuple-element.25), channel_id=1, source_target_pairs={{0,16},{16,32},{32,48},{48,64},{64,80},{80,96},{96,112},{112,128},... | collective-permute-start | bytes 2654216 | tf_op jit(solution)/shard_map/ppermute | solution.py:21
  18.6 25.2 %collective-permute-start.5 = (f32[4,48,3,384]{3,1,2,0:T(8,128)}, f32[4,48,3,384]{3,1,2,0:T(8,128)}, u32[]{:S(2)}, u32[]{:S(2)}) collective-permute-start(f32[4,48,3,384]{3,1,2,0:T(8,128)} %get-tuple-element.24), channel_id=1, source_target_pairs={{16,0},{32,16},{48,32},{64,48},{80,64},{96,80},{112,96},{128,112},... | collective-permute-start | bytes 2654216 | tf_op jit(solution)/shard_map/ppermute | solution.py:24
  21.6 11.7 %collective-permute-start.2 = (f32[4,48,4,1]{3,1,2,0:T(8,128)S(1)}, f32[4,48,4,1]{3,1,2,0:T(8,128)S(1)}, u32[]{:S(2)}, u32[]{:S(2)}) collective-permute-start(f32[4,48,4,1]{3,1,2,0:T(8,128)S(1)} %get-tuple-element.58), channel_id=1, source_target_pairs={{0,1},{1,2},{2,3},{3,4},{4,5},{5,6},{6,7},{7,8},{8,9},{9,10},{10,1... | collective-permute-start | bytes 9224 | tf_op jit(solution)/shard_map/ppermute | solution.py:21
  27.5 10.7 %collective-permute-start.3 = (f32[4,48,4,1]{3,1,2,0:T(8,128)S(1)}, f32[4,48,4,1]{3,1,2,0:T(8,128)S(1)}, u32[]{:S(2)}, u32[]{:S(2)}) collective-permute-start(f32[4,48,4,1]{3,1,2,0:T(8,128)S(1)} %get-tuple-element.59), channel_id=1, source_target_pairs={{1,0},{2,1},{3,2},{4,3},{5,4},{6,5},{7,6},{8,7},{9,8},{10,9},{11,1... | collective-permute-start | bytes 9224 | tf_op jit(solution)/shard_map/ppermute | solution.py:24
  41.7 1.7 copy-start.9
  45.0 1.8 copy-start.3
  47.2 25.2 %collective-permute-start.6 = (f32[4,48,12,3]{1,0,3,2:T(4,128)S(1)}, f32[4,48,12,3]{1,0,3,2:T(4,128)S(1)}, u32[]{:S(2)}, u32[]{:S(2)}) collective-permute-start(f32[4,48,12,3]{1,0,3,2:T(4,128)S(1)} %copy.417), channel_id=1, source_target_pairs={{0,1},{1,2},{2,3},{3,4},{4,5},{5,6},{6,7},{7,8},{8,9},{9,10},{10,1... | collective-permute-start | bytes 82952 | tf_op jit(solution)/shard_map/ppermute | solution.py:21
  54.4 18.5 %collective-permute-start.7 = (f32[4,48,12,3]{1,0,3,2:T(4,128)S(1)}, f32[4,48,12,3]{1,0,3,2:T(4,128)}, u32[]{:S(2)}, u32[]{:S(2)}) collective-permute-start(f32[4,48,12,3]{1,0,3,2:T(4,128)S(1)} %copy.418), channel_id=1, source_target_pairs={{1,0},{2,1},{3,2},{4,3},{5,4},{6,5},{7,6},{8,7},{9,8},{10,9},{11,1... | collective-permute-start | bytes 82952 | tf_op jit(solution)/shard_map/ppermute | solution.py:24
  78.6 22.7 %copy-start.7 = (f32[48,6,384]{2,0,1:T(8,128)}, f32[48,6,384]{2,0,1:T(8,128)S(1)}, u32[]{:S(2)}) copy-start(f32[48,6,384]{2,0,1:T(8,128)S(1)} %slice_bitcast_fusion.5) | copy-start | bytes 1327108
  78.6 5.8 %collective-permute-start.9 = (f32[48,1,384]{2,0,1:T(8,128)S(1)}, f32[48,1,384]{2,0,1:T(8,128)S(1)}, u32[]{:S(2)}, u32[]{:S(2)}) collective-permute-start(f32[48,1,384]{2,0,1:T(8,128)S(1)} %get-tuple-element.57), channel_id=1, source_target_pairs={{0,16},{16,32},{32,48},{48,64},{64,80},{80,96},{96,112},{112,128},... | collective-permute-start | bytes 221192 | tf_op jit(solution)/shard_map/ppermute | solution.py:21
  81.1 8.8 %collective-permute-start.8 = (f32[48,1,384]{2,0,1:T(8,128)S(1)}, f32[48,1,384]{2,0,1:T(8,128)S(1)}, u32[]{:S(2)}, u32[]{:S(2)}) collective-permute-start(f32[48,1,384]{2,0,1:T(8,128)S(1)} %get-tuple-element.56), channel_id=1, source_target_pairs={{16,0},{32,16},{48,32},{64,48},{80,64},{96,80},{112,96},{128,112},... | collective-permute-start | bytes 221192 | tf_op jit(solution)/shard_map/ppermute | solution.py:24
  90.2 8.8 %collective-permute-start.10 = (f32[48,8,1]{2,1,0:T(8,128)S(1)}, f32[48,8,1]{2,1,0:T(8,128)S(1)}, u32[]{:S(2)}, u32[]{:S(2)}) collective-permute-start(f32[48,8,1]{2,1,0:T(8,128)S(1)} %get-tuple-element.46), channel_id=1, source_target_pairs={{1,0},{2,1},{3,2},{4,3},{5,4},{6,5},{7,6},{8,7},{9,8},{10,9},{11,1... | collective-permute-start | bytes 4616 | tf_op jit(solution)/shard_map/ppermute | solution.py:24
  93.2 6.9 %collective-permute-start.11 = (f32[48,8,1]{2,1,0:T(8,128)S(1)}, f32[48,8,1]{2,1,0:T(8,128)S(1)}, u32[]{:S(2)}, u32[]{:S(2)}) collective-permute-start(f32[48,8,1]{2,1,0:T(8,128)S(1)} %get-tuple-element.47), channel_id=1, source_target_pairs={{0,1},{1,2},{2,3},{3,4},{4,5},{5,6},{6,7},{7,8},{8,9},{9,10},{10,1... | collective-permute-start | bytes 4616 | tf_op jit(solution)/shard_map/ppermute | solution.py:21
  101.5 26.3 %copy-start.4 = (f32[48,6,384]{2,0,1:T(8,128)}, f32[48,6,384]{2,0,1:T(8,128)S(1)}, u32[]{:S(2)}) copy-start(f32[48,6,384]{2,0,1:T(8,128)S(1)} %get-tuple-element.20) | copy-start | bytes 1327108
  101.6 7.3 %collective-permute-start.13 = (f32[2,48,1,384]{3,1,2,0:T(8,128)S(1)}, f32[2,48,1,384]{3,1,2,0:T(8,128)S(1)}, u32[]{:S(2)}, u32[]{:S(2)}) collective-permute-start(f32[2,48,1,384]{3,1,2,0:T(8,128)S(1)} %get-tuple-element.39), channel_id=1, source_target_pairs={{0,16},{16,32},{32,48},{48,64},{64,80},{80,96},{96,112},{112,128},... | collective-permute-start | bytes 442376 | tf_op jit(solution)/shard_map/ppermute | solution.py:21
  103.5 10.6 %collective-permute-start.12 = (f32[2,48,1,384]{3,1,2,0:T(8,128)S(1)}, f32[2,48,1,384]{3,1,2,0:T(8,128)S(1)}, u32[]{:S(2)}, u32[]{:S(2)}) collective-permute-start(f32[2,48,1,384]{3,1,2,0:T(8,128)S(1)} %get-tuple-element.38), channel_id=1, source_target_pairs={{16,0},{32,16},{48,32},{64,48},{80,64},{96,80},{112,96},{128,112},... | collective-permute-start | bytes 442376 | tf_op jit(solution)/shard_map/ppermute | solution.py:24
  114.7 10.8 %collective-permute-start.14 = (f32[2,48,8,1]{3,2,1,0:T(8,128)S(1)}, f32[2,48,8,1]{3,2,1,0:T(8,128)S(1)}, u32[]{:S(2)}, u32[]{:S(2)}) collective-permute-start(f32[2,48,8,1]{3,2,1,0:T(8,128)S(1)} %get-tuple-element.34), channel_id=1, source_target_pairs={{1,0},{2,1},{3,2},{4,3},{5,4},{6,5},{7,6},{8,7},{9,8},{10,9},{11,1... | collective-permute-start | bytes 9224 | tf_op jit(solution)/shard_map/ppermute | solution.py:24
  117.5 9.2 %collective-permute-start.15 = (f32[2,48,8,1]{3,2,1,0:T(8,128)S(1)}, f32[2,48,8,1]{3,2,1,0:T(8,128)S(1)}, u32[]{:S(2)}, u32[]{:S(2)}) collective-permute-start(f32[2,48,8,1]{3,2,1,0:T(8,128)S(1)} %get-tuple-element.35), channel_id=1, source_target_pairs={{0,1},{1,2},{2,3},{3,4},{4,5},{5,6},{6,7},{7,8},{8,9},{9,10},{10,1... | collective-permute-start | bytes 9224 | tf_op jit(solution)/shard_map/ppermute | solution.py:21
  135.5 5.9 %collective-permute-start.17 = (f32[48,1,384]{2,0,1:T(8,128)S(1)}, f32[48,1,384]{2,0,1:T(8,128)S(1)}, u32[]{:S(2)}, u32[]{:S(2)}) collective-permute-start(f32[48,1,384]{2,0,1:T(8,128)S(1)} %get-tuple-element.53), channel_id=1, source_target_pairs={{0,16},{16,32},{32,48},{48,64},{64,80},{80,96},{96,112},{112,128},... | collective-permute-start | bytes 221192 | tf_op jit(solution)/shard_map/ppermute | solution.py:21
  137.4 9.2 %collective-permute-start.16 = (f32[48,1,384]{2,0,1:T(8,128)S(1)}, f32[48,1,384]{2,0,1:T(8,128)S(1)}, u32[]{:S(2)}, u32[]{:S(2)}) collective-permute-start(f32[48,1,384]{2,0,1:T(8,128)S(1)} %get-tuple-element.52), channel_id=1, source_target_pairs={{16,0},{32,16},{48,32},{64,48},{80,64},{96,80},{112,96},{128,112},... | collective-permute-start | bytes 221192 | tf_op jit(solution)/shard_map/ppermute | solution.py:24
  147.0 11.8 %copy-start.5 = (f32[48,6,384]{2,0,1:T(8,128)S(1)}, f32[48,6,384]{2,0,1:T(8,128)}, u32[]{:S(2)}) copy-start(f32[48,6,384]{2,0,1:T(8,128)} %copy-done.4) | copy-start | bytes 1327108
  147.0 11.8 %copy-start.8 = (f32[48,6,384]{2,0,1:T(8,128)S(1)}, f32[48,6,384]{2,0,1:T(8,128)}, u32[]{:S(2)}) copy-start(f32[48,6,384]{2,0,1:T(8,128)} %copy-done.7) | copy-start | bytes 1327108
  147.0 9.4 %collective-permute-start.18 = (f32[48,8,1]{2,1,0:T(8,128)S(1)}, f32[48,8,1]{2,1,0:T(8,128)S(1)}, u32[]{:S(2)}, u32[]{:S(2)}) collective-permute-start(f32[48,8,1]{2,1,0:T(8,128)S(1)} %get-tuple-element.42), channel_id=1, source_target_pairs={{1,0},{2,1},{3,2},{4,3},{5,4},{6,5},{7,6},{8,7},{9,8},{10,9},{11,1... | collective-permute-start | bytes 4616 | tf_op jit(solution)/shard_map/ppermute | solution.py:24
  149.7 7.9 %collective-permute-start.19 = (f32[48,8,1]{2,1,0:T(8,128)S(1)}, f32[48,8,1]{2,1,0:T(8,128)S(1)}, u32[]{:S(2)}, u32[]{:S(2)}) collective-permute-start(f32[48,8,1]{2,1,0:T(8,128)S(1)} %get-tuple-element.43), channel_id=1, source_target_pairs={{0,1},{1,2},{2,3},{3,4},{4,5},{5,6},{6,7},{7,8},{8,9},{9,10},{10,1... | collective-permute-start | bytes 4616 | tf_op jit(solution)/shard_map/ppermute | solution.py:21
  158.8 7.3 %copy-start.19 = (f32[4,48,2,128]{3,2,1,0:T(2,128)S(1)}, f32[4,48,2,128]{3,2,1,0:T(2,128)}, u32[]{:S(2)}) copy-start(f32[4,48,2,128]{3,2,1,0:T(2,128)} %param.7) | copy-start | bytes 589828
  159.9 35.6 %copy-start.1 = (f32[48,6,384]{2,0,1:T(8,128)}, f32[48,6,384]{2,0,1:T(8,128)S(1)}, u32[]{:S(2)}) copy-start(f32[48,6,384]{2,0,1:T(8,128)S(1)} %get-tuple-element.62) | copy-start | bytes 1327108
  160.7 8.7 %collective-permute-start.21 = (f32[2,48,1,384]{3,1,2,0:T(8,128)}, f32[2,48,1,384]{3,1,2,0:T(8,128)S(1)}, u32[]{:S(2)}, u32[]{:S(2)}) collective-permute-start(f32[2,48,1,384]{3,1,2,0:T(8,128)} %get-tuple-element.37), channel_id=1, source_target_pairs={{0,16},{16,32},{32,48},{48,64},{64,80},{80,96},{96,112},{112,128},... | collective-permute-start | bytes 442376 | tf_op jit(solution)/shard_map/ppermute | solution.py:21
  162.6 10.7 %collective-permute-start.20 = (f32[2,48,1,384]{3,1,2,0:T(8,128)}, f32[2,48,1,384]{3,1,2,0:T(8,128)}, u32[]{:S(2)}, u32[]{:S(2)}) collective-permute-start(f32[2,48,1,384]{3,1,2,0:T(8,128)} %get-tuple-element.36), channel_id=1, source_target_pairs={{16,0},{32,16},{48,32},{64,48},{80,64},{96,80},{112,96},{128,112},... | collective-permute-start | bytes 442376 | tf_op jit(solution)/shard_map/ppermute | solution.py:24
  169.3 5.0 %copy-start.6 = (f32[2,48,6,384]{3,2,1,0:T(8,128)}, f32[2,48,6,384]{3,2,1,0:T(8,128)S(1)}, u32[]{:S(2)}) copy-start(f32[2,48,6,384]{3,2,1,0:T(8,128)S(1)} %copy.392) | copy-start | bytes 2654212
  169.4 14.1 %copy-start.10 = (f32[48,6,384]{2,0,1:T(8,128)S(1)}, f32[48,6,384]{2,0,1:T(8,128)}, u32[]{:S(2)}) copy-start(f32[48,6,384]{2,0,1:T(8,128)} %get-tuple-element.18) | copy-start | bytes 1327108
  175.7 17.2 %collective-permute-start.22 = (f32[2,48,8,1]{3,2,1,0:T(8,128)}, f32[2,48,8,1]{3,2,1,0:T(8,128)}, u32[]{:S(2)}, u32[]{:S(2)}) collective-permute-start(f32[2,48,8,1]{3,2,1,0:T(8,128)} %get-tuple-element.30), channel_id=1, source_target_pairs={{1,0},{2,1},{3,2},{4,3},{5,4},{6,5},{7,6},{8,7},{9,8},{10,9},{11,1... | collective-permute-start | bytes 9224 | tf_op jit(solution)/shard_map/ppermute | solution.py:24
  178.0 15.0 %collective-permute-start.23 = (f32[2,48,8,1]{3,2,1,0:T(8,128)}, f32[2,48,8,1]{3,2,1,0:T(8,128)}, u32[]{:S(2)}, u32[]{:S(2)}) collective-permute-start(f32[2,48,8,1]{3,2,1,0:T(8,128)} %get-tuple-element.31), channel_id=1, source_target_pairs={{0,1},{1,2},{2,3},{3,4},{4,5},{5,6},{6,7},{7,8},{8,9},{9,10},{10,1... | collective-permute-start | bytes 9224 | tf_op jit(solution)/shard_map/ppermute | solution.py:21
  192.9 2.6 copy-start.20
  192.9 2.6 copy-start.21
  192.9 2.6 copy-start.23
  215.7 3.6 %copy-start.13 = (f32[1,48,2,3,128,3]{1,5,4,3,2,0:T(4,128)S(1)}, f32[1,48,2,3,128,3]{1,5,4,3,2,0:T(4,128)}, u32[]{:S(2)}) copy-start(f32[1,48,2,3,128,3]{1,5,4,3,2,0:T(4,128)} %stack.46) | copy-start | bytes 1327108
  226.6 26.0 %copy-start.2 = (f32[48,6,384]{2,0,1:T(8,128)S(1)}, f32[48,6,384]{2,0,1:T(8,128)}, u32[]{:S(2)}) copy-start(f32[48,6,384]{2,0,1:T(8,128)} %copy-done.1) | copy-start | bytes 1327108
  226.7 26.0 %copy-start.14 = (f32[1,48,6,384]{3,1,2,0:T(8,128)S(1)}, f32[1,48,6,384]{3,1,2,0:T(8,128)}, u32[]{:S(2)}) copy-start(f32[1,48,6,384]{3,1,2,0:T(8,128)} %copy_select_fusion) | copy-start | bytes 1327108
  226.7 26.0 %copy-start.15 = (f32[48,6,384]{2,0,1:T(8,128)S(1)}, f32[48,6,384]{2,0,1:T(8,128)}, u32[]{:S(2)}) copy-start(f32[48,6,384]{2,0,1:T(8,128)} %subtract_select_fusion) | copy-start | bytes 1327108
  226.8 13.6 %collective-permute-start.24 = (f32[4,48,2,128]{1,3,2,0:T(8,128)S(1)}, f32[4,48,2,128]{1,3,2,0:T(8,128)S(1)}, u32[]{:S(2)}, u32[]{:S(2)}) collective-permute-start(f32[4,48,2,128]{1,3,2,0:T(8,128)S(1)} %broadcast_multiply_fusion), channel_id=1, source_target_pairs={{0,16},{16,32},{32,48},{48,64},{64,80},{80,96},{96,112},{112,128},... | collective-permute-start | bytes 589832 | tf_op jit(solution)/shard_map/ppermute | solution.py:21
  229.2 16.2 %collective-permute-start.25 = (f32[4,48,2,128]{1,3,2,0:T(8,128)S(1)}, f32[4,48,2,128]{1,3,2,0:T(8,128)S(1)}, u32[]{:S(2)}, u32[]{:S(2)}) collective-permute-start(f32[4,48,2,128]{1,3,2,0:T(8,128)S(1)} %broadcast_multiply_fusion), channel_id=1, source_target_pairs={{16,0},{32,16},{48,32},{64,48},{80,64},{96,80},{112,96},{128,112},... | collective-permute-start | bytes 589832 | tf_op jit(solution)/shard_map/ppermute | solution.py:24
  245.4 8.6 %collective-permute-start.26 = (f32[4,48,6,2]{1,2,3,0:T(8,128)S(1)}, f32[4,48,6,2]{1,2,3,0:T(8,128)S(1)}, u32[]{:S(2)}, u32[]{:S(2)}) collective-permute-start(f32[4,48,6,2]{1,2,3,0:T(8,128)S(1)} %copy.410), channel_id=1, source_target_pairs={{0,1},{1,2},{2,3},{3,4},{4,5},{5,6},{6,7},{7,8},{8,9},{9,10},{10,1... | collective-permute-start | bytes 27656 | tf_op jit(solution)/shard_map/ppermute | solution.py:21
  250.7 6.4 %collective-permute-start.27 = (f32[4,48,6,2]{1,2,3,0:T(8,128)S(1)}, f32[4,48,6,2]{1,2,3,0:T(8,128)S(1)}, u32[]{:S(2)}, u32[]{:S(2)}) collective-permute-start(f32[4,48,6,2]{1,2,3,0:T(8,128)S(1)} %copy.411), channel_id=1, source_target_pairs={{1,0},{2,1},{3,2},{4,3},{5,4},{6,5},{7,6},{8,7},{9,8},{10,9},{11,1... | collective-permute-start | bytes 27656 | tf_op jit(solution)/shard_map/ppermute | solution.py:24
  (5 other events, 5.7 us)
where the time goes:
time: 262 us; the launch traced here: 260 us
  starting transfers between devices  96.5 us (37%)
  local copies, waits for them, and re-layouts  71.3 us (27%)
  waiting for transfers between devices  52 us (20%)
  other arithmetic  31 us (12%)
  between operations  5.69 us (2%)
  matrix products  3.61 us (1%)
    ppermute x14, starting transfers between devices, padded_2(): lax.ppermute(lax.slice_in_dim(block, block.shape[dim] - width, None, axis...  59.8 us
    ppermute x14, waiting for transfers between devices, padded_2(): lax.ppermute(lax.slice_in_dim(block, 0, width, axis=dim), axis, backward)  38.2 us
    ppermute x14, starting transfers between devices, padded_2(): lax.ppermute(lax.slice_in_dim(block, 0, width, axis=dim), axis, backward)  36.6 us
    unnamed x61, local copies, waits for them, and re-layouts  15.1 us
    ppermute x14, waiting for transfers between devices, padded_2(): lax.ppermute(lax.slice_in_dim(block, block.shape[dim] - width, None, axis...  13.8 us
    slice x10, local copies, waits for them, and re-layouts, level_up(): return jnp.concatenate([field[1:], jnp.zeros_like(field[:1])], 0)  8.78 us
    another operation x4, local copies, waits for them, and re-layouts, acoustic(): return jnp.stack([u_next, v_next, w_next, p_next])  7.39 us
    concatenate x7, other arithmetic, padded_2(): block = jnp.concatenate([low, block, high], axis=dim)  7.12 us
  transfers between devices with their start and end apart: 28, of which 18 were waited for; matrix products, arithmetic and copies ran while one was open for 16% of the time, Pallas kernels for 0%

commit v1 on v0

v1 whole, which is shorter than its diff:
```python
import functools

import jax
import jax.numpy as jnp
from jax import lax
from jax.experimental import pallas as pl
from jax.experimental.pallas import tpu as pltpu
from jax.sharding import PartitionSpec as P

RATIO = 3
GRAD = 0.25
DIV = 0.25
COUPLE = 0.25
LIFT = 0.5
F32 = jnp.float32
BF16 = jnp.bfloat16
VMEM_BYTES = 60 * 1024 * 1024

ROWS = 6
COLS = 384
LANES = 128
WIDE = COLS + LANES
SIDE = 8
PER_TILE = LANES // SIDE
P_DEEP, U_DEEP, V_DEEP, W_DEEP = 5, 4, 3, 3
KEEP = 3
WIN = ROWS + 2 * KEEP
P_AT = 0
U_AT = P_AT + P_DEEP
V_AT = U_AT + U_DEEP
W_AT = V_AT + V_DEEP
S_AT = W_AT + W_DEEP
PACK_AT = S_AT + ROWS
MESSAGE = PACK_AT + 2
S_GROUP = 4 * ROWS
EDGE_GROUP = S_GROUP + ROWS
GROUPS = EDGE_GROUP + 4
PACK = -(-GROUPS // PER_TILE) * LANES
U, V, W, PR = 0, 1, 2, 3


def lanes_of(shape):
    return lax.broadcasted_iota(jnp.int32, shape, len(shape) - 1)


def column_of_lane(shape):
    lane = lanes_of(shape)
    return jnp.where(lane < COLS + LANES // 2, lane, lane - WIDE)


def is_edge(index, count):
    return (index < RATIO) | (index >= count - RATIO)


def expand(coarse, first):
    lane = lanes_of(coarse.shape)
    return jnp.take_along_axis(coarse, (lane + first) // RATIO, axis=1)


def expand_all(coarse):
    parts = [expand(coarse, first) for first in range(0, COLS, LANES)]
    return jnp.concatenate(parts, axis=1)


def turn(x, amount):
    amount = amount % x.shape[1]
    return x if amount == 0 else pltpu.roll(x, amount, 1)


def next_col(x):
    return pltpu.roll(x, x.shape[1] - 1, 1)


def prev_col(x):
    return pltpu.roll(x, 1, 1)


def level_up(x):
    levels = x.shape[0]
    level = lax.broadcasted_iota(jnp.int32, x.shape, 0)
    return jnp.where(level < levels - 1, pltpu.roll(x, levels - 1, 0), 0.0)


def level_down(x):
    level = lax.broadcasted_iota(jnp.int32, x.shape, 0)
    return jnp.where(level > 0, pltpu.roll(x, 1, 0), 0.0)


def split_dot(table, x):
    high = x.astype(BF16)
    low = (x - high.astype(F32)).astype(BF16)
    stacked = jnp.concatenate([high, low, high], axis=0)
    return jnp.dot(table, stacked, preferred_element_type=F32)


def prepare_kernel(counts, off_ref, nest_ref, stiff_ref, parent_ref, cur_ref, left_ref, right_ref, edge_ref):
    nx, ny = counts
    gx, gy = lax.axis_index("gx"), lax.axis_index("gy")
    off_x, off_y = off_ref[0], off_ref[1]
    levels = nest_ref.shape[2]
    col = lanes_of((levels, COLS)) + (gy * COLS - RATIO * off_y)
    edge_col = is_edge(col, ny)
    place = lanes_of((levels, LANES)) // SIDE
    packs = {}

    def pack(row, group):
        tile, slot = group // PER_TILE, group % PER_TILE
        to_left = turn(row[:, :LANES], SIDE * slot)
        to_right = turn(row[:, COLS - LANES :], SIDE * (slot + 1) - LANES)
        if slot == 0:
            packs[tile] = (to_left, to_right)
        else:
            left, right = packs[tile]
            here = place == slot
            packs[tile] = (jnp.where(here, to_left, left), jnp.where(here, to_right, right))
        if slot == PER_TILE - 1 or group == GROUPS - 1:
            at = slice(LANES * tile, LANES * (tile + 1))
            left_ref[:, at] = packs[tile][0]
            right_ref[:, at] = packs[tile][1]

    rims = []
    for field in range(4):
        bounds = [expand_all(parent_ref[field, :, coarse, :]) for coarse in range(ROWS // RATIO)]
        for row in range(ROWS):
            i = gx * ROWS + row - RATIO * off_x
            held = is_edge(i, nx).astype(jnp.int32)
            value = jnp.where(edge_col | (held > 0), bounds[row // RATIO], nest_ref[field, row])
            cur_ref[field, row] = value
            pack(value, field * ROWS + row)
        rim = jnp.where(gx == 0, bounds[0], bounds[-1])
        edge_ref[field] = rim
        rims.append(rim)
    for row in range(ROWS):
        pack(stiff_ref[row], S_GROUP + row)
    for field in range(4):
        pack(rims[field], EDGE_GROUP + field)


def message_kernel(last_y, cur_ref, stiff_ref, parent_ref, left_ref, right_ref, up_ref, down_ref):
    gx, gy = lax.axis_index("gx"), lax.axis_index("gy")
    up_ref[PACK_AT] = left_ref[...]
    up_ref[PACK_AT + 1] = right_ref[...]
    levels = stiff_ref.shape[1]
    place = lanes_of((levels, LANES)) // SIDE

    def fill(slot_row, cell):
        for tile in range(PACK // LANES):
            at = slice(LANES * tile, LANES * (tile + 1))
            out = up_ref[slot_row, :, at]
            for slot in range(PER_TILE):
                group = tile * PER_TILE + slot
                if group < S_GROUP:
                    field, coarse = group // ROWS, (group % ROWS) // RATIO
                    value = parent_ref[field, :, coarse, cell : cell + 1]
                elif EDGE_GROUP <= group < GROUPS:
                    field = group - EDGE_GROUP
                    value = jnp.where(
                        gx == 0,
                        parent_ref[field, :, 0, cell : cell + 1],
                        parent_ref[field, :, ROWS // RATIO - 1, cell : cell + 1],
                    )
                else:
                    continue
                out = jnp.where(place == slot, value, out)
            up_ref[slot_row, :, at] = out

    @pl.when(gy == 0)
    def _():
        fill(PACK_AT, 0)

    @pl.when(gy == last_y)
    def _():
        fill(PACK_AT + 1, COLS // RATIO - 1)

    for pack in range(2):
        down_ref[PACK_AT + pack] = up_ref[PACK_AT + pack]
    for field, at, deep in ((PR, P_AT, P_DEEP), (U, U_AT, U_DEEP), (V, V_AT, V_DEEP), (W, W_AT, W_DEEP)):
        for row in range(deep):
            up_ref[at + row] = cur_ref[field, ROWS - deep + row]
            down_ref[at + row] = cur_ref[field, row]
    for row in range(ROWS):
        up_ref[S_AT + row] = stiff_ref[row]
        down_ref[S_AT + row] = stiff_ref[row]


def held_lanes(gy, off_y, ny, shape):
    j = column_of_lane(shape) + (gy * COLS - RATIO * off_y)
    return is_edge(j, ny).astype(jnp.int32)


def held_row(gx, row, off_x, nx):
    return is_edge(gx * ROWS + row - RATIO * off_x, nx).astype(jnp.int32)


def winds_x(held, gx, off_x, nx, p_ref, u_ref, out_ref):
    def body(at, carry):
        keep = (held + held_row(gx, at - U_DEEP, off_x, nx)) > 0
        wind = u_ref[at]
        out_ref[at] = jnp.where(keep, wind, wind - GRAD * (p_ref[at + 2] - p_ref[at]))
        return carry

    lax.fori_loop(0, ROWS + 2 * U_DEEP, body, 0)


def column_step(held, gx, off_x, nx, table, u_ref, p_ref, v_of, w_of, s_of, put):
    def body(at, carry):
        keep = (held + held_row(gx, at - KEEP, off_x, nx)) > 0
        pressure = p_ref[at + P_DEEP - KEEP]
        wind = v_of(at)
        wind = jnp.where(keep, wind, wind - GRAD * (next_col(pressure) - prev_col(pressure)))
        lift = w_of(at)
        divergence = (u_ref[at + 2] - u_ref[at]) + (next_col(wind) - prev_col(wind))
        right_side = pressure - DIV * divergence - COUPLE * (level_up(lift) - level_down(lift))
        levels = pressure.shape[0]
        both = split_dot(table, right_side)
        first, around = both[:levels], both[levels:]
        leftover = right_side - ((1.0 + s_of(at)) * first - 0.25 * around)
        solved = first + split_dot(table[:levels], leftover)
        p_next = jnp.where(keep, pressure, solved)
        w_next = jnp.where(keep, lift, lift - LIFT * (level_up(p_next) - p_next))
        put(at, wind, w_next, p_next)
        return carry

    lax.fori_loop(0, WIN, body, 0)


def first_kernel(
    counts, off_ref, cur_ref, stiff_ref, edge_ref, mine_ref, low_ref, high_ref, table_ref,
    u_out, v_out, w_out, p_out, s_out, up_out, down_out,
    p_win, u_win, v_win, w_win, s_win,
):
    nx, ny = counts
    gx, gy = lax.axis_index("gx"), lax.axis_index("gy")
    off_x, off_y = off_ref[0], off_ref[1]
    levels = stiff_ref.shape[1]
    lane = lanes_of((levels, LANES))

    def beside(source, group):
        tile, slot = group // PER_TILE, group % PER_TILE
        at = slice(LANES * tile, LANES * (tile + 1))
        left = turn(source[PACK_AT, :, at], LANES - SIDE * (slot + 1))
        right = turn(source[PACK_AT + 1, :, at], -SIDE * slot)
        return jnp.where(lane < LANES // 2, right, left)

    def place(window, at, main, ext):
        window[at, :, :COLS] = main
        window[at, :, COLS:] = ext

    for field, at, deep, window in (
        (PR, P_AT, P_DEEP, p_win),
        (U, U_AT, U_DEEP, u_win),
        (V, V_AT, V_DEEP, v_win),
        (W, W_AT, W_DEEP, w_win),
    ):
        for row in range(deep):
            place(window, row, low_ref[at + row], beside(low_ref, field * ROWS + ROWS - deep + row))
            place(window, deep + ROWS + row, high_ref[at + row], beside(high_ref, field * ROWS + row))
        for row in range(ROWS):
            place(window, deep + row, cur_ref[field, row], beside(mine_ref, field * ROWS + row))

        @pl.when(gx == 0)
        def _(field=field, deep=deep, window=window):
            for row in range(deep - KEEP, deep):
                place(window, row, edge_ref[field], beside(mine_ref, EDGE_GROUP + field))

        @pl.when(gx == nx // ROWS - 1)
        def _(field=field, deep=deep, window=window):
            for row in range(deep + ROWS, deep + ROWS + KEEP):
                place(window, row, edge_ref[field], beside(mine_ref, EDGE_GROUP + field))

    for row in range(ROWS):
        place(s_win, row, low_ref[S_AT + row], beside(low_ref, S_GROUP + row))
        place(s_win, ROWS + row, stiff_ref[row], beside(mine_ref, S_GROUP + row))
        place(s_win, 2 * ROWS + row, high_ref[S_AT + row], beside(high_ref, S_GROUP + row))

    held = held_lanes(gy, off_y, ny, (levels, WIDE))
    winds_x(held, gx, off_x, nx, p_win, u_win, u_out)
    move_y = lax.rem(RATIO * off_y + WIDE, WIDE)

    def stiffness(at):
        value = pltpu.roll(s_win[at + ROWS - KEEP - RATIO * off_x], move_y, 1)
        s_out[at] = value
        return value

    def put(at, v_next, w_next, p_next):
        v_out[at] = v_next
        w_out[at] = w_next
        p_out[at] = p_next

    column_step(
        held, gx, off_x, nx, table_ref[...], u_out, p_win,
        lambda at: v_win[at], lambda at: w_win[at], stiffness, put,
    )
    far = P_DEEP - KEEP
    for row in range(far):
        up_out[row] = p_out[KEEP + ROWS - P_DEEP + row]
        down_out[row] = p_out[KEEP + KEEP + row]


def second_kernel(
    counts, off_ref, u_ref, v_ref, w_ref, p_ref, s_ref, low_ref, high_ref, table_ref, parent_ref,
    new_ref, back_ref,
    p_win, u_win, v_win, w_win, q_win,
):
    nx, ny = counts
    gx, gy = lax.axis_index("gx"), lax.axis_index("gy")
    off_x, off_y = off_ref[0], off_ref[1]
    levels = u_ref.shape[1]
    far = P_DEEP - KEEP
    for row in range(far):
        p_win[row] = low_ref[row]
        p_win[far + WIN + row] = high_ref[row]
    for row in range(WIN):
        p_win[far + row] = p_ref[row]
    held = held_lanes(gy, off_y, ny, (levels, WIDE))
    winds_x(held, gx, off_x, nx, p_win, u_ref, u_win)

    def put(at, v_next, w_next, p_next):
        v_win[at] = v_next
        w_win[at] = w_next
        q_win[at] = p_next

    column_step(
        held, gx, off_x, nx, table_ref[...], u_win, p_win,
        lambda at: v_ref[at], lambda at: w_ref[at], lambda at: s_ref[at], put,
    )
    move_y = lax.rem(WIDE - RATIO * off_y, WIDE)
    windows = ((U, u_win, U_DEEP), (V, v_win, KEEP), (W, w_win, KEEP), (PR, q_win, KEEP))
    for field, window, deep in windows:
        for row in range(ROWS):
            moved = pltpu.roll(window[row + deep + RATIO * off_x], move_y, 1)
            new_ref[field, row] = moved[:, :COLS]

    cells_x, cells_y = nx // RATIO, ny // RATIO
    coarse_rows, coarse_cols = ROWS // RATIO, COLS // RATIO
    first_cell = gy * coarse_cols - off_y

    def inside(index, count):
        return (index >= 1) & (index <= count - 2)

    lane = lax.broadcasted_iota(jnp.int32, (WIDE, coarse_cols), 0)
    source = jnp.where(lane < COLS + LANES // 2, lane, lane - WIDE)
    apart = source - RATIO * lax.broadcasted_iota(jnp.int32, (WIDE, coarse_cols), 1)
    spread = jnp.where(
        (apart >= 0) & (apart < RATIO),
        0.5,
        jnp.where((apart >= -RATIO) & (apart < 2 * RATIO), 0.25, 0.0),
    ).astype(BF16)
    cell = lanes_of((levels, coarse_cols)) + first_cell
    weight_y = (
        0.25 * inside(cell - 1, cells_y).astype(F32)
        + 0.5 * inside(cell, cells_y).astype(F32)
        + 0.25 * inside(cell + 1, cells_y).astype(F32)
    )
    centre_y = inside(cell, cells_y).astype(jnp.int32)
    for coarse in range(coarse_rows):
        a = gx * coarse_rows + coarse - off_x
        inner = [inside(a + d, cells_x).astype(F32) for d in (-1, 0, 1)]
        weights = [s * m for s, m in zip((0.25, 0.5, 0.25), inner)]
        weight_x = weights[0] + weights[1] + weights[2]
        centre = (centre_y * inside(a, cells_x).astype(jnp.int32)) > 0
        scale = jnp.where(centre, 1.0 / jnp.where(centre, 9.0 * weight_x * weight_y, 1.0), 0.0)
        for field, window, deep in windows:
            start = deep - KEEP + RATIO * coarse
            total = None
            for d in range(3):
                part = window[start + 3 * d] + window[start + 3 * d + 1] + window[start + 3 * d + 2]
                part = jnp.where(inner[d] > 0, part * weights[d], 0.0)
                total = part if total is None else total + part
            total = jnp.where(held > 0, 0.0, total)
            high = total.astype(BF16)
            low = (total - high.astype(F32)).astype(BF16)
            summed = jnp.dot(high, spread, preferred_element_type=F32) + jnp.dot(
                low, spread, preferred_element_type=F32
            )
            back_ref[field, :, coarse, :] = jnp.where(centre, summed * scale, parent_ref[field, :, coarse, :])


def vmem_specs(count):
    return [pl.BlockSpec(memory_space=pltpu.VMEM)] * count


def call(body, ins, outs, scratch=()):
    smem = [pl.BlockSpec(memory_space=pltpu.SMEM) if x.dtype == jnp.int32 else pl.BlockSpec(memory_space=pltpu.VMEM) for x in ins]
    return pl.pallas_call(
        body,
        out_shape=[jax.ShapeDtypeStruct(shape, F32) for shape in outs],
        in_specs=smem,
        out_specs=vmem_specs(len(outs)),
        scratch_shapes=[pltpu.VMEM(shape, F32) for shape in scratch],
        compiler_params=pltpu.CompilerParams(vmem_limit_bytes=VMEM_BYTES),
    )(*ins)


def steps(axis, by):
    count = lax.axis_size(axis)
    return [(i, i + by) for i in range(count) if 0 <= i + by < count]


def per_device(nest_state, stiffness, parent, inverse_table, offsets):
    levels = nest_state.shape[1]
    nx = nest_state.shape[2] * lax.axis_size("gx")
    ny = nest_state.shape[3] * lax.axis_size("gy")
    counts = (nx, ny)
    nest = jnp.transpose(nest_state, (0, 2, 1, 3))
    stiff = jnp.transpose(stiffness, (1, 0, 2))

    shifted = jnp.concatenate([inverse_table[1:], jnp.zeros_like(inverse_table[:1])], 0) + jnp.concatenate(
        [jnp.zeros_like(inverse_table[:1]), inverse_table[:-1]], 0
    )
    stack = jnp.concatenate([inverse_table, shifted], 0)
    top = lax.reduce_precision(stack, 8, 7)
    table = jnp.concatenate([top, top, stack - top], 1).astype(BF16)

    cur, to_left, to_right, edge = call(
        functools.partial(prepare_kernel, counts),
        (offsets, nest, stiff, parent),
        [nest.shape, (levels, PACK), (levels, PACK), (4, levels, COLS)],
    )
    from_left = lax.ppermute(to_right, "gy", steps("gy", 1))
    from_right = lax.ppermute(to_left, "gy", steps("gy", -1))
    message = (MESSAGE, levels, COLS)
    up, down = call(
        functools.partial(message_kernel, lax.axis_size("gy") - 1),
        (cur, stiff, parent, from_left, from_right),
        [message, message],
    )
    low = lax.ppermute(up, "gx", steps("gx", 1))
    high = lax.ppermute(down, "gx", steps("gx", -1))
    win = (WIN, levels, WIDE)
    u_shape = (ROWS + 2 * U_DEEP, levels, WIDE)
    p_shape = (ROWS + 2 * P_DEEP, levels, WIDE)
    far = (P_DEEP - KEEP, levels, WIDE)
    u1, v1, w1, p1, s1, up, down = call(
        functools.partial(first_kernel, counts),
        (offsets, cur, stiff, edge, up, low, high, table),
        [u_shape, win, win, win, win, far, far],
        [p_shape, u_shape, win, win, (3 * ROWS, levels, WIDE)],
    )
    low = lax.ppermute(up, "gx", steps("gx", 1))
    high = lax.ppermute(down, "gx", steps("gx", -1))
    new, back = call(
        functools.partial(second_kernel, counts),
        (offsets, u1, v1, w1, p1, s1, low, high, table, parent),
        [nest.shape, parent.shape],
        [p_shape, u_shape, win, win, win],
    )
    return jnp.transpose(new, (0, 2, 1, 3)), back


def solution(mesh):
    return jax.shard_map(
        per_device,
        mesh=mesh,
        in_specs=(
            P(None, None, "gx", "gy"),
            P(None, "gx", "gy"),
            P(None, None, "gx", "gy"),
            P(),
            P(),
        ),
        out_specs=(P(None, None, "gx", "gy"), P(None, None, "gx", "gy")),
        check_vma=False,
    )
```

time: 262 us -> 111 us (0.42)
  the two profiles are of different devices: /device:TPU:223 before, /device:TPU:214 now
where the time goes in v1:
time: 111 us
  waiting for transfers between devices  49 us (44%)
  Pallas kernels  33.6 us (30%)
  starting transfers between devices  24.3 us (22%)
  local copies, waits for them, and re-layouts  2.56 us (2%)
    ppermute x2, waiting for transfers between devices, per_device(): high = lax.ppermute(down, 'gx', steps('gx', -1))  42.1 us
    pallas_call x4, Pallas kernels, call(): pl.pallas_call(body, out_shape=[jax.ShapeDtypeStruct(shape, F32) for shap...  33.6 us
    ppermute x2, starting transfers between devices, per_device(): low = lax.ppermute(up, 'gx', steps('gx', 1))  14 us
    ppermute x2, waiting for transfers between devices, per_device(): low = lax.ppermute(up, 'gx', steps('gx', 1))  4.69 us
    ppermute x2, starting transfers between devices, per_device(): high = lax.ppermute(down, 'gx', steps('gx', -1))  4.64 us
    ppermute x1, starting transfers between devices, per_device(): from_right = lax.ppermute(to_left, 'gy', steps('gy', -1))  3.64 us
    unnamed x14, local copies, waits for them, and re-layouts  2.55 us
  transfers between devices with their start and end apart: 6, of which 6 were waited for; matrix products, arithmetic and copies ran while one was open for 1% of the time, Pallas kernels for 0%

profile of v1, /device:TPU:214, one launch (start us, length us, event | category | flops | bytes accessed | tf_op | source)
XLA Modules:
  0.0 111.0 jit_solution(5784511108829862402)
XLA Ops:
  0.6 3.6 %shard_map.68 = (f32[4,6,48,384]{3,2,1,0:T(8,128)}, f32[48,384]{1,0:T(8,128)}, f32[48,384]{1,0:T(8,128)}, f32[4,48,384]{2,1,0:T(8,128)}) custom-call(s32[2]{0:T(128)} %off_ref.5, f32[4,6,48,384]{3,2,1,0:T(8,128)} %bitcast.6, f32[6,48,384]{2,1,0:T(8,128)} %bitcast.3, f32[4,48,2,128]{3,2,1,0:T(2,128)} %parent_ref.5), custom_call_target="tpu_custom_call" | custom-call | tf_op jit(solution)/shard_map/pallas_call | solution.py:385
  4.2 0.0 copy-start.2
  4.2 2.0 %collective-permute-start = (f32[48,384]{1,0:T(8,128)}, f32[48,384]{1,0:T(8,128)S(1)}, u32[]{:S(2)}, u32[]{:S(2)}) collective-permute-start(f32[48,384]{1,0:T(8,128)} %get-tuple-element.19), channel_id=1, source_target_pairs={{0,1},{1,2},{2,3},{3,4},{4,5},{5,6},{6,7},{7,8},{8,9},{9,10},{10,1... | collective-permute-start | bytes 221192 | tf_op jit(solution)/shard_map/ppermute | solution.py:420
  6.3 3.6 %collective-permute-start.1 = (f32[48,384]{1,0:T(8,128)}, f32[48,384]{1,0:T(8,128)S(1)}, u32[]{:S(2)}, u32[]{:S(2)}) collective-permute-start(f32[48,384]{1,0:T(8,128)} %get-tuple-element.20), channel_id=1, source_target_pairs={{1,0},{2,1},{3,2},{4,3},{5,4},{6,5},{7,6},{8,7},{9,8},{10,9},{11,1... | collective-permute-start | bytes 221192 | tf_op jit(solution)/shard_map/ppermute | solution.py:421
  9.9 0.3 collective-permute-done.left_ref
  10.2 0.0 copy-start.5
  10.2 2.0 %collective-permute-done.1.right_ref = f32[48,384]{1,0:T(8,128)S(1)} collective-permute-done((f32[48,384]{1,0:T(8,128)}, f32[48,384]{1,0:T(8,128)S(1)}, u32[]{:S(2)}, u32[]{:S(2)}) %collective-permute-start.1) | collective-permute-done | bytes 73760 | tf_op jit(solution)/shard_map/ppermute | solution.py:421
  12.2 0.0 copy-start.6
  12.2 0.0 copy-done.5
  12.2 0.6 copy-done.6
  12.8 3.6 %shard_map.69 = (f32[23,48,384]{2,1,0:T(8,128)}, f32[23,48,384]{2,1,0:T(8,128)}) custom-call(f32[4,6,48,384]{3,2,1,0:T(8,128)} %get-tuple-element.17.cur_ref, f32[6,48,384]{2,1,0:T(8,128)} %bitcast.4, f32[4,48,2,128]{3,2,1,0:T(2,128)} %parent_ref.5, f32[48,384]{1,0:T(8,128)} %copy-done.5, f32[48,384]{1,0:T(8,128)} %copy-done.6), custom_call_target="tpu_custom_call" | custom-call | tf_op jit(solution)/shard_map/pallas_call | solution.py:385
  16.4 2.7 %collective-permute-start.3 = (f32[23,48,384]{2,1,0:T(8,128)}, f32[23,48,384]{2,1,0:T(8,128)S(1)}, u32[]{:S(2)}, u32[]{:S(2)}) collective-permute-start(f32[23,48,384]{2,1,0:T(8,128)} %get-tuple-element.22), channel_id=1, source_target_pairs={{16,0},{32,16},{48,32},{64,48},{80,64},{96,80},{112,96},{128,112},... | collective-permute-start | bytes 5087240 | tf_op jit(solution)/shard_map/ppermute | solution.py:429
  19.2 6.4 %collective-permute-start.2 = (f32[23,48,384]{2,1,0:T(8,128)}, f32[23,48,384]{2,1,0:T(8,128)S(1)}, u32[]{:S(2)}, u32[]{:S(2)}) collective-permute-start(f32[23,48,384]{2,1,0:T(8,128)} %get-tuple-element.21.mine_ref), channel_id=1, source_target_pairs={{0,16},{16,32},{32,48},{48,64},{64,80},{80,96},{96,112},{112,128},... | collective-permute-start | bytes 5087240 | tf_op jit(solution)/shard_map/ppermute | solution.py:428
  25.6 0.0 copy-done.2
  25.7 0.7 pad_maximum_fusion.1.table_ref
  26.4 34.7 %collective-permute-done.3.high_ref = f32[23,48,384]{2,1,0:T(8,128)S(1)} collective-permute-done((f32[23,48,384]{2,1,0:T(8,128)}, f32[23,48,384]{2,1,0:T(8,128)S(1)}, u32[]{:S(2)}, u32[]{:S(2)}) %collective-permute-start.3) | collective-permute-done | bytes 1695776 | tf_op jit(solution)/shard_map/ppermute | solution.py:429
  61.1 0.0 copy-start
  61.1 1.9 %collective-permute-done.2.low_ref = f32[23,48,384]{2,1,0:T(8,128)S(1)} collective-permute-done((f32[23,48,384]{2,1,0:T(8,128)}, f32[23,48,384]{2,1,0:T(8,128)S(1)}, u32[]{:S(2)}, u32[]{:S(2)}) %collective-permute-start.2) | collective-permute-done | bytes 1695776 | tf_op jit(solution)/shard_map/ppermute | solution.py:428
  63.0 0.0 copy-start.1
  63.0 0.0 copy-done
  63.0 1.2 %copy-done.1 = f32[23,48,384]{2,1,0:T(8,128)} copy-done((f32[23,48,384]{2,1,0:T(8,128)}, f32[23,48,384]{2,1,0:T(8,128)S(1)}, u32[]{:S(2)}) %copy-start.1) | copy-done | bytes 1695768
  64.2 14.0 %shard_map.70 = (f32[14,48,512]{2,1,0:T(8,128)}, f32[12,48,512]{2,1,0:T(8,128)}, f32[12,48,512]{2,1,0:T(8,128)}, f32[12,48,512]{2,1,0:T(8,128)}, f32[12,48,512]{...) custom-call(s32[2]{0:T(128)} %off_ref.5, f32[4,6,48,384]{3,2,1,0:T(8,128)} %get-tuple-element.17.cur_ref, ...), custom_call_target="tpu_custom_call" | custom-call | tf_op jit(solution)/shard_map/pallas_call | solution.py:385
  78.2 7.6 %collective-permute-start.4 = (f32[2,48,512]{2,1,0:T(8,128)}, f32[2,48,512]{2,1,0:T(8,128)S(1)}, u32[]{:S(2)}, u32[]{:S(2)}) collective-permute-start(f32[2,48,512]{2,1,0:T(8,128)} %get-tuple-element.28), channel_id=1, source_target_pairs={{0,16},{16,32},{32,48},{48,64},{64,80},{80,96},{96,112},{112,128},... | collective-permute-start | bytes 589832 | tf_op jit(solution)/shard_map/ppermute | solution.py:440
  85.8 1.9 %collective-permute-start.5 = (f32[2,48,512]{2,1,0:T(8,128)}, f32[2,48,512]{2,1,0:T(8,128)S(1)}, u32[]{:S(2)}, u32[]{:S(2)}) collective-permute-start(f32[2,48,512]{2,1,0:T(8,128)} %get-tuple-element.29), channel_id=1, source_target_pairs={{16,0},{32,16},{48,32},{64,48},{80,64},{96,80},{112,96},{128,112},... | collective-permute-start | bytes 589832 | tf_op jit(solution)/shard_map/ppermute | solution.py:441
  87.8 2.8 %collective-permute-done.4.low_ref = f32[2,48,512]{2,1,0:T(8,128)S(1)} collective-permute-done((f32[2,48,512]{2,1,0:T(8,128)}, f32[2,48,512]{2,1,0:T(8,128)S(1)}, u32[]{:S(2)}, u32[]{:S(2)}) %collective-permute-start.4) | collective-permute-done | bytes 196640 | tf_op jit(solution)/shard_map/ppermute | solution.py:440
  90.6 0.0 copy-start.3
  90.6 7.3 %collective-permute-done.5.high_ref = f32[2,48,512]{2,1,0:T(8,128)S(1)} collective-permute-done((f32[2,48,512]{2,1,0:T(8,128)}, f32[2,48,512]{2,1,0:T(8,128)S(1)}, u32[]{:S(2)}, u32[]{:S(2)}) %collective-permute-start.5) | collective-permute-done | bytes 196640 | tf_op jit(solution)/shard_map/ppermute | solution.py:441
  97.9 0.0 copy-start.4
  97.9 0.0 copy-done.3
  97.9 0.7 copy-done.4
  98.6 12.4 %shard_map.71 = (f32[4,6,48,384]{3,2,1,0:T(8,128)}, f32[4,48,2,128]{3,2,1,0:T(2,128)}) custom-call(s32[2]{0:T(128)} %off_ref.5, f32[14,48,512]{2,1,0:T(8,128)} %get-tuple-element.23.u_ref, f32[12,48,512]{2,1,0:T(8,128)} %get-tuple-element.24.v_ref, f32[12,48,512]{2,1,0:T(8,128)} %get-tuple-element.25.w_ref, f32[12,48,512]{2,1,0:T(8,128)} %get-tuple-element.26.p_ref, ...), custom_call_target="tpu_custom_call" | custom-call | tf_op jit(solution)/shard_map/pallas_call | solution.py:385
  (3 shorter events, 0.0 us)
Async XLA Ops:
  4.2 21.4 %copy-start.2 = (f32[48,48]{1,0:T(8,128)S(1)}, f32[48,48]{1,0:T(8,128)}, u32[]{:S(2)}) copy-start(f32[48,48]{1,0:T(8,128)} %param.8) | copy-start | bytes 27652
  4.2 6.0 %collective-permute-start = (f32[48,384]{1,0:T(8,128)}, f32[48,384]{1,0:T(8,128)S(1)}, u32[]{:S(2)}, u32[]{:S(2)}) collective-permute-start(f32[48,384]{1,0:T(8,128)} %get-tuple-element.19), channel_id=1, source_target_pairs={{0,1},{1,2},{2,3},{3,4},{4,5},{5,6},{6,7},{7,8},{8,9},{9,10},{10,1... | collective-permute-start | bytes 221192 | tf_op jit(solution)/shard_map/ppermute | solution.py:420
  6.3 5.9 %collective-permute-start.1 = (f32[48,384]{1,0:T(8,128)}, f32[48,384]{1,0:T(8,128)S(1)}, u32[]{:S(2)}, u32[]{:S(2)}) collective-permute-start(f32[48,384]{1,0:T(8,128)} %get-tuple-element.20), channel_id=1, source_target_pairs={{1,0},{2,1},{3,2},{4,3},{5,4},{6,5},{7,6},{8,7},{9,8},{10,9},{11,1... | collective-permute-start | bytes 221192 | tf_op jit(solution)/shard_map/ppermute | solution.py:421
  10.2 2.0 %copy-start.5 = (f32[48,384]{1,0:T(8,128)}, f32[48,384]{1,0:T(8,128)S(1)}, u32[]{:S(2)}) copy-start(f32[48,384]{1,0:T(8,128)S(1)} %collective-permute-done.left_ref) | copy-start | bytes 221188
  12.2 0.6 copy-start.6
  16.4 44.7 %collective-permute-start.3 = (f32[23,48,384]{2,1,0:T(8,128)}, f32[23,48,384]{2,1,0:T(8,128)S(1)}, u32[]{:S(2)}, u32[]{:S(2)}) collective-permute-start(f32[23,48,384]{2,1,0:T(8,128)} %get-tuple-element.22), channel_id=1, source_target_pairs={{16,0},{32,16},{48,32},{64,48},{80,64},{96,80},{112,96},{128,112},... | collective-permute-start | bytes 5087240 | tf_op jit(solution)/shard_map/ppermute | solution.py:429
  19.2 43.8 %collective-permute-start.2 = (f32[23,48,384]{2,1,0:T(8,128)}, f32[23,48,384]{2,1,0:T(8,128)S(1)}, u32[]{:S(2)}, u32[]{:S(2)}) collective-permute-start(f32[23,48,384]{2,1,0:T(8,128)} %get-tuple-element.21.mine_ref), channel_id=1, source_target_pairs={{0,16},{16,32},{32,48},{48,64},{64,80},{80,96},{96,112},{112,128},... | collective-permute-start | bytes 5087240 | tf_op jit(solution)/shard_map/ppermute | solution.py:428
  61.1 1.9 %copy-start = (f32[23,48,384]{2,1,0:T(8,128)}, f32[23,48,384]{2,1,0:T(8,128)S(1)}, u32[]{:S(2)}) copy-start(f32[23,48,384]{2,1,0:T(8,128)S(1)} %collective-permute-done.3.high_ref) | copy-start | bytes 5087236
  63.0 1.2 %copy-start.1 = (f32[23,48,384]{2,1,0:T(8,128)}, f32[23,48,384]{2,1,0:T(8,128)S(1)}, u32[]{:S(2)}) copy-start(f32[23,48,384]{2,1,0:T(8,128)S(1)} %collective-permute-done.2.low_ref) | copy-start | bytes 5087236
  78.2 12.3 %collective-permute-start.4 = (f32[2,48,512]{2,1,0:T(8,128)}, f32[2,48,512]{2,1,0:T(8,128)S(1)}, u32[]{:S(2)}, u32[]{:S(2)}) collective-permute-start(f32[2,48,512]{2,1,0:T(8,128)} %get-tuple-element.28), channel_id=1, source_target_pairs={{0,16},{16,32},{32,48},{48,64},{64,80},{80,96},{96,112},{112,128},... | collective-permute-start | bytes 589832 | tf_op jit(solution)/shard_map/ppermute | solution.py:440
  85.8 12.1 %collective-permute-start.5 = (f32[2,48,512]{2,1,0:T(8,128)}, f32[2,48,512]{2,1,0:T(8,128)S(1)}, u32[]{:S(2)}, u32[]{:S(2)}) collective-permute-start(f32[2,48,512]{2,1,0:T(8,128)} %get-tuple-element.29), channel_id=1, source_target_pairs={{16,0},{32,16},{48,32},{64,48},{80,64},{96,80},{112,96},{128,112},... | collective-permute-start | bytes 589832 | tf_op jit(solution)/shard_map/ppermute | solution.py:441
  90.6 7.3 %copy-start.3 = (f32[2,48,512]{2,1,0:T(8,128)}, f32[2,48,512]{2,1,0:T(8,128)S(1)}, u32[]{:S(2)}) copy-start(f32[2,48,512]{2,1,0:T(8,128)S(1)} %collective-permute-done.4.low_ref) | copy-start | bytes 589828
  97.9 0.7 copy-start.4

commit v2 on v1

--- a/solution.py
+++ b/solution.py
@@ -14,7 +14,7 @@
 LIFT = 0.5
 F32 = jnp.float32
 BF16 = jnp.bfloat16
-VMEM_BYTES = 60 * 1024 * 1024
+VMEM_BYTES = 32 * 1024 * 1024
 
 ROWS = 6
 COLS = 384
@@ -199,7 +199,7 @@
         out_ref[at] = jnp.where(keep, wind, wind - GRAD * (p_ref[at + 2] - p_ref[at]))
         return carry
 
-    lax.fori_loop(0, ROWS + 2 * U_DEEP, body, 0)
+    lax.fori_loop(0, ROWS + 2 * U_DEEP, body, 0, unroll=2)
 
 
 def column_step(held, gx, off_x, nx, table, u_ref, p_ref, v_of, w_of, s_of, put):
@@ -221,7 +221,7 @@
         put(at, wind, w_next, p_next)
         return carry
 
-    lax.fori_loop(0, WIN, body, 0)
+    lax.fori_loop(0, WIN, body, 0, unroll=6)
 
 
 def first_kernel(

time: 111 us -> 92.3 us (0.83)
  Pallas kernels: 33.6 us -> 13.8 us
  local copies, waits for them, and re-layouts: 2.56 us -> 4.08 us
    pallas_call x4, Pallas kernels: 33.6 us -> 13.8 us  [call(): pl.pallas_call(body, out_shape=[jax.ShapeDtypeStruct(shape, F32) for shap...]
    unnamed x14 -> x12, local copies, waits for them, and re-layouts: 2.55 us -> 4.07 us
  transfers between devices with their start and end apart: 6 -> 6, of which waited for: 6 -> 6; matrix products, arithmetic and copies ran while one was open for 1% -> 0% of each run, Pallas kernels for 0% -> 0%
where the time goes in v2:
time: 92.3 us; the launch traced here: 91.9 us
  waiting for transfers between devices  48.8 us (53%)
  starting transfers between devices  24.4 us (26%)
  Pallas kernels  13.8 us (15%)
  local copies, waits for them, and re-layouts  4.08 us (4%)
    ppermute x2, waiting for transfers between devices, per_device(): high = lax.ppermute(down, 'gx', steps('gx', -1))  42.5 us
    ppermute x2, starting transfers between devices, per_device(): low = lax.ppermute(up, 'gx', steps('gx', 1))  14.1 us
    pallas_call x4, Pallas kernels, call(): pl.pallas_call(body, out_shape=[jax.ShapeDtypeStruct(shape, F32) for shap...  13.8 us
    ppermute x2, starting transfers between devices, per_device(): high = lax.ppermute(down, 'gx', steps('gx', -1))  4.66 us
    ppermute x2, waiting for transfers between devices, per_device(): low = lax.ppermute(up, 'gx', steps('gx', 1))  4.39 us
    unnamed x12, local copies, waits for them, and re-layouts  4.07 us
    ppermute x1, starting transfers between devices, per_device(): from_right = lax.ppermute(to_left, 'gy', steps('gy', -1))  3.64 us
    ppermute x1, starting transfers between devices, per_device(): from_left = lax.ppermute(to_right, 'gy', steps('gy', 1))  1.92 us
  transfers between devices with their start and end apart: 6, of which 6 were waited for; matrix products, arithmetic and copies ran while one was open for 0% of the time, Pallas kernels for 0%

profile of v2, /device:TPU:214, one launch (start us, length us, event | category | flops | bytes accessed | tf_op | source)
XLA Modules:
  0.0 91.9 jit_solution(6792811650728662343)
XLA Ops:
  0.6 0.0 copy-start
  0.6 1.0 %copy-done = f32[48,6,384]{2,0,1:T(8,128)S(1)} copy-done((f32[48,6,384]{2,0,1:T(8,128)S(1)}, f32[48,6,384]{2,0,1:T(8,128)}, u32[]{:S(2)}) %copy-start) | copy-done | bytes 442392
  1.6 0.0 copy-start.1
  1.6 0.9 %copy-done.1 = f32[4,48,2,128]{3,2,1,0:T(2,128)S(1)} copy-done((f32[4,48,2,128]{3,2,1,0:T(2,128)S(1)}, f32[4,48,2,128]{3,2,1,0:T(2,128)}, u32[]{:S(2)}) %copy-start.1) | copy-done | bytes 196632
  2.6 0.0 copy-start.3
  2.6 1.5 %copy-done.3 = f32[4,48,6,384]{3,1,2,0:T(8,128)S(1)} copy-done((f32[4,48,6,384]{3,1,2,0:T(8,128)S(1)}, f32[4,48,6,384]{3,1,2,0:T(8,128)}, u32[]{:S(2)}) %copy-start.3) | copy-done | bytes 1769496
  4.0 0.0 copy-start.4
  4.1 0.7 copy-done.4
  4.7 0.0 copy-start.2
  4.7 1.4 %shard_map.68 = (f32[4,6,48,384]{3,2,1,0:T(8,128)S(1)}, f32[48,384]{1,0:T(8,128)S(1)}, f32[48,384]{1,0:T(8,128)S(1)}, f32[4,48,384]{2,1,0:T(8,128)S(1)}) custom-call(s32[2]{0:T(128)S(1)} %copy-done.4, f32[4,6,48,384]{3,2,1,0:T(8,128)S(1)} %bitcast.6, f32[6,48,384]{2,1,0:T(8,128)S(1)} %bitcast.3, f32[4,48,2,128]{3,2,1,0:T(2,128)S(1)} %copy-done.1), custom_call_target="tpu_custom_call" | custom-call | tf_op jit(solution)/shard_map/pallas_call | solution.py:385
  6.1 0.0 copy-start.5
  6.2 1.9 %collective-permute-start = (f32[48,384]{1,0:T(8,128)S(1)}, f32[48,384]{1,0:T(8,128)S(1)}, u32[]{:S(2)}, u32[]{:S(2)}) collective-permute-start(f32[48,384]{1,0:T(8,128)S(1)} %get-tuple-element.19), channel_id=1, source_target_pairs={{0,1},{1,2},{2,3},{3,4},{4,5},{5,6},{6,7},{7,8},{8,9},{9,10},{10,1... | collective-permute-start | bytes 221192 | tf_op jit(solution)/shard_map/ppermute | solution.py:420
  8.1 3.6 %collective-permute-start.1 = (f32[48,384]{1,0:T(8,128)S(1)}, f32[48,384]{1,0:T(8,128)S(1)}, u32[]{:S(2)}, u32[]{:S(2)}) collective-permute-start(f32[48,384]{1,0:T(8,128)S(1)} %get-tuple-element.20), channel_id=1, source_target_pairs={{1,0},{2,1},{3,2},{4,3},{5,4},{6,5},{7,6},{8,7},{9,8},{10,9},{11,1... | collective-permute-start | bytes 221192 | tf_op jit(solution)/shard_map/ppermute | solution.py:421
  11.7 0.1 collective-permute-done.left_ref
  11.8 1.9 %collective-permute-done.1.right_ref = f32[48,384]{1,0:T(8,128)S(1)} collective-permute-done((f32[48,384]{1,0:T(8,128)S(1)}, f32[48,384]{1,0:T(8,128)S(1)}, u32[]{:S(2)}, u32[]{:S(2)}) %collective-permute-start.1) | collective-permute-done | bytes 73760 | tf_op jit(solution)/shard_map/ppermute | solution.py:421
  13.7 0.0 copy-done.2
  13.7 0.2 shard_map.69
  13.9 2.7 %collective-permute-start.3 = (f32[23,48,384]{2,1,0:T(8,128)S(1)}, f32[23,48,384]{2,1,0:T(8,128)S(1)}, u32[]{:S(2)}, u32[]{:S(2)}) collective-permute-start(f32[23,48,384]{2,1,0:T(8,128)S(1)} %get-tuple-element.22), channel_id=1, source_target_pairs={{16,0},{32,16},{48,32},{64,48},{80,64},{96,80},{112,96},{128,112},... | collective-permute-start | bytes 5087240 | tf_op jit(solution)/shard_map/ppermute | solution.py:429
  16.7 6.4 %collective-permute-start.2 = (f32[23,48,384]{2,1,0:T(8,128)S(1)}, f32[23,48,384]{2,1,0:T(8,128)S(1)}, u32[]{:S(2)}, u32[]{:S(2)}) collective-permute-start(f32[23,48,384]{2,1,0:T(8,128)S(1)} %get-tuple-element.21.mine_ref), channel_id=1, source_target_pairs={{0,16},{16,32},{32,48},{48,64},{64,80},{80,96},{96,112},{112,128},... | collective-permute-start | bytes 5087240 | tf_op jit(solution)/shard_map/ppermute | solution.py:428
  23.1 0.0 copy-done.5
  23.2 0.1 pad_maximum_fusion.1.table_ref
  23.3 35.0 %collective-permute-done.3.high_ref = f32[23,48,384]{2,1,0:T(8,128)S(1)} collective-permute-done((f32[23,48,384]{2,1,0:T(8,128)S(1)}, f32[23,48,384]{2,1,0:T(8,128)S(1)}, u32[]{:S(2)}, u32[]{:S(2)}) %collective-permute-start.3) | collective-permute-done | bytes 1695776 | tf_op jit(solution)/shard_map/ppermute | solution.py:429
  58.3 1.8 %collective-permute-done.2.low_ref = f32[23,48,384]{2,1,0:T(8,128)S(1)} collective-permute-done((f32[23,48,384]{2,1,0:T(8,128)S(1)}, f32[23,48,384]{2,1,0:T(8,128)S(1)}, u32[]{:S(2)}, u32[]{:S(2)}) %collective-permute-start.2) | collective-permute-done | bytes 1695776 | tf_op jit(solution)/shard_map/ppermute | solution.py:428
  60.1 5.3 %shard_map.70 = (f32[14,48,512]{2,1,0:T(8,128)S(1)}, f32[12,48,512]{2,1,0:T(8,128)S(1)}, f32[12,48,512]{2,1,0:T(8,128)S(1)}, f32[12,48,512]{2,1,0:T(8,128)S(1)},...) custom-call(s32[2]{0:T(128)S(1)} %copy-done.4, ...), custom_call_target="tpu_custom_call" | custom-call | tf_op jit(solution)/shard_map/pallas_call | solution.py:385
  65.4 7.7 %collective-permute-start.4 = (f32[2,48,512]{2,1,0:T(8,128)S(1)}, f32[2,48,512]{2,1,0:T(8,128)S(1)}, u32[]{:S(2)}, u32[]{:S(2)}) collective-permute-start(f32[2,48,512]{2,1,0:T(8,128)S(1)} %get-tuple-element.28), channel_id=1, source_target_pairs={{0,16},{16,32},{32,48},{48,64},{64,80},{80,96},{96,112},{112,128},... | collective-permute-start | bytes 589832 | tf_op jit(solution)/shard_map/ppermute | solution.py:440
  73.1 1.9 %collective-permute-start.5 = (f32[2,48,512]{2,1,0:T(8,128)S(1)}, f32[2,48,512]{2,1,0:T(8,128)S(1)}, u32[]{:S(2)}, u32[]{:S(2)}) collective-permute-start(f32[2,48,512]{2,1,0:T(8,128)S(1)} %get-tuple-element.29), channel_id=1, source_target_pairs={{16,0},{32,16},{48,32},{64,48},{80,64},{96,80},{112,96},{128,112},... | collective-permute-start | bytes 589832 | tf_op jit(solution)/shard_map/ppermute | solution.py:441
  75.0 2.6 %collective-permute-done.4.low_ref = f32[2,48,512]{2,1,0:T(8,128)S(1)} collective-permute-done((f32[2,48,512]{2,1,0:T(8,128)S(1)}, f32[2,48,512]{2,1,0:T(8,128)S(1)}, u32[]{:S(2)}, u32[]{:S(2)}) %collective-permute-start.4) | collective-permute-done | bytes 196640 | tf_op jit(solution)/shard_map/ppermute | solution.py:440
  77.6 7.4 %collective-permute-done.5.high_ref = f32[2,48,512]{2,1,0:T(8,128)S(1)} collective-permute-done((f32[2,48,512]{2,1,0:T(8,128)S(1)}, f32[2,48,512]{2,1,0:T(8,128)S(1)}, u32[]{:S(2)}, u32[]{:S(2)}) %collective-permute-start.5) | collective-permute-done | bytes 196640 | tf_op jit(solution)/shard_map/ppermute | solution.py:441
  85.1 6.9 %shard_map.71 = (f32[4,6,48,384]{3,2,1,0:T(8,128)}, f32[4,48,2,128]{3,2,1,0:T(2,128)}) custom-call(s32[2]{0:T(128)S(1)} %copy-done.4, f32[14,48,512]{2,1,0:T(8,128)S(1)} %get-tuple-element.23.u_ref, f32[12,48,512]{2,1,0:T(8,128)S(1)} %get-tuple-element.24.v_ref, f32[12,48,512]{2,1,0:T(8,128)S(1)} %get-tuple-element.25.w_ref, ...), custom_call_target="tpu_custom_call" | custom-call | tf_op jit(solution)/shard_map/pallas_call | solution.py:385
  (3 shorter events, 0.0 us)
Async XLA Ops:
  0.6 1.0 %copy-start = (f32[48,6,384]{2,0,1:T(8,128)S(1)}, f32[48,6,384]{2,0,1:T(8,128)}, u32[]{:S(2)}) copy-start(f32[48,6,384]{2,0,1:T(8,128)} %param.6) | copy-start | bytes 1327108
  1.6 0.9 %copy-start.1 = (f32[4,48,2,128]{3,2,1,0:T(2,128)S(1)}, f32[4,48,2,128]{3,2,1,0:T(2,128)}, u32[]{:S(2)}) copy-start(f32[4,48,2,128]{3,2,1,0:T(2,128)} %parent_ref.5) | copy-start | bytes 589828
  2.6 1.5 %copy-start.3 = (f32[4,48,6,384]{3,1,2,0:T(8,128)S(1)}, f32[4,48,6,384]{3,1,2,0:T(8,128)}, u32[]{:S(2)}) copy-start(f32[4,48,6,384]{3,1,2,0:T(8,128)} %param.5) | copy-start | bytes 5308420
  4.0 0.7 copy-start.4
  4.7 9.0 %copy-start.2 = (f32[4,48,2,128]{3,2,1,0:T(2,128)S(1)}, f32[4,48,2,128]{3,2,1,0:T(2,128)}, u32[]{:S(2)}) copy-start(f32[4,48,2,128]{3,2,1,0:T(2,128)} %parent_ref.5) | copy-start | bytes 589828
  6.1 17.0 %copy-start.5 = (f32[48,48]{1,0:T(8,128)S(1)}, f32[48,48]{1,0:T(8,128)}, u32[]{:S(2)}) copy-start(f32[48,48]{1,0:T(8,128)} %param.8) | copy-start | bytes 27652
  6.2 5.7 %collective-permute-start = (f32[48,384]{1,0:T(8,128)S(1)}, f32[48,384]{1,0:T(8,128)S(1)}, u32[]{:S(2)}, u32[]{:S(2)}) collective-permute-start(f32[48,384]{1,0:T(8,128)S(1)} %get-tuple-element.19), channel_id=1, source_target_pairs={{0,1},{1,2},{2,3},{3,4},{4,5},{5,6},{6,7},{7,8},{8,9},{9,10},{10,1... | collective-permute-start | bytes 221192 | tf_op jit(solution)/shard_map/ppermute | solution.py:420
  8.1 5.6 %collective-permute-start.1 = (f32[48,384]{1,0:T(8,128)S(1)}, f32[48,384]{1,0:T(8,128)S(1)}, u32[]{:S(2)}, u32[]{:S(2)}) collective-permute-start(f32[48,384]{1,0:T(8,128)S(1)} %get-tuple-element.20), channel_id=1, source_target_pairs={{1,0},{2,1},{3,2},{4,3},{5,4},{6,5},{7,6},{8,7},{9,8},{10,9},{11,1... | collective-permute-start | bytes 221192 | tf_op jit(solution)/shard_map/ppermute | solution.py:421
  13.9 44.4 %collective-permute-start.3 = (f32[23,48,384]{2,1,0:T(8,128)S(1)}, f32[23,48,384]{2,1,0:T(8,128)S(1)}, u32[]{:S(2)}, u32[]{:S(2)}) collective-permute-start(f32[23,48,384]{2,1,0:T(8,128)S(1)} %get-tuple-element.22), channel_id=1, source_target_pairs={{16,0},{32,16},{48,32},{64,48},{80,64},{96,80},{112,96},{128,112},... | collective-permute-start | bytes 5087240 | tf_op jit(solution)/shard_map/ppermute | solution.py:429
  16.7 43.4 %collective-permute-start.2 = (f32[23,48,384]{2,1,0:T(8,128)S(1)}, f32[23,48,384]{2,1,0:T(8,128)S(1)}, u32[]{:S(2)}, u32[]{:S(2)}) collective-permute-start(f32[23,48,384]{2,1,0:T(8,128)S(1)} %get-tuple-element.21.mine_ref), channel_id=1, source_target_pairs={{0,16},{16,32},{32,48},{48,64},{64,80},{80,96},{96,112},{112,128},... | collective-permute-start | bytes 5087240 | tf_op jit(solution)/shard_map/ppermute | solution.py:428
  65.4 12.3 %collective-permute-start.4 = (f32[2,48,512]{2,1,0:T(8,128)S(1)}, f32[2,48,512]{2,1,0:T(8,128)S(1)}, u32[]{:S(2)}, u32[]{:S(2)}) collective-permute-start(f32[2,48,512]{2,1,0:T(8,128)S(1)} %get-tuple-element.28), channel_id=1, source_target_pairs={{0,16},{16,32},{32,48},{48,64},{64,80},{80,96},{96,112},{112,128},... | collective-permute-start | bytes 589832 | tf_op jit(solution)/shard_map/ppermute | solution.py:440
  73.1 12.0 %collective-permute-start.5 = (f32[2,48,512]{2,1,0:T(8,128)S(1)}, f32[2,48,512]{2,1,0:T(8,128)S(1)}, u32[]{:S(2)}, u32[]{:S(2)}) collective-permute-start(f32[2,48,512]{2,1,0:T(8,128)S(1)} %get-tuple-element.29), channel_id=1, source_target_pairs={{16,0},{32,16},{48,32},{64,48},{80,64},{96,80},{112,96},{128,112},... | collective-permute-start | bytes 589832 | tf_op jit(solution)/shard_map/ppermute | solution.py:441

commit v3 on v2

v3 whole, which is shorter than its diff:
```python
import functools

import jax
import jax.numpy as jnp
from jax import lax
from jax.experimental import pallas as pl
from jax.experimental.pallas import tpu as pltpu
from jax.sharding import PartitionSpec as P

RATIO = 3
GRAD = 0.25
DIV = 0.25
COUPLE = 0.25
LIFT = 0.5
F32 = jnp.float32
BF16 = jnp.bfloat16
VMEM_BYTES = 24 * 1024 * 1024

ROWS = 6
COLS = 384
LANES = 128
WIDE = COLS + LANES
SIDE = 8
SLOTS = LANES // SIDE
U, V, W, PR = 0, 1, 2, 3
DEEP = {PR: 5, U: 4, V: 3, W: 3}
NEAR = {PR: 2, U: 1}
KEEP = 3
S_GROUP = 4 * ROWS
EDGE_GROUP = S_GROUP + ROWS
GROUPS = EDGE_GROUP + 4
PACK = -(-GROUPS // SLOTS) * LANES
CHUNK_1 = ((V, 0, 3), (W, 0, 3), ("s", 0, 3))
CHUNK_2 = ((PR, 0, 2), (U, 0, 1), ("s", 3, 3))
CHUNK_3 = ((PR, 2, 3), (U, 1, 3))
SENT = [(PR, n) for n in range(5)] + [(U, n) for n in range(4)] + [(V, n) for n in range(3)]
SENT += [(W, n) for n in range(3)] + [("s", n) for n in range(6)]


def rows_of(chunk):
    return [(what, first + n) for what, first, count in chunk for n in range(count)]


def lanes_of(shape):
    return lax.broadcasted_iota(jnp.int32, shape, len(shape) - 1)


def column_of_lane(lane):
    return jnp.where(lane < COLS + LANES // 2, lane, lane - WIDE)


def is_edge(index, count):
    return (index < RATIO) | (index >= count - RATIO)


def expand_all(coarse):
    lane = lanes_of(coarse.shape)
    parts = [
        jnp.take_along_axis(coarse, (lane + first) // RATIO, axis=1) for first in range(0, COLS, LANES)
    ]
    return jnp.concatenate(parts, axis=1)


def turn(x, amount):
    amount = amount % x.shape[1]
    return x if amount == 0 else pltpu.roll(x, amount, 1)


def next_col(x):
    return pltpu.roll(x, x.shape[1] - 1, 1)


def prev_col(x):
    return pltpu.roll(x, 1, 1)


def level_up(x):
    levels = x.shape[0]
    level = lax.broadcasted_iota(jnp.int32, x.shape, 0)
    return jnp.where(level < levels - 1, pltpu.roll(x, levels - 1, 0), 0.0)


def level_down(x):
    level = lax.broadcasted_iota(jnp.int32, x.shape, 0)
    return jnp.where(level > 0, pltpu.roll(x, 1, 0), 0.0)


def split_dot(table, x):
    high = x.astype(BF16)
    low = (x - high.astype(F32)).astype(BF16)
    stacked = jnp.concatenate([high, low, high], axis=0)
    return jnp.dot(table, stacked, preferred_element_type=F32)


def own_row(near, side):
    return ROWS - 1 - near if side == 0 else near


def prepare_kernel(
    counts, off_ref, nest_ref, stiff_hbm, parent_hbm,
    cur_ref, stiff_ref, parent_ref, left_ref, right_ref, edge_ref, up_ref, down_ref,
    nest_win, parent_win, sems,
):
    nx, ny = counts
    copies = [pltpu.make_async_copy(parent_hbm, parent_win, sems.at[4])]
    copies += [pltpu.make_async_copy(nest_ref.at[f], nest_win.at[f], sems.at[f]) for f in (V, W, PR, U)]
    copies.append(pltpu.make_async_copy(stiff_hbm, stiff_ref, sems.at[5]))
    for copy in copies:
        copy.start()
    gx, gy = lax.axis_index("gx"), lax.axis_index("gy")
    off_x, off_y = off_ref[0], off_ref[1]
    levels = nest_win.shape[2]
    col = lanes_of((levels, COLS)) + (gy * COLS - RATIO * off_y)
    edge_col = is_edge(col, ny)
    place = lanes_of((levels, LANES)) // SIDE
    packs = [[None, None] for _ in range(PACK // LANES)]

    def pack(row, group):
        tile, slot = group // SLOTS, group % SLOTS
        sides = (
            turn(row[:, :LANES], SIDE * slot),
            turn(row[:, COLS - LANES :], SIDE * (slot + 1) - LANES),
        )
        for side, value in enumerate(sides):
            held = packs[tile][side]
            packs[tile][side] = value if held is None else jnp.where(place == slot, value, held)

    copies[0].wait()
    rims = []
    for at, field in enumerate((V, W, PR, U)):
        bounds = []
        for coarse in range(ROWS // RATIO):
            value = parent_win[field, :, coarse, :]
            parent_ref[field, coarse] = value
            bounds.append(expand_all(value))
        copies[1 + at].wait()
        for row in range(ROWS):
            i = gx * ROWS + row - RATIO * off_x
            held = is_edge(i, nx).astype(jnp.int32)
            value = jnp.where(edge_col | (held > 0), bounds[row // RATIO], nest_win[field, row])
            cur_ref[field, row] = value
            pack(value, field * ROWS + row)
        rim = jnp.where(gx == 0, bounds[0], bounds[-1])
        edge_ref[field] = rim
        pack(rim, EDGE_GROUP + field)
    copies[5].wait()
    for row in range(ROWS):
        pack(stiff_ref[row], S_GROUP + row)
    for tile, (left, right) in enumerate(packs):
        at = slice(LANES * tile, LANES * (tile + 1))
        left_ref[:, at] = left
        right_ref[:, at] = right
    fill_message(CHUNK_1, cur_ref, stiff_ref, up_ref, down_ref)


def fill_message(chunk, cur_ref, stiff_ref, up_ref, down_ref):
    for side, out in ((0, up_ref), (1, down_ref)):
        for at, (what, near) in enumerate(rows_of(chunk)):
            row = own_row(near, side)
            out[at] = stiff_ref[row] if what == "s" else cur_ref[what, row]


def group_of(what, row):
    return S_GROUP + row if what == "s" else what * ROWS + row


def near_kernel(last_y, cur_ref, stiff_ref, parent_ref, left_ref, right_ref, mine_ref, up_ref, down_ref):
    gx, gy = lax.axis_index("gx"), lax.axis_index("gy")
    levels = left_ref.shape[0]
    lane = lanes_of((levels, LANES))
    place = lane // SIDE
    mine_ref[0] = left_ref[...]
    mine_ref[1] = right_ref[...]

    def fill(side, cell):
        for tile in range(PACK // LANES):
            at = slice(LANES * tile, LANES * (tile + 1))
            out = mine_ref[side, :, at]
            for slot in range(SLOTS):
                group = tile * SLOTS + slot
                if group < S_GROUP:
                    value = parent_ref[group // ROWS, (group % ROWS) // RATIO, :, cell : cell + 1]
                elif EDGE_GROUP <= group < GROUPS:
                    field = group - EDGE_GROUP
                    value = jnp.where(
                        gx == 0,
                        parent_ref[field, 0, :, cell : cell + 1],
                        parent_ref[field, ROWS // RATIO - 1, :, cell : cell + 1],
                    )
                else:
                    continue
                out = jnp.where(place == slot, value, out)
            mine_ref[side, :, at] = out

    @pl.when(gy == 0)
    def _():
        fill(0, 0)

    @pl.when(gy == last_y)
    def _():
        fill(1, COLS // RATIO - 1)

    rows = rows_of(CHUNK_2)
    fill_message(CHUNK_2, cur_ref, stiff_ref, up_ref, down_ref)
    for side, out in ((0, up_ref), (1, down_ref)):
        tiles = [None] * (COLS // LANES)
        for hand in range(2):
            for at, (what, near) in enumerate(SENT):
                group = group_of(what, own_row(near, side))
                tile, slot = group // SLOTS, group % SLOTS
                target = hand * len(SENT) + at
                to_tile, to_slot = target // SLOTS, target % SLOTS
                value = turn(mine_ref[hand, :, LANES * tile : LANES * (tile + 1)], SIDE * (to_slot - slot))
                held = tiles[to_tile]
                tiles[to_tile] = value if held is None else jnp.where(place == to_slot, value, held)
        for tile, value in enumerate(tiles):
            out[len(rows), :, LANES * tile : LANES * (tile + 1)] = value


def beside(left, left_slot, right, right_slot):
    lane = lanes_of(left.shape)
    return jnp.where(
        lane < LANES // 2, turn(right, -SIDE * right_slot), turn(left, LANES - SIDE * (left_slot + 1))
    )


def mine_beside(mine_ref, group):
    tile, slot = group // SLOTS, group % SLOTS
    at = slice(LANES * tile, LANES * (tile + 1))
    return beside(mine_ref[0, :, at], slot, mine_ref[1, :, at], slot)


def sent_beside(near_ref, what, near):
    row = len(rows_of(CHUNK_2))
    index = SENT.index((what, near))
    tiles = []
    for target in (index, len(SENT) + index):
        tile = target // SLOTS
        tiles += [near_ref[row, :, LANES * tile : LANES * (tile + 1)], target % SLOTS]
    return beside(*tiles)


def far_kernel(
    cur_ref, stiff_ref, edge_ref, mine_ref, low1, high1, up_ref, down_ref, own_ref, own_s_ref, rim_ref
):
    del low1, high1
    fill_message(CHUNK_3, cur_ref, stiff_ref, up_ref, down_ref)
    for field in range(4):
        for row in range(ROWS):
            own_ref[field, row, :, :COLS] = cur_ref[field, row]
            own_ref[field, row, :, COLS:] = mine_beside(mine_ref, field * ROWS + row)
        rim_ref[field, :, :COLS] = edge_ref[field]
        rim_ref[field, :, COLS:] = mine_beside(mine_ref, EDGE_GROUP + field)
    for row in range(ROWS):
        own_s_ref[row, :, :COLS] = stiff_ref[row]
        own_s_ref[row, :, COLS:] = mine_beside(mine_ref, S_GROUP + row)


def received(refs, near_ref, what, near):
    for chunk, ref in zip((CHUNK_1, CHUNK_2, CHUNK_3), refs):
        rows = rows_of(chunk)
        if (what, near) in rows:
            main = ref[rows.index((what, near))]
    return jnp.concatenate([main, sent_beside(near_ref, what, near)], axis=1)


class Place:
    def __init__(self, counts, off_ref, levels):
        self.nx, self.ny = counts
        self.gx, self.gy = lax.axis_index("gx"), lax.axis_index("gy")
        self.off_x, self.off_y = off_ref[0], off_ref[1]
        j = column_of_lane(lanes_of((levels, WIDE))) + (self.gy * COLS - RATIO * self.off_y)
        self.held = is_edge(j, self.ny).astype(jnp.int32)

    def keep(self, row):
        i = self.gx * ROWS + row - RATIO * self.off_x
        return (self.held + is_edge(i, self.nx).astype(jnp.int32)) > 0

    def field_row(self, own, low, high, rim_ref, field, row):
        if 0 <= row < ROWS:
            return own[field, row]
        if row < 0:
            value = received(low, low[1], field, -1 - row)
            outer = self.gx == 0
        else:
            value = received(high, high[1], field, row - ROWS)
            outer = self.gx == self.nx // ROWS - 1
        return jnp.where(outer, rim_ref[field], value)


def wind_x(keep, wind, p_low, p_high):
    return jnp.where(keep, wind, wind - GRAD * (p_high - p_low))


def column_step(keep, table, pressure, u_low, u_high, wind, lift, stiffness):
    levels = pressure.shape[0]
    wind = jnp.where(keep, wind, wind - GRAD * (next_col(pressure) - prev_col(pressure)))
    divergence = (u_high - u_low) + (next_col(wind) - prev_col(wind))
    right_side = pressure - DIV * divergence - COUPLE * (level_up(lift) - level_down(lift))
    both = split_dot(table, right_side)
    first, around = both[:levels], both[levels:]
    leftover = right_side - ((1.0 + stiffness) * first - 0.25 * around)
    solved = first + split_dot(table[:levels], leftover)
    p_next = jnp.where(keep, pressure, solved)
    w_next = jnp.where(keep, lift, lift - LIFT * (level_up(p_next) - p_next))
    return wind, w_next, p_next


def own_kernel(
    counts, off_ref, own_ref, own_s_ref, rim_ref, low1, low2, high1, high2, table_ref,
    u_out, v_out, w_out, p_out, up_ref, down_ref,
    p_win, s_win,
):
    levels = own_ref.shape[2]
    at = Place(counts, off_ref, levels)
    low, high = (low1, low2, None), (high1, high2, None)
    deep = NEAR[PR]
    for row in range(-deep, ROWS + deep):
        p_win[row + deep] = at.field_row(own_ref, low, high, rim_ref, PR, row)
    for near in range(KEEP):
        s_win[KEEP - 1 - near] = received(low, low2, "s", near)
        s_win[KEEP + ROWS + near] = received(high, high2, "s", near)
    for row in range(ROWS):
        s_win[KEEP + row] = own_s_ref[row]
    for row in range(-1, ROWS + 1):
        wind = at.field_row(own_ref, low, high, rim_ref, U, row)
        u_out[row + 1] = wind_x(at.keep(row), wind, p_win[row + deep - 1], p_win[row + deep + 1])
    move_y = lax.rem(RATIO * at.off_y + WIDE, WIDE)
    table = table_ref[...]

    def body(row, carry):
        stiffness = pltpu.roll(s_win[row + KEEP - RATIO * at.off_x], move_y, 1)
        v_out[row], w_out[row], p_out[row] = column_step(
            at.keep(row), table, p_win[row + deep], u_out[row], u_out[row + 2],
            own_ref[V, row], own_ref[W, row], stiffness,
        )
        return carry

    lax.fori_loop(0, ROWS, body, 0, unroll=ROWS)
    for out, first in ((up_ref, 1), (down_ref, 3)):
        beyond = None
        for n in range(2):
            value = p_out[first + n]
            for tile in range(COLS // LANES):
                out[n * (COLS // LANES) + tile] = value[:, LANES * tile : LANES * (tile + 1)]
            ext = value[:, COLS:]
            beyond = ext if n == 0 else merge_ext(beyond, ext)
        out[2 * (COLS // LANES)] = beyond


def merge_ext(first, second):
    lane = lanes_of(first.shape)
    near = jnp.where(lane < LANES // 2, turn(second, SIDE), turn(second, -SIDE))
    return jnp.where((lane < SIDE) | (lane >= LANES - SIDE), first, near)


def split_ext(merged, n):
    if n == 0:
        return merged
    lane = lanes_of(merged.shape)
    return jnp.where(lane < LANES // 2, turn(merged, -SIDE), turn(merged, SIDE))


def halo_kernel(
    counts, off_ref, own_ref, own_s_ref, rim_ref, low1, low2, low3, high1, high2, high3, table_ref,
    u_own, v_own, w_own, p_own,
    u_rim, v_rim, w_rim, p_rim, s_rim, u_out, v_out, w_out, p_out,
    p_win, s_win, s_mid,
):
    levels = own_ref.shape[2]
    at = Place(counts, off_ref, levels)
    low, high = (low1, low2, low3), (high1, high2, high3)
    table = table_ref[...]
    deep = DEEP[PR]
    for n in range(deep + 1):
        p_win[n] = at.field_row(own_ref, low, high, rim_ref, PR, n - deep)
        p_win[deep + 1 + n] = at.field_row(own_ref, low, high, rim_ref, PR, ROWS - 1 + n)
    for near in range(ROWS):
        s_win[ROWS - 1 - near] = received(low, low2, "s", near)
        s_win[2 * ROWS + near] = received(high, high2, "s", near)
        s_win[ROWS + near] = own_s_ref[near]
    move_y = lax.rem(RATIO * at.off_y + WIDE, WIDE)

    def stiffness(row):
        return pltpu.roll(s_win[row + ROWS - RATIO * at.off_x], move_y, 1)

    def p_before(row):
        return p_win[row + deep] if row <= 0 else p_win[row - ROWS + 1 + deep + 1]

    def rim_of(depth, row):
        return row + depth if row < 0 else row - ROWS + depth

    for row in (-4, -3, -2, 7, 8, 9):
        wind = at.field_row(own_ref, low, high, rim_ref, U, row)
        u_rim[rim_of(4, row)] = wind_x(at.keep(row), wind, p_before(row - 1), p_before(row + 1))

    def u_after(row):
        return u_own[row + 1] if -1 <= row <= ROWS else u_rim[rim_of(4, row)]

    outer = (-3, -2, -1, 6, 7, 8)
    for row in outer:
        n = rim_of(KEEP, row)
        stiff = stiffness(row)
        if row in (-3, -2, 7, 8):
            s_rim[(-3, -2, 7, 8).index(row)] = stiff
        else:
            s_mid[0 if row < 0 else ROWS + 1] = stiff
        v_rim[n], w_rim[n], p_rim[n] = column_step(
            at.keep(row), table, p_before(row), u_after(row - 1), u_after(row + 1),
            at.field_row(own_ref, low, high, rim_ref, V, row),
            at.field_row(own_ref, low, high, rim_ref, W, row),
            stiff,
        )
    for row in range(ROWS):
        s_mid[row + 1] = stiffness(row)

    def pick(own, rim, row):
        return own[row] if 0 <= row < ROWS else rim[rim_of(KEEP, row)]

    for row in range(-2, ROWS + 2):
        u_out[row + 2] = wind_x(
            at.keep(row), u_after(row), pick(p_own, p_rim, row - 1), pick(p_own, p_rim, row + 1)
        )
    for row in range(-1, ROWS + 1):
        v_out[row + 1], w_out[row + 1], p_out[row + 1] = column_step(
            at.keep(row), table, pick(p_own, p_rim, row), u_out[row + 1], u_out[row + 3],
            pick(v_own, v_rim, row), pick(w_own, w_rim, row), s_mid[row + 1],
        )


def last_kernel(
    counts, off_ref, u_rim, v_rim, w_rim, p_rim, s_rim, u_mid, v_mid, w_mid, p_mid,
    low_ref, high_ref, table_ref, parent_ref,
    new_ref, back_ref,
    u_win, v_win, w_win, q_win,
):
    levels = u_rim.shape[1]
    at = Place(counts, off_ref, levels)
    table = table_ref[...]
    tiles = COLS // LANES

    def sent(ref, n):
        parts = [ref[n * tiles + tile] for tile in range(tiles)] + [split_ext(ref[2 * tiles], n)]
        return jnp.concatenate(parts, axis=1)

    for row in range(ROWS + 4):
        u_win[row + 2] = u_mid[row]
    for row in range(ROWS + 2):
        v_win[row + 2] = v_mid[row]
        w_win[row + 2] = w_mid[row]
        q_win[row + 2] = p_mid[row]
    low_p = [sent(low_ref, 0), sent(low_ref, 1), p_rim[0], p_rim[1]]
    high_p = [p_rim[4], p_rim[5], sent(high_ref, 0), sent(high_ref, 1)]
    for n, row in enumerate((-4, -3)):
        u_win[n] = wind_x(at.keep(row), u_rim[n], low_p[n], low_p[n + 2])
    for n, row in enumerate((8, 9)):
        u_win[12 + n] = wind_x(at.keep(row), u_rim[6 + n], high_p[n], high_p[n + 2])
    for n, row in enumerate((-3, -2, 7, 8)):
        rim = (0, 1, 4, 5)[n]
        v_win[row + KEEP], w_win[row + KEEP], q_win[row + KEEP] = column_step(
            at.keep(row), table, p_rim[rim], u_win[row + 3], u_win[row + 5],
            v_rim[rim], w_rim[rim], s_rim[n],
        )
    windows = ((U, u_win, 4), (V, v_win, KEEP), (W, w_win, KEEP), (PR, q_win, KEEP))
    finish(at, windows, parent_ref, new_ref, back_ref)


def finish(at, windows, parent_ref, new_ref, back_ref):
    levels = parent_ref.shape[2]
    move_y = lax.rem(WIDE - RATIO * at.off_y, WIDE)
    for field, window, deep in windows:
        for row in range(ROWS):
            moved = pltpu.roll(window[row + deep + RATIO * at.off_x], move_y, 1)
            new_ref[field, row] = moved[:, :COLS]

    cells_x, cells_y = at.nx // RATIO, at.ny // RATIO
    coarse_rows, coarse_cols = ROWS // RATIO, COLS // RATIO

    def inside(index, count):
        return (index >= 1) & (index <= count - 2)

    source = column_of_lane(lax.broadcasted_iota(jnp.int32, (WIDE, coarse_cols), 0))
    apart = source - RATIO * lax.broadcasted_iota(jnp.int32, (WIDE, coarse_cols), 1)
    spread = jnp.where(
        (apart >= 0) & (apart < RATIO),
        0.5,
        jnp.where((apart >= -RATIO) & (apart < 2 * RATIO), 0.25, 0.0),
    ).astype(BF16)
    cell = lanes_of((levels, coarse_cols)) + (at.gy * coarse_cols - at.off_y)
    weight_y = (
        0.25 * inside(cell - 1, cells_y).astype(F32)
        + 0.5 * inside(cell, cells_y).astype(F32)
        + 0.25 * inside(cell + 1, cells_y).astype(F32)
    )
    centre_y = inside(cell, cells_y).astype(jnp.int32)
    for coarse in range(coarse_rows):
        a = at.gx * coarse_rows + coarse - at.off_x
        inner = [inside(a + d, cells_x).astype(F32) for d in (-1, 0, 1)]
        weights = [s * m for s, m in zip((0.25, 0.5, 0.25), inner)]
        weight_x = weights[0] + weights[1] + weights[2]
        centre = (centre_y * inside(a, cells_x).astype(jnp.int32)) > 0
        scale = jnp.where(centre, 1.0 / jnp.where(centre, 9.0 * weight_x * weight_y, 1.0), 0.0)
        for field, window, deep in windows:
            start = deep - KEEP + RATIO * coarse
            total = None
            for d in range(3):
                part = window[start + 3 * d] + window[start + 3 * d + 1] + window[start + 3 * d + 2]
                part = jnp.where(inner[d] > 0, part * weights[d], 0.0)
                total = part if total is None else total + part
            total = jnp.where(at.held > 0, 0.0, total)
            high = total.astype(BF16)
            low = (total - high.astype(F32)).astype(BF16)
            summed = jnp.dot(high, spread, preferred_element_type=F32) + jnp.dot(
                low, spread, preferred_element_type=F32
            )
            back_ref[field, :, coarse, :] = jnp.where(centre, summed * scale, parent_ref[field, coarse])


def call(body, ins, outs, scratch=(), spaces=None):
    def space(x):
        if x.dtype == jnp.int32:
            return pltpu.SMEM
        return pltpu.VMEM

    spaces = spaces or [space(x) for x in ins]
    return pl.pallas_call(
        body,
        out_shape=[jax.ShapeDtypeStruct(shape, F32) for shape in outs],
        in_specs=[pl.BlockSpec(memory_space=s) for s in spaces],
        out_specs=[pl.BlockSpec(memory_space=pltpu.VMEM) for _ in outs],
        scratch_shapes=[s if not isinstance(s, tuple) else pltpu.VMEM(s, F32) for s in scratch],
        compiler_params=pltpu.CompilerParams(vmem_limit_bytes=VMEM_BYTES),
    )(*ins)


def exchange(up, down, axis):
    count = lax.axis_size(axis)
    forward = [(i, i + 1) for i in range(count - 1)]
    low = lax.ppermute(up, axis, forward)
    high = lax.ppermute(down, axis, [(target, source) for source, target in forward])
    return low, high


def per_device(nest_state, stiffness, parent, inverse_table, offsets):
    levels = nest_state.shape[1]
    nx = nest_state.shape[2] * lax.axis_size("gx")
    ny = nest_state.shape[3] * lax.axis_size("gy")
    counts = (nx, ny)
    nest = jnp.transpose(nest_state, (0, 2, 1, 3))
    stiff_in = jnp.transpose(stiffness, (1, 0, 2))

    nothing = jnp.zeros_like(inverse_table[:1])
    shifted = jnp.concatenate([inverse_table[1:], nothing], 0)
    shifted += jnp.concatenate([nothing, inverse_table[:-1]], 0)
    stack = jnp.concatenate([inverse_table, shifted], 0)
    top = lax.reduce_precision(stack, 8, 7)
    table = jnp.concatenate([top, top, stack - top], 1).astype(BF16)

    def rows(count, width=WIDE):
        return (count, levels, width)

    first, near, far = (len(rows_of(chunk)) for chunk in (CHUNK_1, CHUNK_2, CHUNK_3))
    cur, stiff, coarse, to_left, to_right, edge, up, down = call(
        functools.partial(prepare_kernel, counts),
        [pltpu.with_memory_space_constraint(x, pltpu.HBM) for x in (offsets, nest, stiff_in, parent)],
        [nest.shape, stiff_in.shape, (4, ROWS // RATIO, levels, LANES), (levels, PACK), (levels, PACK)]
        + [(4, levels, COLS), rows(first, COLS), rows(first, COLS)],
        [nest.shape, parent.shape, pltpu.SemaphoreType.DMA((6,))],
        [pltpu.SMEM, pltpu.HBM, pltpu.HBM, pltpu.HBM],
    )
    low1, high1 = exchange(up, down, "gx")
    from_left, from_right = exchange(to_right, to_left, "gy")
    mine, up, down = call(
        functools.partial(near_kernel, lax.axis_size("gy") - 1),
        (cur, stiff, coarse, from_left, from_right),
        [(2, levels, PACK), rows(near + 1, COLS), rows(near + 1, COLS)],
    )
    low2, high2 = exchange(up, down, "gx")
    up, down, own, own_s, rim = call(
        far_kernel,
        (cur, stiff, edge, mine, low1, high1),
        [rows(far, COLS), rows(far, COLS), (4, ROWS, levels, WIDE), rows(ROWS), rows(4)],
    )
    low3, high3 = exchange(up, down, "gx")
    message = (2 * (COLS // LANES) + 1, levels, LANES)
    u1, v1, w1, p1, up, down = call(
        functools.partial(own_kernel, counts),
        (offsets, own, own_s, rim, low1, low2, high1, high2, table),
        [rows(ROWS + 2), rows(ROWS), rows(ROWS), rows(ROWS), message, message],
        [rows(ROWS + 4), rows(2 * ROWS)],
    )
    low4, high4 = exchange(up, down, "gx")
    outer = call(
        functools.partial(halo_kernel, counts),
        (offsets, own, own_s, rim, low1, low2, low3, high1, high2, high3, table, u1, v1, w1, p1),
        [rows(8), rows(6), rows(6), rows(6), rows(4), rows(ROWS + 4), rows(ROWS + 2), rows(ROWS + 2), rows(ROWS + 2)],
        [rows(12), rows(3 * ROWS), rows(ROWS + 2)],
    )
    new, back = call(
        functools.partial(last_kernel, counts),
        (offsets, *outer, low4, high4, table, coarse),
        [nest.shape, parent.shape],
        [rows(ROWS + 8), rows(ROWS + 6), rows(ROWS + 6), rows(ROWS + 6)],
    )
    return jnp.transpose(new, (0, 2, 1, 3)), back


def solution(mesh):
    return jax.shard_map(
        per_device,
        mesh=mesh,
        in_specs=(
            P(None, None, "gx", "gy"),
            P(None, "gx", "gy"),
            P(None, None, "gx", "gy"),
            P(),
            P(),
        ),
        out_specs=(P(None, None, "gx", "gy"), P(None, None, "gx", "gy")),
        check_vma=False,
    )
```

time: 92.3 us -> 66.8 us (0.72)
  the two profiles are of different devices: /device:TPU:214 before, /device:TPU:230 now
where the time goes in v3:
time: 66.8 us; the launch traced here: 66.4 us
  starting transfers between devices  36.9 us (55%)
  Pallas kernels  15.3 us (23%)
  waiting for transfers between devices  13.2 us (20%)
  between operations  0.83 us (1%)
    ppermute x5, starting transfers between devices, exchange(): low = lax.ppermute(up, axis, forward)  22.4 us
    pallas_call x6, Pallas kernels, call(): pl.pallas_call(body, out_shape=[jax.ShapeDtypeStruct(shape, F32) for shap...  15.3 us
    ppermute x5, starting transfers between devices, exchange(): lax.ppermute(down, axis, [(target, source) for source, target in forward])  14.5 us
    ppermute x5, waiting for transfers between devices, exchange(): lax.ppermute(down, axis, [(target, source) for source, target in forward])  12.9 us
  transfers between devices with their start and end apart: 10, of which 6 were waited for; matrix products, arithmetic and copies ran while one was open for 0% of the time, Pallas kernels for 12%

profile of v3, /device:TPU:230, one launch (start us, length us, event | category | flops | bytes accessed | tf_op | source)
XLA Modules:
  0.0 66.4 jit_solution(4831924487412319051)
XLA Ops:
  0.6 2.9 %shard_map.68 = (f32[4,6,48,384]{3,2,1,0:T(8,128)S(1)}, f32[6,48,384]{2,1,0:T(8,128)S(1)}, f32[4,2,48,128]{3,2,1,0:T(8,128)S(1)}, f32[48,384]{1,0:T(8,128)S(1)},...) custom-call(s32[2]{0:T(128)} %off_ref.7, ...), custom_call_target="tpu_custom_call" | custom-call | tf_op jit(solution)/shard_map/pallas_call | solution.py:526
  3.5 0.0 copy-start.1
  3.6 5.4 %collective-permute-start.2 = (f32[9,48,384]{2,1,0:T(8,128)S(1)}, f32[9,48,384]{2,1,0:T(8,128)S(1)}, u32[]{:S(2)}, u32[]{:S(2)}) collective-permute-start(f32[9,48,384]{2,1,0:T(8,128)S(1)} %get-tuple-element.42), channel_id=1, source_target_pairs={{0,16},{16,32},{32,48},{48,64},{64,80},{80,96},{96,112},{112,128},... | collective-permute-start | bytes 1990664 | tf_op jit(solution)/shard_map/ppermute | solution.py:539
  9.0 1.9 %collective-permute-start.3 = (f32[9,48,384]{2,1,0:T(8,128)S(1)}, f32[9,48,384]{2,1,0:T(8,128)S(1)}, u32[]{:S(2)}, u32[]{:S(2)}) collective-permute-start(f32[9,48,384]{2,1,0:T(8,128)S(1)} %get-tuple-element.43), channel_id=1, source_target_pairs={{16,0},{32,16},{48,32},{64,48},{80,64},{96,80},{112,96},{128,112},... | collective-permute-start | bytes 1990664 | tf_op jit(solution)/shard_map/ppermute | solution.py:540
  10.9 1.9 %collective-permute-start = (f32[48,384]{1,0:T(8,128)S(1)}, f32[48,384]{1,0:T(8,128)S(1)}, u32[]{:S(2)}, u32[]{:S(2)}) collective-permute-start(f32[48,384]{1,0:T(8,128)S(1)} %get-tuple-element.39), channel_id=1, source_target_pairs={{0,1},{1,2},{2,3},{3,4},{4,5},{5,6},{6,7},{7,8},{8,9},{9,10},{10,1... | collective-permute-start | bytes 221192 | tf_op jit(solution)/shard_map/ppermute | solution.py:539
  12.8 4.9 %collective-permute-start.1 = (f32[48,384]{1,0:T(8,128)S(1)}, f32[48,384]{1,0:T(8,128)S(1)}, u32[]{:S(2)}, u32[]{:S(2)}) collective-permute-start(f32[48,384]{1,0:T(8,128)S(1)} %get-tuple-element.40), channel_id=1, source_target_pairs={{1,0},{2,1},{3,2},{4,3},{5,4},{6,5},{7,6},{8,7},{9,8},{10,9},{11,1... | collective-permute-start | bytes 221192 | tf_op jit(solution)/shard_map/ppermute | solution.py:540
  17.7 0.1 collective-permute-done.left_ref
  17.8 1.9 %collective-permute-done.1.right_ref = f32[48,384]{1,0:T(8,128)S(1)} collective-permute-done((f32[48,384]{1,0:T(8,128)S(1)}, f32[48,384]{1,0:T(8,128)S(1)}, u32[]{:S(2)}, u32[]{:S(2)}) %collective-permute-start.1) | collective-permute-done | bytes 73760 | tf_op jit(solution)/shard_map/ppermute | solution.py:540
  19.6 0.3 shard_map.69
  20.0 7.2 %collective-permute-start.4 = (f32[7,48,384]{2,1,0:T(8,128)S(1)}, f32[7,48,384]{2,1,0:T(8,128)S(1)}, u32[]{:S(2)}, u32[]{:S(2)}) collective-permute-start(f32[7,48,384]{2,1,0:T(8,128)S(1)} %get-tuple-element.47), channel_id=1, source_target_pairs={{0,16},{16,32},{32,48},{48,64},{64,80},{80,96},{96,112},{112,128},... | collective-permute-start | bytes 1548296 | tf_op jit(solution)/shard_map/ppermute | solution.py:539
  27.2 1.9 %collective-permute-start.6 = (f32[7,48,384]{2,1,0:T(8,128)S(1)}, f32[7,48,384]{2,1,0:T(8,128)S(1)}, u32[]{:S(2)}, u32[]{:S(2)}) collective-permute-start(f32[7,48,384]{2,1,0:T(8,128)S(1)} %get-tuple-element.49), channel_id=1, source_target_pairs={{16,0},{32,16},{48,32},{64,48},{80,64},{96,80},{112,96},{128,112},... | collective-permute-start | bytes 1548296 | tf_op jit(solution)/shard_map/ppermute | solution.py:540
  29.2 0.0 copy-done.1
  29.2 0.0 collective-permute-done.2.low1
  29.2 1.3 %collective-permute-done.3.high1 = f32[9,48,384]{2,1,0:T(8,128)S(1)} collective-permute-done((f32[9,48,384]{2,1,0:T(8,128)S(1)}, f32[9,48,384]{2,1,0:T(8,128)S(1)}, u32[]{:S(2)}, u32[]{:S(2)}) %collective-permute-start.3) | collective-permute-done | bytes 663584 | tf_op jit(solution)/shard_map/ppermute | solution.py:540
  30.6 0.0 copy-start
  30.6 0.6 shard_map.70
  31.1 5.9 %collective-permute-start.5 = (f32[6,48,384]{2,1,0:T(8,128)S(1)}, f32[6,48,384]{2,1,0:T(8,128)S(1)}, u32[]{:S(2)}, u32[]{:S(2)}) collective-permute-start(f32[6,48,384]{2,1,0:T(8,128)S(1)} %get-tuple-element.48), channel_id=1, source_target_pairs={{0,16},{16,32},{32,48},{48,64},{64,80},{80,96},{96,112},{112,128},... | collective-permute-start | bytes 1327112 | tf_op jit(solution)/shard_map/ppermute | solution.py:539
  37.1 1.9 %collective-permute-start.7 = (f32[6,48,384]{2,1,0:T(8,128)S(1)}, f32[6,48,384]{2,1,0:T(8,128)S(1)}, u32[]{:S(2)}, u32[]{:S(2)}) collective-permute-start(f32[6,48,384]{2,1,0:T(8,128)S(1)} %get-tuple-element.50), channel_id=1, source_target_pairs={{16,0},{32,16},{48,32},{64,48},{80,64},{96,80},{112,96},{128,112},... | collective-permute-start | bytes 1327112 | tf_op jit(solution)/shard_map/ppermute | solution.py:540
  39.0 0.1 pad_maximum_fusion.1.table_ref
  39.1 0.2 collective-permute-done.4.low2
  39.4 7.8 %collective-permute-done.6.high2 = f32[7,48,384]{2,1,0:T(8,128)S(1)} collective-permute-done((f32[7,48,384]{2,1,0:T(8,128)S(1)}, f32[7,48,384]{2,1,0:T(8,128)S(1)}, u32[]{:S(2)}, u32[]{:S(2)}) %collective-permute-start.6) | collective-permute-done | bytes 516128 | tf_op jit(solution)/shard_map/ppermute | solution.py:540
  47.1 0.0 copy-done
  47.1 2.5 %shard_map.71 = (f32[8,48,512]{2,1,0:T(8,128)S(1)}, f32[6,48,512]{2,1,0:T(8,128)S(1)}, f32[6,48,512]{2,1,0:T(8,128)S(1)}, f32[6,48,512]{2,1,0:T(8,128)S(1)}, f32...) custom-call(s32[2]{0:T(128)S(1)} %copy-done, f32[4,6,48,512]{3,2,1,0:T(8,128)S(1)} %get-tuple-element.44.own_ref, ...), custom_call_target="tpu_custom_call" | custom-call | tf_op jit(solution)/shard_map/pallas_call | solution.py:526
  49.6 1.9 %collective-permute-start.8 = (f32[7,48,128]{2,1,0:T(8,128)S(1)}, f32[7,48,128]{2,1,0:T(8,128)S(1)}, u32[]{:S(2)}, u32[]{:S(2)}) collective-permute-start(f32[7,48,128]{2,1,0:T(8,128)S(1)} %get-tuple-element.64), channel_id=1, source_target_pairs={{0,16},{16,32},{32,48},{48,64},{64,80},{80,96},{96,112},{112,128},... | collective-permute-start | bytes 516104 | tf_op jit(solution)/shard_map/ppermute | solution.py:539
  51.5 3.9 %collective-permute-start.9 = (f32[7,48,128]{2,1,0:T(8,128)S(1)}, f32[7,48,128]{2,1,0:T(8,128)S(1)}, u32[]{:S(2)}, u32[]{:S(2)}) collective-permute-start(f32[7,48,128]{2,1,0:T(8,128)S(1)} %get-tuple-element.65), channel_id=1, source_target_pairs={{16,0},{32,16},{48,32},{64,48},{80,64},{96,80},{112,96},{128,112},... | collective-permute-start | bytes 516104 | tf_op jit(solution)/shard_map/ppermute | solution.py:540
  55.4 0.0 collective-permute-done.5.low3
  55.5 0.0 collective-permute-done.7.high3
  55.5 4.8 %shard_map.72 = (f32[8,48,512]{2,1,0:T(8,128)S(1)}, f32[6,48,512]{2,1,0:T(8,128)S(1)}, f32[6,48,512]{2,1,0:T(8,128)S(1)}, f32[6,48,512]{2,1,0:T(8,128)S(1)}, f32...) custom-call(s32[2]{0:T(128)S(1)} %copy-done, ...), custom_call_target="tpu_custom_call" | custom-call | tf_op jit(solution)/shard_map/pallas_call | solution.py:526
  60.2 0.0 collective-permute-done.8.low_ref
  60.2 1.9 %collective-permute-done.9.high_ref = f32[7,48,128]{2,1,0:T(8,128)S(1)} collective-permute-done((f32[7,48,128]{2,1,0:T(8,128)S(1)}, f32[7,48,128]{2,1,0:T(8,128)S(1)}, u32[]{:S(2)}, u32[]{:S(2)}) %collective-permute-start.9) | collective-permute-done | bytes 172064 | tf_op jit(solution)/shard_map/ppermute | solution.py:540
  62.1 4.2 %shard_map.73 = (f32[4,6,48,384]{3,2,1,0:T(8,128)}, f32[4,48,2,128]{3,2,1,0:T(2,128)}) custom-call(s32[2]{0:T(128)S(1)} %copy-done, f32[8,48,512]{2,1,0:T(8,128)S(1)} %get-tuple-element.55.u_rim, f32[6,48,512]{2,1,0:T(8,128)S(1)} %get-tuple-element.56.v_rim, f32[6,48,512]{2,1,0:T(8,128)S(1)} %get-tuple-element.57.w_rim, ...), custom_call_target="tpu_custom_call" | custom-call | tf_op jit(solution)/shard_map/pallas_call | solution.py:526
  (3 shorter events, 0.0 us)
Async XLA Ops:
  3.5 25.6 %copy-start.1 = (f32[48,48]{1,0:T(8,128)S(1)}, f32[48,48]{1,0:T(8,128)}, u32[]{:S(2)}) copy-start(f32[48,48]{1,0:T(8,128)} %param.8) | copy-start | bytes 27652
  3.6 25.6 %collective-permute-start.2 = (f32[9,48,384]{2,1,0:T(8,128)S(1)}, f32[9,48,384]{2,1,0:T(8,128)S(1)}, u32[]{:S(2)}, u32[]{:S(2)}) collective-permute-start(f32[9,48,384]{2,1,0:T(8,128)S(1)} %get-tuple-element.42), channel_id=1, source_target_pairs={{0,16},{16,32},{32,48},{48,64},{64,80},{80,96},{96,112},{112,128},... | collective-permute-start | bytes 1990664 | tf_op jit(solution)/shard_map/ppermute | solution.py:539
  9.0 21.6 %collective-permute-start.3 = (f32[9,48,384]{2,1,0:T(8,128)S(1)}, f32[9,48,384]{2,1,0:T(8,128)S(1)}, u32[]{:S(2)}, u32[]{:S(2)}) collective-permute-start(f32[9,48,384]{2,1,0:T(8,128)S(1)} %get-tuple-element.43), channel_id=1, source_target_pairs={{16,0},{32,16},{48,32},{64,48},{80,64},{96,80},{112,96},{128,112},... | collective-permute-start | bytes 1990664 | tf_op jit(solution)/shard_map/ppermute | solution.py:540
  10.9 6.9 %collective-permute-start = (f32[48,384]{1,0:T(8,128)S(1)}, f32[48,384]{1,0:T(8,128)S(1)}, u32[]{:S(2)}, u32[]{:S(2)}) collective-permute-start(f32[48,384]{1,0:T(8,128)S(1)} %get-tuple-element.39), channel_id=1, source_target_pairs={{0,1},{1,2},{2,3},{3,4},{4,5},{5,6},{6,7},{7,8},{8,9},{9,10},{10,1... | collective-permute-start | bytes 221192 | tf_op jit(solution)/shard_map/ppermute | solution.py:539
  12.8 6.8 %collective-permute-start.1 = (f32[48,384]{1,0:T(8,128)S(1)}, f32[48,384]{1,0:T(8,128)S(1)}, u32[]{:S(2)}, u32[]{:S(2)}) collective-permute-start(f32[48,384]{1,0:T(8,128)S(1)} %get-tuple-element.40), channel_id=1, source_target_pairs={{1,0},{2,1},{3,2},{4,3},{5,4},{6,5},{7,6},{8,7},{9,8},{10,9},{11,1... | collective-permute-start | bytes 221192 | tf_op jit(solution)/shard_map/ppermute | solution.py:540
  20.0 19.4 %collective-permute-start.4 = (f32[7,48,384]{2,1,0:T(8,128)S(1)}, f32[7,48,384]{2,1,0:T(8,128)S(1)}, u32[]{:S(2)}, u32[]{:S(2)}) collective-permute-start(f32[7,48,384]{2,1,0:T(8,128)S(1)} %get-tuple-element.47), channel_id=1, source_target_pairs={{0,16},{16,32},{32,48},{48,64},{64,80},{80,96},{96,112},{112,128},... | collective-permute-start | bytes 1548296 | tf_op jit(solution)/shard_map/ppermute | solution.py:539
  27.2 19.9 %collective-permute-start.6 = (f32[7,48,384]{2,1,0:T(8,128)S(1)}, f32[7,48,384]{2,1,0:T(8,128)S(1)}, u32[]{:S(2)}, u32[]{:S(2)}) collective-permute-start(f32[7,48,384]{2,1,0:T(8,128)S(1)} %get-tuple-element.49), channel_id=1, source_target_pairs={{16,0},{32,16},{48,32},{64,48},{80,64},{96,80},{112,96},{128,112},... | collective-permute-start | bytes 1548296 | tf_op jit(solution)/shard_map/ppermute | solution.py:540
  30.6 16.6 %copy-start = (s32[2]{0:T(128)S(1)}, s32[2]{0:T(128)}, u32[]{:S(2)}) copy-start(s32[2]{0:T(128)} %off_ref.7) | copy-start | bytes 28
  31.1 24.3 %collective-permute-start.5 = (f32[6,48,384]{2,1,0:T(8,128)S(1)}, f32[6,48,384]{2,1,0:T(8,128)S(1)}, u32[]{:S(2)}, u32[]{:S(2)}) collective-permute-start(f32[6,48,384]{2,1,0:T(8,128)S(1)} %get-tuple-element.48), channel_id=1, source_target_pairs={{0,16},{16,32},{32,48},{48,64},{64,80},{80,96},{96,112},{112,128},... | collective-permute-start | bytes 1327112 | tf_op jit(solution)/shard_map/ppermute | solution.py:539
  37.1 18.4 %collective-permute-start.7 = (f32[6,48,384]{2,1,0:T(8,128)S(1)}, f32[6,48,384]{2,1,0:T(8,128)S(1)}, u32[]{:S(2)}, u32[]{:S(2)}) collective-permute-start(f32[6,48,384]{2,1,0:T(8,128)S(1)} %get-tuple-element.50), channel_id=1, source_target_pairs={{16,0},{32,16},{48,32},{64,48},{80,64},{96,80},{112,96},{128,112},... | collective-permute-start | bytes 1327112 | tf_op jit(solution)/shard_map/ppermute | solution.py:540
  49.6 10.6 %collective-permute-start.8 = (f32[7,48,128]{2,1,0:T(8,128)S(1)}, f32[7,48,128]{2,1,0:T(8,128)S(1)}, u32[]{:S(2)}, u32[]{:S(2)}) collective-permute-start(f32[7,48,128]{2,1,0:T(8,128)S(1)} %get-tuple-element.64), channel_id=1, source_target_pairs={{0,16},{16,32},{32,48},{48,64},{64,80},{80,96},{96,112},{112,128},... | collective-permute-start | bytes 516104 | tf_op jit(solution)/shard_map/ppermute | solution.py:539
  51.5 10.6 %collective-permute-start.9 = (f32[7,48,128]{2,1,0:T(8,128)S(1)}, f32[7,48,128]{2,1,0:T(8,128)S(1)}, u32[]{:S(2)}, u32[]{:S(2)}) collective-permute-start(f32[7,48,128]{2,1,0:T(8,128)S(1)} %get-tuple-element.65), channel_id=1, source_target_pairs={{16,0},{32,16},{48,32},{64,48},{80,64},{96,80},{112,96},{128,112},... | collective-permute-start | bytes 516104 | tf_op jit(solution)/shard_map/ppermute | solution.py:540

commit v4 on v3

--- a/solution.py
+++ b/solution.py
@@ -23,16 +23,15 @@
 SIDE = 8
 SLOTS = LANES // SIDE
 U, V, W, PR = 0, 1, 2, 3
-DEEP = {PR: 5, U: 4, V: 3, W: 3}
-NEAR = {PR: 2, U: 1}
+NEAR = {PR: 2}
 KEEP = 3
 S_GROUP = 4 * ROWS
 EDGE_GROUP = S_GROUP + ROWS
 GROUPS = EDGE_GROUP + 4
 PACK = -(-GROUPS // SLOTS) * LANES
 CHUNK_1 = ((V, 0, 3), (W, 0, 3), ("s", 0, 3))
-CHUNK_2 = ((PR, 0, 2), (U, 0, 1), ("s", 3, 3))
-CHUNK_3 = ((PR, 2, 3), (U, 1, 3))
+CHUNK_2 = ((PR, 0, 2), (U, 0, 1), ("s", 3, 1))
+CHUNK_3 = ((PR, 2, 1), (U, 1, 3), ("s", 4, 2))
 SENT = [(PR, n) for n in range(5)] + [(U, n) for n in range(4)] + [(V, n) for n in range(3)]
 SENT += [(W, n) for n in range(3)] + [("s", n) for n in range(6)]
 
@@ -94,6 +93,28 @@
 
 def own_row(near, side):
     return ROWS - 1 - near if side == 0 else near
+
+
+def is_odd(index):
+    return lax.rem(index, 2) == 1
+
+
+def by_pair(odd, up, down):
+    return jnp.where(odd, up, down), jnp.where(odd, down, up)
+
+
+class Received:
+    def __init__(self, in_first, first, second):
+        self.in_first, self.first, self.second = in_first, first, second
+
+    def __getitem__(self, at):
+        return jnp.where(self.in_first, self.first[at], self.second[at])
+
+
+def low_high(odd, first, second):
+    if first is None:
+        return None, None
+    return Received(jnp.logical_not(odd), first, second), Received(odd, first, second)
 
 
 def prepare_kernel(
@@ -148,15 +169,15 @@
         pack(stiff_ref[row], S_GROUP + row)
     for tile, (left, right) in enumerate(packs):
         at = slice(LANES * tile, LANES * (tile + 1))
-        left_ref[:, at] = left
-        right_ref[:, at] = right
+        left_ref[:, at], right_ref[:, at] = by_pair(is_odd(gy), right, left)
     fill_message(CHUNK_1, cur_ref, stiff_ref, up_ref, down_ref)
 
 
-def fill_message(chunk, cur_ref, stiff_ref, up_ref, down_ref):
-    for side, out in ((0, up_ref), (1, down_ref)):
-        for at, (what, near) in enumerate(rows_of(chunk)):
-            row = own_row(near, side)
+def fill_message(chunk, cur_ref, stiff_ref, first_ref, second_ref):
+    odd = is_odd(lax.axis_index("gx"))
+    for at, (what, near) in enumerate(rows_of(chunk)):
+        rows = by_pair(odd, own_row(near, 0), own_row(near, 1))
+        for row, out in zip(rows, (first_ref, second_ref)):
             out[at] = stiff_ref[row] if what == "s" else cur_ref[what, row]
 
 
@@ -169,8 +190,9 @@
     levels = left_ref.shape[0]
     lane = lanes_of((levels, LANES))
     place = lane // SIDE
-    mine_ref[0] = left_ref[...]
-    mine_ref[1] = right_ref[...]
+    from_left, from_right = low_high(is_odd(gy), left_ref, right_ref)
+    mine_ref[0] = from_left[...]
+    mine_ref[1] = from_right[...]
 
     def fill(side, cell):
         for tile in range(PACK // LANES):
@@ -202,7 +224,8 @@
 
     rows = rows_of(CHUNK_2)
     fill_message(CHUNK_2, cur_ref, stiff_ref, up_ref, down_ref)
-    for side, out in ((0, up_ref), (1, down_ref)):
+    tight = []
+    for side in range(2):
         tiles = [None] * (COLS // LANES)
         for hand in range(2):
             for at, (what, near) in enumerate(SENT):
@@ -213,8 +236,8 @@
                 value = turn(mine_ref[hand, :, LANES * tile : LANES * (tile + 1)], SIDE * (to_slot - slot))
                 held = tiles[to_tile]
                 tiles[to_tile] = value if held is None else jnp.where(place == to_slot, value, held)
-        for tile, value in enumerate(tiles):
-            out[len(rows), :, LANES * tile : LANES * (tile + 1)] = value
+        tight.append(jnp.concatenate(tiles, axis=1))
+    up_ref[len(rows)], down_ref[len(rows)] = by_pair(is_odd(gx), *tight)
 
 
 def beside(left, left_slot, right, right_slot):
@@ -241,10 +264,17 @@
 
 
 def far_kernel(
-    cur_ref, stiff_ref, edge_ref, mine_ref, low1, high1, up_ref, down_ref, own_ref, own_s_ref, rim_ref
+    counts, off_ref, cur_ref, stiff_ref, edge_ref, mine_ref, low1, high1, up_ref, down_ref, own_ref, own_s_ref, rim_ref
 ):
     del low1, high1
+    at = Place(counts, off_ref, stiff_ref.shape[1])
     fill_message(CHUNK_3, cur_ref, stiff_ref, up_ref, down_ref)
+    for n, (what, near) in enumerate(rows_of(CHUNK_3)):
+        if what == U:
+            rows = by_pair(is_odd(at.gx), own_row(near, 0), own_row(near, 1))
+            for row, out in zip(rows, (up_ref, down_ref)):
+                keep = at.keep(row)[:, :COLS]
+                out[n] = wind_x(keep, cur_ref[U, row], cur_ref[PR, row - 1], cur_ref[PR, row + 1])
     for field in range(4):
         for row in range(ROWS):
             own_ref[field, row, :, :COLS] = cur_ref[field, row]
@@ -268,9 +298,13 @@
     def __init__(self, counts, off_ref, levels):
         self.nx, self.ny = counts
         self.gx, self.gy = lax.axis_index("gx"), lax.axis_index("gy")
+        self.last_x = self.nx // ROWS - 1
         self.off_x, self.off_y = off_ref[0], off_ref[1]
         j = column_of_lane(lanes_of((levels, WIDE))) + (self.gy * COLS - RATIO * self.off_y)
         self.held = is_edge(j, self.ny).astype(jnp.int32)
+
+    def neighbours(self, *swaps):
+        return zip(*[low_high(is_odd(self.gx), first, second) for first, second in swaps])
 
     def keep(self, row):
         i = self.gx * ROWS + row - RATIO * self.off_x
@@ -284,7 +318,7 @@
             outer = self.gx == 0
         else:
             value = received(high, high[1], field, row - ROWS)
-            outer = self.gx == self.nx // ROWS - 1
+            outer = self.gx == self.last_x
         return jnp.where(outer, rim_ref[field], value)
 
 
@@ -313,13 +347,13 @@
 ):
     levels = own_ref.shape[2]
     at = Place(counts, off_ref, levels)
-    low, high = (low1, low2, None), (high1, high2, None)
+    low, high = at.neighbours((low1, high1), (low2, high2), (None, None))
     deep = NEAR[PR]
     for row in range(-deep, ROWS + deep):
         p_win[row + deep] = at.field_row(own_ref, low, high, rim_ref, PR, row)
     for near in range(KEEP):
-        s_win[KEEP - 1 - near] = received(low, low2, "s", near)
-        s_win[KEEP + ROWS + near] = received(high, high2, "s", near)
+        s_win[KEEP - 1 - near] = received(low, low[1], "s", near)
+        s_win[KEEP + ROWS + near] = received(high, high[1], "s", near)
     for row in range(ROWS):
         s_win[KEEP + row] = own_s_ref[row]
     for row in range(-1, ROWS + 1):
@@ -337,7 +371,8 @@
         return carry
 
     lax.fori_loop(0, ROWS, body, 0, unroll=ROWS)
-    for out, first in ((up_ref, 1), (down_ref, 3)):
+    starts = by_pair(is_odd(at.gx), 1, 3)
+    for out, first in zip((up_ref, down_ref), starts):
         beyond = None
         for n in range(2):
             value = p_out[first + n]
@@ -369,15 +404,15 @@
 ):
     levels = own_ref.shape[2]
     at = Place(counts, off_ref, levels)
-    low, high = (low1, low2, low3), (high1, high2, high3)
+    low, high = at.neighbours((low1, high1), (low2, high2), (low3, high3))
     table = table_ref[...]
-    deep = DEEP[PR]
+    deep = KEEP
     for n in range(deep + 1):
         p_win[n] = at.field_row(own_ref, low, high, rim_ref, PR, n - deep)
         p_win[deep + 1 + n] = at.field_row(own_ref, low, high, rim_ref, PR, ROWS - 1 + n)
     for near in range(ROWS):
-        s_win[ROWS - 1 - near] = received(low, low2, "s", near)
-        s_win[2 * ROWS + near] = received(high, high2, "s", near)
+        s_win[ROWS - 1 - near] = received(low, low[1], "s", near)
+        s_win[2 * ROWS + near] = received(high, high[1], "s", near)
         s_win[ROWS + near] = own_s_ref[near]
     move_y = lax.rem(RATIO * at.off_y + WIDE, WIDE)
 
@@ -391,8 +426,14 @@
         return row + depth if row < 0 else row - ROWS + depth
 
     for row in (-4, -3, -2, 7, 8, 9):
-        wind = at.field_row(own_ref, low, high, rim_ref, U, row)
-        u_rim[rim_of(4, row)] = wind_x(at.keep(row), wind, p_before(row - 1), p_before(row + 1))
+        near = -1 - row if row < 0 else row - ROWS
+        near_ref, outer = (low[1], at.gx == 0) if row < 0 else (high[1], at.gx == at.last_x)
+        outward, inward = (sent_beside(near_ref, PR, near + by) for by in (1, -1))
+        p_low, p_high = (outward, inward) if row < 0 else (inward, outward)
+        main = received(low if row < 0 else high, near_ref, U, near)
+        ext = wind_x(at.keep(row)[:, COLS:], main[:, COLS:], p_low, p_high)
+        value = jnp.concatenate([main[:, :COLS], ext], axis=1)
+        u_rim[rim_of(4, row)] = jnp.where(outer, rim_ref[U], value)
 
     def u_after(row):
         return u_own[row + 1] if -1 <= row <= ROWS else u_rim[rim_of(4, row)]
@@ -443,6 +484,7 @@
         parts = [ref[n * tiles + tile] for tile in range(tiles)] + [split_ext(ref[2 * tiles], n)]
         return jnp.concatenate(parts, axis=1)
 
+    low_ref, high_ref = low_high(is_odd(at.gx), low_ref, high_ref)
     for row in range(ROWS + 4):
         u_win[row + 2] = u_mid[row]
     for row in range(ROWS + 2):
@@ -533,12 +575,12 @@
     )(*ins)
 
 
-def exchange(up, down, axis):
-    count = lax.axis_size(axis)
-    forward = [(i, i + 1) for i in range(count - 1)]
-    low = lax.ppermute(up, axis, forward)
-    high = lax.ppermute(down, axis, [(target, source) for source, target in forward])
-    return low, high
+def exchange(first, second, axis):
+    def swap(x, start):
+        pairs = [(i, i + 1) for i in range(start, lax.axis_size(axis) - 1, 2)]
+        return lax.ppermute(x, axis, pairs + [(high, low) for low, high in pairs])
+
+    return swap(first, 1), swap(second, 0)
 
 
 def per_device(nest_state, stiffness, parent, inverse_table, offsets):
@@ -569,7 +611,7 @@
         [pltpu.SMEM, pltpu.HBM, pltpu.HBM, pltpu.HBM],
     )
     low1, high1 = exchange(up, down, "gx")
-    from_left, from_right = exchange(to_right, to_left, "gy")
+    from_left, from_right = exchange(to_left, to_right, "gy")
     mine, up, down = call(
         functools.partial(near_kernel, lax.axis_size("gy") - 1),
         (cur, stiff, coarse, from_left, from_right),
@@ -577,8 +619,8 @@
     )
     low2, high2 = exchange(up, down, "gx")
     up, down, own, own_s, rim = call(
-        far_kernel,
-        (cur, stiff, edge, mine, low1, high1),
+        functools.partial(far_kernel, counts),
+        (offsets, cur, stiff, edge, mine, low1, high1),
         [rows(far, COLS), rows(far, COLS), (4, ROWS, levels, WIDE), rows(ROWS), rows(4)],
     )
     low3, high3 = exchange(up, down, "gx")
@@ -594,7 +636,7 @@
         functools.partial(halo_kernel, counts),
         (offsets, own, own_s, rim, low1, low2, low3, high1, high2, high3, table, u1, v1, w1, p1),
         [rows(8), rows(6), rows(6), rows(6), rows(4), rows(ROWS + 4), rows(ROWS + 2), rows(ROWS + 2), rows(ROWS + 2)],
-        [rows(12), rows(3 * ROWS), rows(ROWS + 2)],
+        [rows(8), rows(3 * ROWS), rows(ROWS + 2)],
     )
     new, back = call(
         functools.partial(last_kernel, counts),

time: 66.8 us -> 56.2 us (0.84)
  the two profiles are of different devices: /device:TPU:230 before, /device:TPU:252 now
where the time goes in v4:
time: 56.2 us; the launch traced here: 55.8 us
  starting transfers between devices  34.2 us (61%)
  Pallas kernels  16.1 us (29%)
  waiting for transfers between devices  4.49 us (8%)
  between operations  0.86 us (2%)
    ppermute x10, starting transfers between devices, swap(): return lax.ppermute(x, axis, pairs + [(high, low) for low, high in pairs])  34.2 us
    pallas_call x6, Pallas kernels, call(): pl.pallas_call(body, out_shape=[jax.ShapeDtypeStruct(shape, F32) for shap...  16.1 us
    ppermute x10, waiting for transfers between devices, swap(): return lax.ppermute(x, axis, pairs + [(high, low) for low, high in pairs])  4.49 us
  transfers between devices with their start and end apart: 10, of which 2 were waited for; matrix products, arithmetic and copies ran while one was open for 0% of the time, Pallas kernels for 16%

profile of v4, /device:TPU:252, one launch (start us, length us, event | category | flops | bytes accessed | tf_op | source)
XLA Modules:
  0.0 55.8 jit_solution(3126468682517504962)
XLA Ops:
  0.6 2.9 %shard_map.68 = (f32[4,6,48,384]{3,2,1,0:T(8,128)S(1)}, f32[6,48,384]{2,1,0:T(8,128)S(1)}, f32[4,2,48,128]{3,2,1,0:T(8,128)S(1)}, f32[48,384]{1,0:T(8,128)S(1)},...) custom-call(s32[2]{0:T(128)} %off_ref.9, ...), custom_call_target="tpu_custom_call" | custom-call | tf_op jit(solution)/shard_map/pallas_call | solution.py:568
  3.5 0.0 copy-start.1
  3.6 0.0 copy-start
  3.6 2.4 %collective-permute-start.2 = (f32[9,48,384]{2,1,0:T(8,128)S(1)}, f32[9,48,384]{2,1,0:T(8,128)S(1)}, u32[]{:S(2)}, u32[]{:S(2)}) collective-permute-start(f32[9,48,384]{2,1,0:T(8,128)S(1)} %get-tuple-element.42), channel_id=1, source_target_pairs={{16,32},{48,64},{80,96},{112,128},{144,160},{176,192},{208,224},{2... | collective-permute-start | bytes 1990664 | tf_op jit(solution)/shard_map/ppermute | solution.py:581
  6.0 6.1 %collective-permute-start.3 = (f32[9,48,384]{2,1,0:T(8,128)S(1)}, f32[9,48,384]{2,1,0:T(8,128)S(1)}, u32[]{:S(2)}, u32[]{:S(2)}) collective-permute-start(f32[9,48,384]{2,1,0:T(8,128)S(1)} %get-tuple-element.43), channel_id=1, source_target_pairs={{0,16},{32,48},{64,80},{96,112},{128,144},{160,176},{192,208},{224... | collective-permute-start | bytes 1990664 | tf_op jit(solution)/shard_map/ppermute | solution.py:581
  12.1 2.1 %collective-permute-start = (f32[48,384]{1,0:T(8,128)S(1)}, f32[48,384]{1,0:T(8,128)S(1)}, u32[]{:S(2)}, u32[]{:S(2)}) collective-permute-start(f32[48,384]{1,0:T(8,128)S(1)} %get-tuple-element.39), channel_id=1, source_target_pairs={{1,2},{3,4},{5,6},{7,8},{9,10},{11,12},{13,14},{2,1},{4,3},{6,5},{... | collective-permute-start | bytes 221192 | tf_op jit(solution)/shard_map/ppermute | solution.py:581
  14.2 1.9 %collective-permute-start.1 = (f32[48,384]{1,0:T(8,128)S(1)}, f32[48,384]{1,0:T(8,128)S(1)}, u32[]{:S(2)}, u32[]{:S(2)}) collective-permute-start(f32[48,384]{1,0:T(8,128)S(1)} %get-tuple-element.40), channel_id=1, source_target_pairs={{0,1},{2,3},{4,5},{6,7},{8,9},{10,11},{12,13},{14,15},{1,0},{3,2},... | collective-permute-start | bytes 221192 | tf_op jit(solution)/shard_map/ppermute | solution.py:581
  16.2 1.6 %collective-permute-done.left_ref = f32[48,384]{1,0:T(8,128)S(1)} collective-permute-done((f32[48,384]{1,0:T(8,128)S(1)}, f32[48,384]{1,0:T(8,128)S(1)}, u32[]{:S(2)}, u32[]{:S(2)}) %collective-permute-start) | collective-permute-done | bytes 73760 | tf_op jit(solution)/shard_map/ppermute | solution.py:581
  17.8 0.0 collective-permute-done.1.right_ref
  17.8 0.4 shard_map.69
  18.1 1.9 %collective-permute-start.4 = (f32[5,48,384]{2,1,0:T(8,128)S(1)}, f32[5,48,384]{2,1,0:T(8,128)S(1)}, u32[]{:S(2)}, u32[]{:S(2)}) collective-permute-start(f32[5,48,384]{2,1,0:T(8,128)S(1)} %get-tuple-element.47), channel_id=1, source_target_pairs={{16,32},{48,64},{80,96},{112,128},{144,160},{176,192},{208,224},{2... | collective-permute-start | bytes 1105928 | tf_op jit(solution)/shard_map/ppermute | solution.py:581
  20.1 4.9 %collective-permute-start.6 = (f32[5,48,384]{2,1,0:T(8,128)S(1)}, f32[5,48,384]{2,1,0:T(8,128)S(1)}, u32[]{:S(2)}, u32[]{:S(2)}) collective-permute-start(f32[5,48,384]{2,1,0:T(8,128)S(1)} %get-tuple-element.49), channel_id=1, source_target_pairs={{0,16},{32,48},{64,80},{96,112},{128,144},{160,176},{192,208},{224... | collective-permute-start | bytes 1105928 | tf_op jit(solution)/shard_map/ppermute | solution.py:581
  24.9 0.0 copy-done.1
  25.0 0.0 collective-permute-done.2.low1
  25.0 2.9 %collective-permute-done.3.high1 = f32[9,48,384]{2,1,0:T(8,128)S(1)} collective-permute-done((f32[9,48,384]{2,1,0:T(8,128)S(1)}, f32[9,48,384]{2,1,0:T(8,128)S(1)}, u32[]{:S(2)}, u32[]{:S(2)}) %collective-permute-start.3) | collective-permute-done | bytes 663584 | tf_op jit(solution)/shard_map/ppermute | solution.py:581
  27.8 0.0 copy-done
  27.9 1.2 %shard_map.70 = (f32[6,48,384]{2,1,0:T(8,128)S(1)}, f32[6,48,384]{2,1,0:T(8,128)S(1)}, f32[4,6,48,512]{3,2,1,0:T(8,128)S(1)}, f32[6,48,512]{2,1,0:T(8,128)S(1)}, f32[4,48,512]{2,1,0:T(8,128)S(1)}) custom-call(s32[2]{0:T(128)S(1)} %copy-done, f32[4,6,48,384]{3,2,1,0:T(8,128)S(1)} %get-tuple-element.35.cur_ref, f32[6,48,384]{2,1,0:T(8,128)S(1)} %get-tuple-element.36.stiff_ref, ...), custom_call_target="tpu_custom_call" | custom-call | tf_op jit(solution)/shard_map/pallas_call | solution.py:568
  29.0 1.9 %collective-permute-start.5 = (f32[6,48,384]{2,1,0:T(8,128)S(1)}, f32[6,48,384]{2,1,0:T(8,128)S(1)}, u32[]{:S(2)}, u32[]{:S(2)}) collective-permute-start(f32[6,48,384]{2,1,0:T(8,128)S(1)} %get-tuple-element.48), channel_id=1, source_target_pairs={{16,32},{48,64},{80,96},{112,128},{144,160},{176,192},{208,224},{2... | collective-permute-start | bytes 1327112 | tf_op jit(solution)/shard_map/ppermute | solution.py:581
  30.9 5.3 %collective-permute-start.7 = (f32[6,48,384]{2,1,0:T(8,128)S(1)}, f32[6,48,384]{2,1,0:T(8,128)S(1)}, u32[]{:S(2)}, u32[]{:S(2)}) collective-permute-start(f32[6,48,384]{2,1,0:T(8,128)S(1)} %get-tuple-element.50), channel_id=1, source_target_pairs={{0,16},{32,48},{64,80},{96,112},{128,144},{160,176},{192,208},{224... | collective-permute-start | bytes 1327112 | tf_op jit(solution)/shard_map/ppermute | solution.py:581
  36.3 0.1 pad_maximum_fusion.1.table_ref
  36.4 0.0 collective-permute-done.4.low2
  36.4 0.0 collective-permute-done.6.high2
  36.4 2.5 %shard_map.71 = (f32[8,48,512]{2,1,0:T(8,128)S(1)}, f32[6,48,512]{2,1,0:T(8,128)S(1)}, f32[6,48,512]{2,1,0:T(8,128)S(1)}, f32[6,48,512]{2,1,0:T(8,128)S(1)}, f32...) custom-call(s32[2]{0:T(128)S(1)} %copy-done, f32[4,6,48,512]{3,2,1,0:T(8,128)S(1)} %get-tuple-element.44.own_ref, ...), custom_call_target="tpu_custom_call" | custom-call | tf_op jit(solution)/shard_map/pallas_call | solution.py:568
  39.0 1.9 %collective-permute-start.8 = (f32[7,48,128]{2,1,0:T(8,128)S(1)}, f32[7,48,128]{2,1,0:T(8,128)S(1)}, u32[]{:S(2)}, u32[]{:S(2)}) collective-permute-start(f32[7,48,128]{2,1,0:T(8,128)S(1)} %get-tuple-element.64), channel_id=1, source_target_pairs={{16,32},{48,64},{80,96},{112,128},{144,160},{176,192},{208,224},{2... | collective-permute-start | bytes 516104 | tf_op jit(solution)/shard_map/ppermute | solution.py:581
  40.9 5.6 %collective-permute-start.9 = (f32[7,48,128]{2,1,0:T(8,128)S(1)}, f32[7,48,128]{2,1,0:T(8,128)S(1)}, u32[]{:S(2)}, u32[]{:S(2)}) collective-permute-start(f32[7,48,128]{2,1,0:T(8,128)S(1)} %get-tuple-element.65), channel_id=1, source_target_pairs={{0,16},{32,48},{64,80},{96,112},{128,144},{160,176},{192,208},{224... | collective-permute-start | bytes 516104 | tf_op jit(solution)/shard_map/ppermute | solution.py:581
  46.5 0.0 collective-permute-done.5.low3
  46.5 0.0 collective-permute-done.7.high3
  46.5 4.9 %shard_map.72 = (f32[8,48,512]{2,1,0:T(8,128)S(1)}, f32[6,48,512]{2,1,0:T(8,128)S(1)}, f32[6,48,512]{2,1,0:T(8,128)S(1)}, f32[6,48,512]{2,1,0:T(8,128)S(1)}, f32...) custom-call(s32[2]{0:T(128)S(1)} %copy-done, ...), custom_call_target="tpu_custom_call" | custom-call | tf_op jit(solution)/shard_map/pallas_call | solution.py:568
  51.5 0.0 collective-permute-done.8.low_ref
  51.5 0.0 collective-permute-done.9.high_ref
  51.5 4.3 %shard_map.73 = (f32[4,6,48,384]{3,2,1,0:T(8,128)}, f32[4,48,2,128]{3,2,1,0:T(2,128)}) custom-call(s32[2]{0:T(128)S(1)} %copy-done, f32[8,48,512]{2,1,0:T(8,128)S(1)} %get-tuple-element.55.u_rim, f32[6,48,512]{2,1,0:T(8,128)S(1)} %get-tuple-element.56.v_rim, f32[6,48,512]{2,1,0:T(8,128)S(1)} %get-tuple-element.57.w_rim, ...), custom_call_target="tpu_custom_call" | custom-call | tf_op jit(solution)/shard_map/pallas_call | solution.py:568
  (3 shorter events, 0.0 us)
Async XLA Ops:
  3.5 21.4 %copy-start.1 = (f32[48,48]{1,0:T(8,128)S(1)}, f32[48,48]{1,0:T(8,128)}, u32[]{:S(2)}) copy-start(f32[48,48]{1,0:T(8,128)} %param.8) | copy-start | bytes 27652
  3.6 24.3 %copy-start = (s32[2]{0:T(128)S(1)}, s32[2]{0:T(128)}, u32[]{:S(2)}) copy-start(s32[2]{0:T(128)} %off_ref.9) | copy-start | bytes 28
  3.6 21.4 %collective-permute-start.2 = (f32[9,48,384]{2,1,0:T(8,128)S(1)}, f32[9,48,384]{2,1,0:T(8,128)S(1)}, u32[]{:S(2)}, u32[]{:S(2)}) collective-permute-start(f32[9,48,384]{2,1,0:T(8,128)S(1)} %get-tuple-element.42), channel_id=1, source_target_pairs={{16,32},{48,64},{80,96},{112,128},{144,160},{176,192},{208,224},{2... | collective-permute-start | bytes 1990664 | tf_op jit(solution)/shard_map/ppermute | solution.py:581
  6.0 21.8 %collective-permute-start.3 = (f32[9,48,384]{2,1,0:T(8,128)S(1)}, f32[9,48,384]{2,1,0:T(8,128)S(1)}, u32[]{:S(2)}, u32[]{:S(2)}) collective-permute-start(f32[9,48,384]{2,1,0:T(8,128)S(1)} %get-tuple-element.43), channel_id=1, source_target_pairs={{0,16},{32,48},{64,80},{96,112},{128,144},{160,176},{192,208},{224... | collective-permute-start | bytes 1990664 | tf_op jit(solution)/shard_map/ppermute | solution.py:581
  12.1 5.7 %collective-permute-start = (f32[48,384]{1,0:T(8,128)S(1)}, f32[48,384]{1,0:T(8,128)S(1)}, u32[]{:S(2)}, u32[]{:S(2)}) collective-permute-start(f32[48,384]{1,0:T(8,128)S(1)} %get-tuple-element.39), channel_id=1, source_target_pairs={{1,2},{3,4},{5,6},{7,8},{9,10},{11,12},{13,14},{2,1},{4,3},{6,5},{... | collective-permute-start | bytes 221192 | tf_op jit(solution)/shard_map/ppermute | solution.py:581
  14.2 3.5 %collective-permute-start.1 = (f32[48,384]{1,0:T(8,128)S(1)}, f32[48,384]{1,0:T(8,128)S(1)}, u32[]{:S(2)}, u32[]{:S(2)}) collective-permute-start(f32[48,384]{1,0:T(8,128)S(1)} %get-tuple-element.40), channel_id=1, source_target_pairs={{0,1},{2,3},{4,5},{6,7},{8,9},{10,11},{12,13},{14,15},{1,0},{3,2},... | collective-permute-start | bytes 221192 | tf_op jit(solution)/shard_map/ppermute | solution.py:581
  18.1 18.3 %collective-permute-start.4 = (f32[5,48,384]{2,1,0:T(8,128)S(1)}, f32[5,48,384]{2,1,0:T(8,128)S(1)}, u32[]{:S(2)}, u32[]{:S(2)}) collective-permute-start(f32[5,48,384]{2,1,0:T(8,128)S(1)} %get-tuple-element.47), channel_id=1, source_target_pairs={{16,32},{48,64},{80,96},{112,128},{144,160},{176,192},{208,224},{2... | collective-permute-start | bytes 1105928 | tf_op jit(solution)/shard_map/ppermute | solution.py:581
  20.1 16.4 %collective-permute-start.6 = (f32[5,48,384]{2,1,0:T(8,128)S(1)}, f32[5,48,384]{2,1,0:T(8,128)S(1)}, u32[]{:S(2)}, u32[]{:S(2)}) collective-permute-start(f32[5,48,384]{2,1,0:T(8,128)S(1)} %get-tuple-element.49), channel_id=1, source_target_pairs={{0,16},{32,48},{64,80},{96,112},{128,144},{160,176},{192,208},{224... | collective-permute-start | bytes 1105928 | tf_op jit(solution)/shard_map/ppermute | solution.py:581
  29.0 17.5 %collective-permute-start.5 = (f32[6,48,384]{2,1,0:T(8,128)S(1)}, f32[6,48,384]{2,1,0:T(8,128)S(1)}, u32[]{:S(2)}, u32[]{:S(2)}) collective-permute-start(f32[6,48,384]{2,1,0:T(8,128)S(1)} %get-tuple-element.48), channel_id=1, source_target_pairs={{16,32},{48,64},{80,96},{112,128},{144,160},{176,192},{208,224},{2... | collective-permute-start | bytes 1327112 | tf_op jit(solution)/shard_map/ppermute | solution.py:581
  30.9 15.6 %collective-permute-start.7 = (f32[6,48,384]{2,1,0:T(8,128)S(1)}, f32[6,48,384]{2,1,0:T(8,128)S(1)}, u32[]{:S(2)}, u32[]{:S(2)}) collective-permute-start(f32[6,48,384]{2,1,0:T(8,128)S(1)} %get-tuple-element.50), channel_id=1, source_target_pairs={{0,16},{32,48},{64,80},{96,112},{128,144},{160,176},{192,208},{224... | collective-permute-start | bytes 1327112 | tf_op jit(solution)/shard_map/ppermute | solution.py:581
  39.0 12.5 %collective-permute-start.8 = (f32[7,48,128]{2,1,0:T(8,128)S(1)}, f32[7,48,128]{2,1,0:T(8,128)S(1)}, u32[]{:S(2)}, u32[]{:S(2)}) collective-permute-start(f32[7,48,128]{2,1,0:T(8,128)S(1)} %get-tuple-element.64), channel_id=1, source_target_pairs={{16,32},{48,64},{80,96},{112,128},{144,160},{176,192},{208,224},{2... | collective-permute-start | bytes 516104 | tf_op jit(solution)/shard_map/ppermute | solution.py:581
  40.9 10.6 %collective-permute-start.9 = (f32[7,48,128]{2,1,0:T(8,128)S(1)}, f32[7,48,128]{2,1,0:T(8,128)S(1)}, u32[]{:S(2)}, u32[]{:S(2)}) collective-permute-start(f32[7,48,128]{2,1,0:T(8,128)S(1)} %get-tuple-element.65), channel_id=1, source_target_pairs={{0,16},{32,48},{64,80},{96,112},{128,144},{160,176},{192,208},{224... | collective-permute-start | bytes 516104 | tf_op jit(solution)/shard_map/ppermute | solution.py:581

commit v5 on v4

--- a/solution.py
+++ b/solution.py
@@ -10,7 +10,6 @@
 RATIO = 3
 GRAD = 0.25
 DIV = 0.25
-COUPLE = 0.25
 LIFT = 0.5
 F32 = jnp.float32
 BF16 = jnp.bfloat16
@@ -23,6 +22,7 @@
 SIDE = 8
 SLOTS = LANES // SIDE
 U, V, W, PR = 0, 1, 2, 3
+GROUP = 2
 NEAR = {PR: 2}
 KEEP = 3
 S_GROUP = 4 * ROWS
@@ -73,15 +73,22 @@
     return pltpu.roll(x, 1, 1)
 
 
+SUB = 8
+
+
 def level_up(x):
     levels = x.shape[0]
-    level = lax.broadcasted_iota(jnp.int32, x.shape, 0)
-    return jnp.where(level < levels - 1, pltpu.roll(x, levels - 1, 0), 0.0)
+    turned = pltpu.roll(x, levels - 1, 0)
+    last = turned[levels - SUB :]
+    level = lax.broadcasted_iota(jnp.int32, last.shape, 0)
+    return jnp.concatenate([turned[: levels - SUB], jnp.where(level < SUB - 1, last, 0.0)], axis=0)
 
 
 def level_down(x):
-    level = lax.broadcasted_iota(jnp.int32, x.shape, 0)
-    return jnp.where(level > 0, pltpu.roll(x, 1, 0), 0.0)
+    turned = pltpu.roll(x, 1, 0)
+    first = turned[:SUB]
+    level = lax.broadcasted_iota(jnp.int32, first.shape, 0)
+    return jnp.concatenate([jnp.where(level > 0, first, 0.0), turned[SUB:]], axis=0)
 
 
 def split_dot(table, x):
@@ -300,15 +307,20 @@
         self.gx, self.gy = lax.axis_index("gx"), lax.axis_index("gy")
         self.last_x = self.nx // ROWS - 1
         self.off_x, self.off_y = off_ref[0], off_ref[1]
-        j = column_of_lane(lanes_of((levels, WIDE))) + (self.gy * COLS - RATIO * self.off_y)
-        self.held = is_edge(j, self.ny).astype(jnp.int32)
+        j = column_of_lane(lanes_of((SUB, WIDE))) + (self.gy * COLS - RATIO * self.off_y)
+        self.copies = levels // SUB
+        self.held_once = is_edge(j, self.ny).astype(jnp.int32)
+        self.held = self.over_levels(self.held_once)
 
     def neighbours(self, *swaps):
         return zip(*[low_high(is_odd(self.gx), first, second) for first, second in swaps])
 
     def keep(self, row):
         i = self.gx * ROWS + row - RATIO * self.off_x
-        return (self.held + is_edge(i, self.nx).astype(jnp.int32)) > 0
+        return self.over_levels(self.held_once + is_edge(i, self.nx).astype(jnp.int32)) > 0
+
+    def over_levels(self, tile):
+        return jnp.concatenate([tile] * self.copies, axis=0)
 
     def field_row(self, own, low, high, rim_ref, field, row):
         if 0 <= row < ROWS:
@@ -326,18 +338,40 @@
     return jnp.where(keep, wind, wind - GRAD * (p_high - p_low))
 
 
-def column_step(keep, table, pressure, u_low, u_high, wind, lift, stiffness):
-    levels = pressure.shape[0]
-    wind = jnp.where(keep, wind, wind - GRAD * (next_col(pressure) - prev_col(pressure)))
-    divergence = (u_high - u_low) + (next_col(wind) - prev_col(wind))
-    right_side = pressure - DIV * divergence - COUPLE * (level_up(lift) - level_down(lift))
-    both = split_dot(table, right_side)
-    first, around = both[:levels], both[levels:]
-    leftover = right_side - ((1.0 + stiffness) * first - 0.25 * around)
-    solved = first + split_dot(table[:levels], leftover)
-    p_next = jnp.where(keep, pressure, solved)
-    w_next = jnp.where(keep, lift, lift - LIFT * (level_up(p_next) - p_next))
-    return wind, w_next, p_next
+def in_groups(rows):
+    rows = list(rows)
+    return [rows[first : first + GROUP] for first in range(0, len(rows), GROUP)]
+
+
+def side_by_side(rows):
+    return rows[0] if len(rows) == 1 else jnp.concatenate(rows, axis=1)
+
+
+def apart(x, count):
+    return [x[:, WIDE * n : WIDE * (n + 1)] for n in range(count)]
+
+
+def column_steps(table, rows):
+    levels = table.shape[0] // 2
+    winds, right_sides = [], []
+    for keep, pressure, u_low, u_high, wind, lift, stiffness in rows:
+        wind = jnp.where(keep, wind, wind - GRAD * (next_col(pressure) - prev_col(pressure)))
+        change = (u_high - u_low) + (next_col(wind) - prev_col(wind)) + (level_up(lift) - level_down(lift))
+        winds.append(wind)
+        right_sides.append(pressure - DIV * change)
+    both = split_dot(table, side_by_side(right_sides))
+    firsts, arounds = apart(both[:levels], len(rows)), apart(both[levels:], len(rows))
+    leftovers = [
+        (right_side - first) - row[6] * first + around
+        for row, right_side, first, around in zip(rows, right_sides, firsts, arounds)
+    ]
+    seconds = apart(split_dot(table[:levels], side_by_side(leftovers)), len(rows))
+    results = []
+    for (keep, pressure, _, _, _, lift, _), wind, first, second in zip(rows, winds, firsts, seconds):
+        p_next = jnp.where(keep, pressure, first + second)
+        w_next = jnp.where(keep, lift, lift - LIFT * (level_up(p_next) - p_next))
+        results.append((wind, w_next, p_next))
+    return results
 
 
 def own_kernel(
@@ -362,15 +396,20 @@
     move_y = lax.rem(RATIO * at.off_y + WIDE, WIDE)
     table = table_ref[...]
 
-    def body(row, carry):
-        stiffness = pltpu.roll(s_win[row + KEEP - RATIO * at.off_x], move_y, 1)
-        v_out[row], w_out[row], p_out[row] = column_step(
-            at.keep(row), table, p_win[row + deep], u_out[row], u_out[row + 2],
-            own_ref[V, row], own_ref[W, row], stiffness,
+    for rows in in_groups(range(ROWS)):
+        results = column_steps(
+            table,
+            [
+                (
+                    at.keep(row), p_win[row + deep], u_out[row], u_out[row + 2],
+                    own_ref[V, row], own_ref[W, row],
+                    pltpu.roll(s_win[row + KEEP - RATIO * at.off_x], move_y, 1),
+                )
+                for row in rows
+            ],
         )
-        return carry
-
-    lax.fori_loop(0, ROWS, body, 0, unroll=ROWS)
+        for row, result in zip(rows, results):
+            v_out[row], w_out[row], p_out[row] = result
     starts = by_pair(is_odd(at.gx), 1, 3)
     for out, first in zip((up_ref, down_ref), starts):
         beyond = None
@@ -438,22 +477,26 @@
     def u_after(row):
         return u_own[row + 1] if -1 <= row <= ROWS else u_rim[rim_of(4, row)]
 
-    outer = (-3, -2, -1, 6, 7, 8)
-    for row in outer:
-        n = rim_of(KEEP, row)
-        stiff = stiffness(row)
-        if row in (-3, -2, 7, 8):
-            s_rim[(-3, -2, 7, 8).index(row)] = stiff
-        else:
-            s_mid[0 if row < 0 else ROWS + 1] = stiff
-        v_rim[n], w_rim[n], p_rim[n] = column_step(
-            at.keep(row), table, p_before(row), u_after(row - 1), u_after(row + 1),
-            at.field_row(own_ref, low, high, rim_ref, V, row),
-            at.field_row(own_ref, low, high, rim_ref, W, row),
-            stiff,
+    for n, row in enumerate((-3, -2, 7, 8)):
+        s_rim[n] = stiffness(row)
+    for row in range(-1, ROWS + 1):
+        s_mid[row + 1] = stiffness(row)
+    for rows in in_groups((-3, -2, -1, 6, 7, 8)):
+        results = column_steps(
+            table,
+            [
+                (
+                    at.keep(row), p_before(row), u_after(row - 1), u_after(row + 1),
+                    at.field_row(own_ref, low, high, rim_ref, V, row),
+                    at.field_row(own_ref, low, high, rim_ref, W, row),
+                    s_rim[(-3, -2, 7, 8).index(row)] if row in (-3, -2, 7, 8) else s_mid[row + 1],
+                )
+                for row in rows
+            ],
         )
-    for row in range(ROWS):
-        s_mid[row + 1] = stiffness(row)
+        for row, result in zip(rows, results):
+            n = rim_of(KEEP, row)
+            v_rim[n], w_rim[n], p_rim[n] = result
 
     def pick(own, rim, row):
         return own[row] if 0 <= row < ROWS else rim[rim_of(KEEP, row)]
@@ -462,18 +505,26 @@
         u_out[row + 2] = wind_x(
             at.keep(row), u_after(row), pick(p_own, p_rim, row - 1), pick(p_own, p_rim, row + 1)
         )
-    for row in range(-1, ROWS + 1):
-        v_out[row + 1], w_out[row + 1], p_out[row + 1] = column_step(
-            at.keep(row), table, pick(p_own, p_rim, row), u_out[row + 1], u_out[row + 3],
-            pick(v_own, v_rim, row), pick(w_own, w_rim, row), s_mid[row + 1],
+    for rows in in_groups(range(-1, ROWS + 1)):
+        results = column_steps(
+            table,
+            [
+                (
+                    at.keep(row), pick(p_own, p_rim, row), u_out[row + 1], u_out[row + 3],
+                    pick(v_own, v_rim, row), pick(w_own, w_rim, row), s_mid[row + 1],
+                )
+                for row in rows
+            ],
         )
+        for row, result in zip(rows, results):
+            v_out[row + 1], w_out[row + 1], p_out[row + 1] = result
 
 
 def last_kernel(
     counts, off_ref, u_rim, v_rim, w_rim, p_rim, s_rim, u_mid, v_mid, w_mid, p_mid,
     low_ref, high_ref, table_ref, parent_ref,
-    new_ref, back_ref,
-    u_win, v_win, w_win, q_win,
+    new_hbm, back_hbm,
+    u_win, v_win, w_win, q_win, new_win, back_win, sems,
 ):
     levels = u_rim.shape[1]
     at = Place(counts, off_ref, levels)
@@ -491,30 +542,60 @@
         v_win[row + 2] = v_mid[row]
         w_win[row + 2] = w_mid[row]
         q_win[row + 2] = p_mid[row]
+    windows = ((U, u_win, 4), (V, v_win, KEEP), (W, w_win, KEEP), (PR, q_win, KEEP))
+    send_out(True, at, windows, new_win, new_hbm, sems)
     low_p = [sent(low_ref, 0), sent(low_ref, 1), p_rim[0], p_rim[1]]
     high_p = [p_rim[4], p_rim[5], sent(high_ref, 0), sent(high_ref, 1)]
     for n, row in enumerate((-4, -3)):
         u_win[n] = wind_x(at.keep(row), u_rim[n], low_p[n], low_p[n + 2])
     for n, row in enumerate((8, 9)):
         u_win[12 + n] = wind_x(at.keep(row), u_rim[6 + n], high_p[n], high_p[n + 2])
-    for n, row in enumerate((-3, -2, 7, 8)):
-        rim = (0, 1, 4, 5)[n]
-        v_win[row + KEEP], w_win[row + KEEP], q_win[row + KEEP] = column_step(
-            at.keep(row), table, p_rim[rim], u_win[row + 3], u_win[row + 5],
-            v_rim[rim], w_rim[rim], s_rim[n],
+    for rows in in_groups(enumerate((-3, -2, 7, 8))):
+        rims = [(0, 1, 4, 5)[n] for n, _ in rows]
+        results = column_steps(
+            table,
+            [
+                (
+                    at.keep(row), p_rim[rim], u_win[row + 3], u_win[row + 5],
+                    v_rim[rim], w_rim[rim], s_rim[n],
+                )
+                for (n, row), rim in zip(rows, rims)
+            ],
         )
-    windows = ((U, u_win, 4), (V, v_win, KEEP), (W, w_win, KEEP), (PR, q_win, KEEP))
-    finish(at, windows, parent_ref, new_ref, back_ref)
-
-
-def finish(at, windows, parent_ref, new_ref, back_ref):
+        for (_, row), result in zip(rows, results):
+            v_win[row + KEEP], w_win[row + KEEP], q_win[row + KEEP] = result
+    send_out(False, at, windows, new_win, new_hbm, sems)
+    feed_back(at, windows, parent_ref, back_win, back_hbm, sems)
+    for ready in (True, False):
+        send_out(ready, at, windows, new_win, new_hbm, sems, wait=True)
+
+
+def send_out(ready, at, windows, new_win, new_hbm, sems, wait=False):
+    move_y = lax.rem(WIDE - RATIO * at.off_y, WIDE)
+    for step in (-1, 0, 1):
+        kept = [row for row in range(ROWS) if (-1 <= row + RATIO * step <= ROWS) == ready]
+        if not kept:
+            continue
+
+        @pl.when(at.off_x == step)
+        def _(step=step, kept=kept):
+            for field, window, deep in windows:
+                if not wait:
+                    for row in kept:
+                        moved = pltpu.roll(window[row + deep + RATIO * step], move_y, 1)
+                        new_win[field, row] = moved[:, :COLS]
+                part = pl.ds(kept[0], len(kept))
+                copy = pltpu.make_async_copy(
+                    new_win.at[field, part], new_hbm.at[field, part], sems.at[field + (0 if ready else 4)]
+                )
+                if wait:
+                    copy.wait()
+                else:
+                    copy.start()
+
+
+def feed_back(at, windows, parent_ref, back_win, back_hbm, sems):
     levels = parent_ref.shape[2]
-    move_y = lax.rem(WIDE - RATIO * at.off_y, WIDE)
-    for field, window, deep in windows:
-        for row in range(ROWS):
-            moved = pltpu.roll(window[row + deep + RATIO * at.off_x], move_y, 1)
-            new_ref[field, row] = moved[:, :COLS]
-
     cells_x, cells_y = at.nx // RATIO, at.ny // RATIO
     coarse_rows, coarse_cols = ROWS // RATIO, COLS // RATIO
 
@@ -535,6 +616,7 @@
         + 0.25 * inside(cell + 1, cells_y).astype(F32)
     )
     centre_y = inside(cell, cells_y).astype(jnp.int32)
+    smooth = []
     for coarse in range(coarse_rows):
         a = at.gx * coarse_rows + coarse - at.off_x
         inner = [inside(a + d, cells_x).astype(F32) for d in (-1, 0, 1)]
@@ -542,7 +624,10 @@
         weight_x = weights[0] + weights[1] + weights[2]
         centre = (centre_y * inside(a, cells_x).astype(jnp.int32)) > 0
         scale = jnp.where(centre, 1.0 / jnp.where(centre, 9.0 * weight_x * weight_y, 1.0), 0.0)
-        for field, window, deep in windows:
+        smooth.append((inner, weights, centre, scale))
+    copies = []
+    for field, window, deep in windows:
+        for coarse, (inner, weights, centre, scale) in enumerate(smooth):
             start = deep - KEEP + RATIO * coarse
             total = None
             for d in range(3):
@@ -555,10 +640,14 @@
             summed = jnp.dot(high, spread, preferred_element_type=F32) + jnp.dot(
                 low, spread, preferred_element_type=F32
             )
-            back_ref[field, :, coarse, :] = jnp.where(centre, summed * scale, parent_ref[field, coarse])
-
-
-def call(body, ins, outs, scratch=(), spaces=None):
+            back_win[field, :, coarse, :] = jnp.where(centre, summed * scale, parent_ref[field, coarse])
+        copies.append(pltpu.make_async_copy(back_win.at[field], back_hbm.at[field], sems.at[8 + field]))
+        copies[-1].start()
+    for copy in copies:
+        copy.wait()
+
+
+def call(body, ins, outs, scratch=(), spaces=None, out_spaces=None):
     def space(x):
         if x.dtype == jnp.int32:
             return pltpu.SMEM
@@ -569,7 +658,7 @@
         body,
         out_shape=[jax.ShapeDtypeStruct(shape, F32) for shape in outs],
         in_specs=[pl.BlockSpec(memory_space=s) for s in spaces],
-        out_specs=[pl.BlockSpec(memory_space=pltpu.VMEM) for _ in outs],
+        out_specs=[pl.BlockSpec(memory_space=s) for s in out_spaces or [pltpu.VMEM] * len(outs)],
         scratch_shapes=[s if not isinstance(s, tuple) else pltpu.VMEM(s, F32) for s in scratch],
         compiler_params=pltpu.CompilerParams(vmem_limit_bytes=VMEM_BYTES),
     )(*ins)
@@ -594,7 +683,7 @@
     nothing = jnp.zeros_like(inverse_table[:1])
     shifted = jnp.concatenate([inverse_table[1:], nothing], 0)
     shifted += jnp.concatenate([nothing, inverse_table[:-1]], 0)
-    stack = jnp.concatenate([inverse_table, shifted], 0)
+    stack = jnp.concatenate([inverse_table, 0.25 * shifted], 0)
     top = lax.reduce_precision(stack, 8, 7)
     table = jnp.concatenate([top, top, stack - top], 1).astype(BF16)
 
@@ -642,7 +731,9 @@
         functools.partial(last_kernel, counts),
         (offsets, *outer, low4, high4, table, coarse),
         [nest.shape, parent.shape],
-        [rows(ROWS + 8), rows(ROWS + 6), rows(ROWS + 6), rows(ROWS + 6)],
+        [rows(ROWS + 8), rows(ROWS + 6), rows(ROWS + 6), rows(ROWS + 6)]
+        + [nest.shape, parent.shape, pltpu.SemaphoreType.DMA((12,))],
+        out_spaces=[pl.ANY, pl.ANY],
     )
     return jnp.transpose(new, (0, 2, 1, 3)), back
 

time: 56.2 us -> 55.6 us (0.989)
  transfers between devices with their start and end apart: 10 -> 10, of which waited for: 2 -> 2; matrix products, arithmetic and copies ran while one was open for 0% -> 0% of each run, Pallas kernels for 16% -> 15%
where the time goes in v5:
time: 55.6 us; the launch traced here: 55.2 us
  starting transfers between devices  34.2 us (62%)
  Pallas kernels  15.6 us (28%)
  waiting for transfers between devices  4.49 us (8%)
  between operations  0.86 us (2%)
    ppermute x10, starting transfers between devices, swap(): return lax.ppermute(x, axis, pairs + [(high, low) for low, high in pairs])  34.2 us
    pallas_call x6, Pallas kernels, call(): pl.pallas_call(body, out_shape=[jax.ShapeDtypeStruct(shape, F32) for shap...  15.6 us
    ppermute x10, waiting for transfers between devices, swap(): return lax.ppermute(x, axis, pairs + [(high, low) for low, high in pairs])  4.49 us
  transfers between devices with their start and end apart: 10, of which 2 were waited for; matrix products, arithmetic and copies ran while one was open for 0% of the time, Pallas kernels for 15%

profile of v5, /device:TPU:252, one launch (start us, length us, event | category | flops | bytes accessed | tf_op | source)
XLA Modules:
  0.0 55.2 jit_solution(9838747572587367317)
XLA Ops:
  0.6 2.9 %shard_map.68 = (f32[4,6,48,384]{3,2,1,0:T(8,128)S(1)}, f32[6,48,384]{2,1,0:T(8,128)S(1)}, f32[4,2,48,128]{3,2,1,0:T(8,128)S(1)}, f32[48,384]{1,0:T(8,128)S(1)},...) custom-call(s32[2]{0:T(128)} %off_ref.9, ...), custom_call_target="tpu_custom_call" | custom-call | tf_op jit(solution)/shard_map/pallas_call | solution.py:657
  3.5 0.0 copy-start.1
  3.6 0.0 copy-start
  3.6 2.4 %collective-permute-start.2 = (f32[9,48,384]{2,1,0:T(8,128)S(1)}, f32[9,48,384]{2,1,0:T(8,128)S(1)}, u32[]{:S(2)}, u32[]{:S(2)}) collective-permute-start(f32[9,48,384]{2,1,0:T(8,128)S(1)} %get-tuple-element.42), channel_id=1, source_target_pairs={{16,32},{48,64},{80,96},{112,128},{144,160},{176,192},{208,224},{2... | collective-permute-start | bytes 1990664 | tf_op jit(solution)/shard_map/ppermute | solution.py:670
  6.0 6.1 %collective-permute-start.3 = (f32[9,48,384]{2,1,0:T(8,128)S(1)}, f32[9,48,384]{2,1,0:T(8,128)S(1)}, u32[]{:S(2)}, u32[]{:S(2)}) collective-permute-start(f32[9,48,384]{2,1,0:T(8,128)S(1)} %get-tuple-element.43), channel_id=1, source_target_pairs={{0,16},{32,48},{64,80},{96,112},{128,144},{160,176},{192,208},{224... | collective-permute-start | bytes 1990664 | tf_op jit(solution)/shard_map/ppermute | solution.py:670
  12.1 2.1 %collective-permute-start = (f32[48,384]{1,0:T(8,128)S(1)}, f32[48,384]{1,0:T(8,128)S(1)}, u32[]{:S(2)}, u32[]{:S(2)}) collective-permute-start(f32[48,384]{1,0:T(8,128)S(1)} %get-tuple-element.39), channel_id=1, source_target_pairs={{1,2},{3,4},{5,6},{7,8},{9,10},{11,12},{13,14},{2,1},{4,3},{6,5},{... | collective-permute-start | bytes 221192 | tf_op jit(solution)/shard_map/ppermute | solution.py:670
  14.2 1.9 %collective-permute-start.1 = (f32[48,384]{1,0:T(8,128)S(1)}, f32[48,384]{1,0:T(8,128)S(1)}, u32[]{:S(2)}, u32[]{:S(2)}) collective-permute-start(f32[48,384]{1,0:T(8,128)S(1)} %get-tuple-element.40), channel_id=1, source_target_pairs={{0,1},{2,3},{4,5},{6,7},{8,9},{10,11},{12,13},{14,15},{1,0},{3,2},... | collective-permute-start | bytes 221192 | tf_op jit(solution)/shard_map/ppermute | solution.py:670
  16.2 1.6 %collective-permute-done.left_ref = f32[48,384]{1,0:T(8,128)S(1)} collective-permute-done((f32[48,384]{1,0:T(8,128)S(1)}, f32[48,384]{1,0:T(8,128)S(1)}, u32[]{:S(2)}, u32[]{:S(2)}) %collective-permute-start) | collective-permute-done | bytes 73760 | tf_op jit(solution)/shard_map/ppermute | solution.py:670
  17.8 0.0 collective-permute-done.1.right_ref
  17.8 0.4 shard_map.69
  18.1 1.9 %collective-permute-start.4 = (f32[5,48,384]{2,1,0:T(8,128)S(1)}, f32[5,48,384]{2,1,0:T(8,128)S(1)}, u32[]{:S(2)}, u32[]{:S(2)}) collective-permute-start(f32[5,48,384]{2,1,0:T(8,128)S(1)} %get-tuple-element.47), channel_id=1, source_target_pairs={{16,32},{48,64},{80,96},{112,128},{144,160},{176,192},{208,224},{2... | collective-permute-start | bytes 1105928 | tf_op jit(solution)/shard_map/ppermute | solution.py:670
  20.1 4.9 %collective-permute-start.6 = (f32[5,48,384]{2,1,0:T(8,128)S(1)}, f32[5,48,384]{2,1,0:T(8,128)S(1)}, u32[]{:S(2)}, u32[]{:S(2)}) collective-permute-start(f32[5,48,384]{2,1,0:T(8,128)S(1)} %get-tuple-element.49), channel_id=1, source_target_pairs={{0,16},{32,48},{64,80},{96,112},{128,144},{160,176},{192,208},{224... | collective-permute-start | bytes 1105928 | tf_op jit(solution)/shard_map/ppermute | solution.py:670
  24.9 0.0 copy-done.1
  25.0 0.0 collective-permute-done.2.low1
  25.0 2.9 %collective-permute-done.3.high1 = f32[9,48,384]{2,1,0:T(8,128)S(1)} collective-permute-done((f32[9,48,384]{2,1,0:T(8,128)S(1)}, f32[9,48,384]{2,1,0:T(8,128)S(1)}, u32[]{:S(2)}, u32[]{:S(2)}) %collective-permute-start.3) | collective-permute-done | bytes 663584 | tf_op jit(solution)/shard_map/ppermute | solution.py:670
  27.8 0.0 copy-done
  27.9 1.2 %shard_map.70 = (f32[6,48,384]{2,1,0:T(8,128)S(1)}, f32[6,48,384]{2,1,0:T(8,128)S(1)}, f32[4,6,48,512]{3,2,1,0:T(8,128)S(1)}, f32[6,48,512]{2,1,0:T(8,128)S(1)}, f32[4,48,512]{2,1,0:T(8,128)S(1)}) custom-call(s32[2]{0:T(128)S(1)} %copy-done, f32[4,6,48,384]{3,2,1,0:T(8,128)S(1)} %get-tuple-element.35.cur_ref, f32[6,48,384]{2,1,0:T(8,128)S(1)} %get-tuple-element.36.stiff_ref, ...), custom_call_target="tpu_custom_call" | custom-call | tf_op jit(solution)/shard_map/pallas_call | solution.py:657
  29.0 1.9 %collective-permute-start.5 = (f32[6,48,384]{2,1,0:T(8,128)S(1)}, f32[6,48,384]{2,1,0:T(8,128)S(1)}, u32[]{:S(2)}, u32[]{:S(2)}) collective-permute-start(f32[6,48,384]{2,1,0:T(8,128)S(1)} %get-tuple-element.48), channel_id=1, source_target_pairs={{16,32},{48,64},{80,96},{112,128},{144,160},{176,192},{208,224},{2... | collective-permute-start | bytes 1327112 | tf_op jit(solution)/shard_map/ppermute | solution.py:670
  30.9 5.3 %collective-permute-start.7 = (f32[6,48,384]{2,1,0:T(8,128)S(1)}, f32[6,48,384]{2,1,0:T(8,128)S(1)}, u32[]{:S(2)}, u32[]{:S(2)}) collective-permute-start(f32[6,48,384]{2,1,0:T(8,128)S(1)} %get-tuple-element.50), channel_id=1, source_target_pairs={{0,16},{32,48},{64,80},{96,112},{128,144},{160,176},{192,208},{224... | collective-permute-start | bytes 1327112 | tf_op jit(solution)/shard_map/ppermute | solution.py:670
  36.3 0.1 pad_maximum_fusion.1.table_ref
  36.4 0.0 collective-permute-done.4.low2
  36.4 0.0 collective-permute-done.6.high2
  36.4 2.3 %shard_map.71 = (f32[8,48,512]{2,1,0:T(8,128)S(1)}, f32[6,48,512]{2,1,0:T(8,128)S(1)}, f32[6,48,512]{2,1,0:T(8,128)S(1)}, f32[6,48,512]{2,1,0:T(8,128)S(1)}, f32...) custom-call(s32[2]{0:T(128)S(1)} %copy-done, f32[4,6,48,512]{3,2,1,0:T(8,128)S(1)} %get-tuple-element.44.own_ref, ...), custom_call_target="tpu_custom_call" | custom-call | tf_op jit(solution)/shard_map/pallas_call | solution.py:657
  38.7 1.9 %collective-permute-start.8 = (f32[7,48,128]{2,1,0:T(8,128)S(1)}, f32[7,48,128]{2,1,0:T(8,128)S(1)}, u32[]{:S(2)}, u32[]{:S(2)}) collective-permute-start(f32[7,48,128]{2,1,0:T(8,128)S(1)} %get-tuple-element.64), channel_id=1, source_target_pairs={{16,32},{48,64},{80,96},{112,128},{144,160},{176,192},{208,224},{2... | collective-permute-start | bytes 516104 | tf_op jit(solution)/shard_map/ppermute | solution.py:670
  40.7 5.6 %collective-permute-start.9 = (f32[7,48,128]{2,1,0:T(8,128)S(1)}, f32[7,48,128]{2,1,0:T(8,128)S(1)}, u32[]{:S(2)}, u32[]{:S(2)}) collective-permute-start(f32[7,48,128]{2,1,0:T(8,128)S(1)} %get-tuple-element.65), channel_id=1, source_target_pairs={{0,16},{32,48},{64,80},{96,112},{128,144},{160,176},{192,208},{224... | collective-permute-start | bytes 516104 | tf_op jit(solution)/shard_map/ppermute | solution.py:670
  46.3 0.0 collective-permute-done.5.low3
  46.3 0.0 collective-permute-done.7.high3
  46.3 4.6 %shard_map.72 = (f32[8,48,512]{2,1,0:T(8,128)S(1)}, f32[6,48,512]{2,1,0:T(8,128)S(1)}, f32[6,48,512]{2,1,0:T(8,128)S(1)}, f32[6,48,512]{2,1,0:T(8,128)S(1)}, f32...) custom-call(s32[2]{0:T(128)S(1)} %copy-done, ...), custom_call_target="tpu_custom_call" | custom-call | tf_op jit(solution)/shard_map/pallas_call | solution.py:657
  51.0 0.0 collective-permute-done.8.low_ref
  51.0 0.0 collective-permute-done.9.high_ref
  51.0 4.2 %shard_map.73 = (f32[4,6,48,384]{3,2,1,0:T(8,128)}, f32[4,48,2,128]{3,2,1,0:T(2,128)}) custom-call(s32[2]{0:T(128)S(1)} %copy-done, f32[8,48,512]{2,1,0:T(8,128)S(1)} %get-tuple-element.55.u_rim, f32[6,48,512]{2,1,0:T(8,128)S(1)} %get-tuple-element.56.v_rim, f32[6,48,512]{2,1,0:T(8,128)S(1)} %get-tuple-element.57.w_rim, ...), custom_call_target="tpu_custom_call" | custom-call | tf_op jit(solution)/shard_map/pallas_call | solution.py:657
  (3 shorter events, 0.0 us)
Async XLA Ops:
  3.5 21.4 %copy-start.1 = (f32[48,48]{1,0:T(8,128)S(1)}, f32[48,48]{1,0:T(8,128)}, u32[]{:S(2)}) copy-start(f32[48,48]{1,0:T(8,128)} %param.8) | copy-start | bytes 27652
  3.6 24.3 %copy-start = (s32[2]{0:T(128)S(1)}, s32[2]{0:T(128)}, u32[]{:S(2)}) copy-start(s32[2]{0:T(128)} %off_ref.9) | copy-start | bytes 28
  3.6 21.4 %collective-permute-start.2 = (f32[9,48,384]{2,1,0:T(8,128)S(1)}, f32[9,48,384]{2,1,0:T(8,128)S(1)}, u32[]{:S(2)}, u32[]{:S(2)}) collective-permute-start(f32[9,48,384]{2,1,0:T(8,128)S(1)} %get-tuple-element.42), channel_id=1, source_target_pairs={{16,32},{48,64},{80,96},{112,128},{144,160},{176,192},{208,224},{2... | collective-permute-start | bytes 1990664 | tf_op jit(solution)/shard_map/ppermute | solution.py:670
  6.0 21.8 %collective-permute-start.3 = (f32[9,48,384]{2,1,0:T(8,128)S(1)}, f32[9,48,384]{2,1,0:T(8,128)S(1)}, u32[]{:S(2)}, u32[]{:S(2)}) collective-permute-start(f32[9,48,384]{2,1,0:T(8,128)S(1)} %get-tuple-element.43), channel_id=1, source_target_pairs={{0,16},{32,48},{64,80},{96,112},{128,144},{160,176},{192,208},{224... | collective-permute-start | bytes 1990664 | tf_op jit(solution)/shard_map/ppermute | solution.py:670
  12.1 5.7 %collective-permute-start = (f32[48,384]{1,0:T(8,128)S(1)}, f32[48,384]{1,0:T(8,128)S(1)}, u32[]{:S(2)}, u32[]{:S(2)}) collective-permute-start(f32[48,384]{1,0:T(8,128)S(1)} %get-tuple-element.39), channel_id=1, source_target_pairs={{1,2},{3,4},{5,6},{7,8},{9,10},{11,12},{13,14},{2,1},{4,3},{6,5},{... | collective-permute-start | bytes 221192 | tf_op jit(solution)/shard_map/ppermute | solution.py:670
  14.2 3.5 %collective-permute-start.1 = (f32[48,384]{1,0:T(8,128)S(1)}, f32[48,384]{1,0:T(8,128)S(1)}, u32[]{:S(2)}, u32[]{:S(2)}) collective-permute-start(f32[48,384]{1,0:T(8,128)S(1)} %get-tuple-element.40), channel_id=1, source_target_pairs={{0,1},{2,3},{4,5},{6,7},{8,9},{10,11},{12,13},{14,15},{1,0},{3,2},... | collective-permute-start | bytes 221192 | tf_op jit(solution)/shard_map/ppermute | solution.py:670
  18.1 18.3 %collective-permute-start.4 = (f32[5,48,384]{2,1,0:T(8,128)S(1)}, f32[5,48,384]{2,1,0:T(8,128)S(1)}, u32[]{:S(2)}, u32[]{:S(2)}) collective-permute-start(f32[5,48,384]{2,1,0:T(8,128)S(1)} %get-tuple-element.47), channel_id=1, source_target_pairs={{16,32},{48,64},{80,96},{112,128},{144,160},{176,192},{208,224},{2... | collective-permute-start | bytes 1105928 | tf_op jit(solution)/shard_map/ppermute | solution.py:670
  20.1 16.4 %collective-permute-start.6 = (f32[5,48,384]{2,1,0:T(8,128)S(1)}, f32[5,48,384]{2,1,0:T(8,128)S(1)}, u32[]{:S(2)}, u32[]{:S(2)}) collective-permute-start(f32[5,48,384]{2,1,0:T(8,128)S(1)} %get-tuple-element.49), channel_id=1, source_target_pairs={{0,16},{32,48},{64,80},{96,112},{128,144},{160,176},{192,208},{224... | collective-permute-start | bytes 1105928 | tf_op jit(solution)/shard_map/ppermute | solution.py:670
  29.0 17.3 %collective-permute-start.5 = (f32[6,48,384]{2,1,0:T(8,128)S(1)}, f32[6,48,384]{2,1,0:T(8,128)S(1)}, u32[]{:S(2)}, u32[]{:S(2)}) collective-permute-start(f32[6,48,384]{2,1,0:T(8,128)S(1)} %get-tuple-element.48), channel_id=1, source_target_pairs={{16,32},{48,64},{80,96},{112,128},{144,160},{176,192},{208,224},{2... | collective-permute-start | bytes 1327112 | tf_op jit(solution)/shard_map/ppermute | solution.py:670
  30.9 15.4 %collective-permute-start.7 = (f32[6,48,384]{2,1,0:T(8,128)S(1)}, f32[6,48,384]{2,1,0:T(8,128)S(1)}, u32[]{:S(2)}, u32[]{:S(2)}) collective-permute-start(f32[6,48,384]{2,1,0:T(8,128)S(1)} %get-tuple-element.50), channel_id=1, source_target_pairs={{0,16},{32,48},{64,80},{96,112},{128,144},{160,176},{192,208},{224... | collective-permute-start | bytes 1327112 | tf_op jit(solution)/shard_map/ppermute | solution.py:670
  38.7 12.2 %collective-permute-start.8 = (f32[7,48,128]{2,1,0:T(8,128)S(1)}, f32[7,48,128]{2,1,0:T(8,128)S(1)}, u32[]{:S(2)}, u32[]{:S(2)}) collective-permute-start(f32[7,48,128]{2,1,0:T(8,128)S(1)} %get-tuple-element.64), channel_id=1, source_target_pairs={{16,32},{48,64},{80,96},{112,128},{144,160},{176,192},{208,224},{2... | collective-permute-start | bytes 516104 | tf_op jit(solution)/shard_map/ppermute | solution.py:670
  40.7 10.3 %collective-permute-start.9 = (f32[7,48,128]{2,1,0:T(8,128)S(1)}, f32[7,48,128]{2,1,0:T(8,128)S(1)}, u32[]{:S(2)}, u32[]{:S(2)}) collective-permute-start(f32[7,48,128]{2,1,0:T(8,128)S(1)} %get-tuple-element.65), channel_id=1, source_target_pairs={{0,16},{32,48},{64,80},{96,112},{128,144},{160,176},{192,208},{224... | collective-permute-start | bytes 516104 | tf_op jit(solution)/shard_map/ppermute | solution.py:670

commit v6 on v5

--- a/solution.py
+++ b/solution.py
@@ -141,9 +141,8 @@
     col = lanes_of((levels, COLS)) + (gy * COLS - RATIO * off_y)
     edge_col = is_edge(col, ny)
     place = lanes_of((levels, LANES)) // SIDE
-    packs = [[None, None] for _ in range(PACK // LANES)]
-
-    def pack(row, group):
+
+    def pack(packs, row, group):
         tile, slot = group // SLOTS, group % SLOTS
         sides = (
             turn(row[:, :LANES], SIDE * slot),
@@ -153,30 +152,44 @@
             held = packs[tile][side]
             packs[tile][side] = value if held is None else jnp.where(place == slot, value, held)
 
-    copies[0].wait()
-    rims = []
-    for at, field in enumerate((V, W, PR, U)):
-        bounds = []
-        for coarse in range(ROWS // RATIO):
-            value = parent_win[field, :, coarse, :]
-            parent_ref[field, coarse] = value
-            bounds.append(expand_all(value))
-        copies[1 + at].wait()
+    def fill(on_rim):
+        packs = [[None, None] for _ in range(PACK // LANES)]
+        if on_rim:
+            copies[0].wait()
+        for at, field in enumerate((V, W, PR, U)):
+            if on_rim:
+                bounds = [expand_all(parent_win[field, :, coarse, :]) for coarse in range(ROWS // RATIO)]
+            copies[1 + at].wait()
+            for row in range(ROWS):
+                value = nest_win[field, row]
+                if on_rim:
+                    i = gx * ROWS + row - RATIO * off_x
+                    held = is_edge(i, nx).astype(jnp.int32)
+                    value = jnp.where(edge_col | (held > 0), bounds[row // RATIO], value)
+                cur_ref[field, row] = value
+                pack(packs, value, field * ROWS + row)
+            rim = jnp.where(gx == 0, bounds[0], bounds[-1]) if on_rim else jnp.zeros((levels, COLS), F32)
+            edge_ref[field] = rim
+            if on_rim:
+                pack(packs, rim, EDGE_GROUP + field)
+        copies[5].wait()
         for row in range(ROWS):
-            i = gx * ROWS + row - RATIO * off_x
-            held = is_edge(i, nx).astype(jnp.int32)
-            value = jnp.where(edge_col | (held > 0), bounds[row // RATIO], nest_win[field, row])
-            cur_ref[field, row] = value
-            pack(value, field * ROWS + row)
-        rim = jnp.where(gx == 0, bounds[0], bounds[-1])
-        edge_ref[field] = rim
-        pack(rim, EDGE_GROUP + field)
-    copies[5].wait()
-    for row in range(ROWS):
-        pack(stiff_ref[row], S_GROUP + row)
-    for tile, (left, right) in enumerate(packs):
-        at = slice(LANES * tile, LANES * (tile + 1))
-        left_ref[:, at], right_ref[:, at] = by_pair(is_odd(gy), right, left)
+            pack(packs, stiff_ref[row], S_GROUP + row)
+        for tile, (left, right) in enumerate(packs):
+            at = slice(LANES * tile, LANES * (tile + 1))
+            if left is None:
+                left = right = jnp.zeros((levels, LANES), F32)
+            left_ref[:, at], right_ref[:, at] = by_pair(is_odd(gy), right, left)
+        if not on_rim:
+            copies[0].wait()
+        for field in range(4):
+            for coarse in range(ROWS // RATIO):
+                parent_ref[field, coarse] = parent_win[field, :, coarse, :]
+
+    rim_x = (gx == 0) | (gx == nx // ROWS - 1)
+    rim_y = (gy == 0) | (gy == ny // COLS - 1)
+    pl.when(rim_x | rim_y)(lambda: fill(True))
+    pl.when(jnp.logical_not(rim_x | rim_y))(lambda: fill(False))
     fill_message(CHUNK_1, cur_ref, stiff_ref, up_ref, down_ref)
 
 

time: 55.6 us -> 55.8 us (level)
  no operation moved by 1% of the time
where the time goes in v6:
time: 55.8 us; the launch traced here: 55.3 us
  starting transfers between devices  34.4 us (62%)
  Pallas kernels  15.5 us (28%)
  waiting for transfers between devices  4.46 us (8%)
  between operations  0.86 us (2%)
    ppermute x10, starting transfers between devices, swap(): return lax.ppermute(x, axis, pairs + [(high, low) for low, high in pairs])  34.4 us
    pallas_call x6, Pallas kernels, call(): pl.pallas_call(body, out_shape=[jax.ShapeDtypeStruct(shape, F32) for shap...  15.5 us
    ppermute x10, waiting for transfers between devices, swap(): return lax.ppermute(x, axis, pairs + [(high, low) for low, high in pairs])  4.46 us
  transfers between devices with their start and end apart: 10, of which 2 were waited for; matrix products, arithmetic and copies ran while one was open for 0% of the time, Pallas kernels for 15%

profile of v6, /device:TPU:252, one launch (start us, length us, event | category | flops | bytes accessed | tf_op | source)
XLA Modules:
  0.0 55.3 jit_solution(11190879332992316464)
XLA Ops:
  0.6 2.8 %shard_map.68 = (f32[4,6,48,384]{3,2,1,0:T(8,128)S(1)}, f32[6,48,384]{2,1,0:T(8,128)S(1)}, f32[4,2,48,128]{3,2,1,0:T(8,128)S(1)}, f32[48,384]{1,0:T(8,128)S(1)},...) custom-call(s32[2]{0:T(128)} %off_ref.9, ...), custom_call_target="tpu_custom_call" | custom-call | tf_op jit(solution)/shard_map/pallas_call | solution.py:670
  3.4 0.0 copy-start.1
  3.4 0.0 copy-start
  3.4 2.4 %collective-permute-start.2 = (f32[9,48,384]{2,1,0:T(8,128)S(1)}, f32[9,48,384]{2,1,0:T(8,128)S(1)}, u32[]{:S(2)}, u32[]{:S(2)}) collective-permute-start(f32[9,48,384]{2,1,0:T(8,128)S(1)} %get-tuple-element.42), channel_id=1, source_target_pairs={{16,32},{48,64},{80,96},{112,128},{144,160},{176,192},{208,224},{2... | collective-permute-start | bytes 1990664 | tf_op jit(solution)/shard_map/ppermute | solution.py:683
  5.9 6.1 %collective-permute-start.3 = (f32[9,48,384]{2,1,0:T(8,128)S(1)}, f32[9,48,384]{2,1,0:T(8,128)S(1)}, u32[]{:S(2)}, u32[]{:S(2)}) collective-permute-start(f32[9,48,384]{2,1,0:T(8,128)S(1)} %get-tuple-element.43), channel_id=1, source_target_pairs={{0,16},{32,48},{64,80},{96,112},{128,144},{160,176},{192,208},{224... | collective-permute-start | bytes 1990664 | tf_op jit(solution)/shard_map/ppermute | solution.py:683
  12.0 2.1 %collective-permute-start = (f32[48,384]{1,0:T(8,128)S(1)}, f32[48,384]{1,0:T(8,128)S(1)}, u32[]{:S(2)}, u32[]{:S(2)}) collective-permute-start(f32[48,384]{1,0:T(8,128)S(1)} %get-tuple-element.39), channel_id=1, source_target_pairs={{1,2},{3,4},{5,6},{7,8},{9,10},{11,12},{13,14},{2,1},{4,3},{6,5},{... | collective-permute-start | bytes 221192 | tf_op jit(solution)/shard_map/ppermute | solution.py:683
  14.1 1.9 %collective-permute-start.1 = (f32[48,384]{1,0:T(8,128)S(1)}, f32[48,384]{1,0:T(8,128)S(1)}, u32[]{:S(2)}, u32[]{:S(2)}) collective-permute-start(f32[48,384]{1,0:T(8,128)S(1)} %get-tuple-element.40), channel_id=1, source_target_pairs={{0,1},{2,3},{4,5},{6,7},{8,9},{10,11},{12,13},{14,15},{1,0},{3,2},... | collective-permute-start | bytes 221192 | tf_op jit(solution)/shard_map/ppermute | solution.py:683
  16.0 1.6 %collective-permute-done.left_ref = f32[48,384]{1,0:T(8,128)S(1)} collective-permute-done((f32[48,384]{1,0:T(8,128)S(1)}, f32[48,384]{1,0:T(8,128)S(1)}, u32[]{:S(2)}, u32[]{:S(2)}) %collective-permute-start) | collective-permute-done | bytes 73760 | tf_op jit(solution)/shard_map/ppermute | solution.py:683
  17.6 0.0 collective-permute-done.1.right_ref
  17.6 0.4 shard_map.69
  18.0 1.9 %collective-permute-start.4 = (f32[5,48,384]{2,1,0:T(8,128)S(1)}, f32[5,48,384]{2,1,0:T(8,128)S(1)}, u32[]{:S(2)}, u32[]{:S(2)}) collective-permute-start(f32[5,48,384]{2,1,0:T(8,128)S(1)} %get-tuple-element.47), channel_id=1, source_target_pairs={{16,32},{48,64},{80,96},{112,128},{144,160},{176,192},{208,224},{2... | collective-permute-start | bytes 1105928 | tf_op jit(solution)/shard_map/ppermute | solution.py:683
  19.9 4.9 %collective-permute-start.6 = (f32[5,48,384]{2,1,0:T(8,128)S(1)}, f32[5,48,384]{2,1,0:T(8,128)S(1)}, u32[]{:S(2)}, u32[]{:S(2)}) collective-permute-start(f32[5,48,384]{2,1,0:T(8,128)S(1)} %get-tuple-element.49), channel_id=1, source_target_pairs={{0,16},{32,48},{64,80},{96,112},{128,144},{160,176},{192,208},{224... | collective-permute-start | bytes 1105928 | tf_op jit(solution)/shard_map/ppermute | solution.py:683
  24.8 0.0 copy-done.1
  24.8 0.0 collective-permute-done.2.low1
  24.8 2.8 %collective-permute-done.3.high1 = f32[9,48,384]{2,1,0:T(8,128)S(1)} collective-permute-done((f32[9,48,384]{2,1,0:T(8,128)S(1)}, f32[9,48,384]{2,1,0:T(8,128)S(1)}, u32[]{:S(2)}, u32[]{:S(2)}) %collective-permute-start.3) | collective-permute-done | bytes 663584 | tf_op jit(solution)/shard_map/ppermute | solution.py:683
  27.7 0.0 copy-done
  27.7 1.2 %shard_map.70 = (f32[6,48,384]{2,1,0:T(8,128)S(1)}, f32[6,48,384]{2,1,0:T(8,128)S(1)}, f32[4,6,48,512]{3,2,1,0:T(8,128)S(1)}, f32[6,48,512]{2,1,0:T(8,128)S(1)}, f32[4,48,512]{2,1,0:T(8,128)S(1)}) custom-call(s32[2]{0:T(128)S(1)} %copy-done, f32[4,6,48,384]{3,2,1,0:T(8,128)S(1)} %get-tuple-element.35.cur_ref, f32[6,48,384]{2,1,0:T(8,128)S(1)} %get-tuple-element.36.stiff_ref, ...), custom_call_target="tpu_custom_call" | custom-call | tf_op jit(solution)/shard_map/pallas_call | solution.py:670
  28.9 1.9 %collective-permute-start.5 = (f32[6,48,384]{2,1,0:T(8,128)S(1)}, f32[6,48,384]{2,1,0:T(8,128)S(1)}, u32[]{:S(2)}, u32[]{:S(2)}) collective-permute-start(f32[6,48,384]{2,1,0:T(8,128)S(1)} %get-tuple-element.48), channel_id=1, source_target_pairs={{16,32},{48,64},{80,96},{112,128},{144,160},{176,192},{208,224},{2... | collective-permute-start | bytes 1327112 | tf_op jit(solution)/shard_map/ppermute | solution.py:683
  30.8 5.3 %collective-permute-start.7 = (f32[6,48,384]{2,1,0:T(8,128)S(1)}, f32[6,48,384]{2,1,0:T(8,128)S(1)}, u32[]{:S(2)}, u32[]{:S(2)}) collective-permute-start(f32[6,48,384]{2,1,0:T(8,128)S(1)} %get-tuple-element.50), channel_id=1, source_target_pairs={{0,16},{32,48},{64,80},{96,112},{128,144},{160,176},{192,208},{224... | collective-permute-start | bytes 1327112 | tf_op jit(solution)/shard_map/ppermute | solution.py:683
  36.1 0.1 pad_maximum_fusion.1.table_ref
  36.3 0.0 collective-permute-done.4.low2
  36.3 0.0 collective-permute-done.6.high2
  36.3 2.3 %shard_map.71 = (f32[8,48,512]{2,1,0:T(8,128)S(1)}, f32[6,48,512]{2,1,0:T(8,128)S(1)}, f32[6,48,512]{2,1,0:T(8,128)S(1)}, f32[6,48,512]{2,1,0:T(8,128)S(1)}, f32...) custom-call(s32[2]{0:T(128)S(1)} %copy-done, f32[4,6,48,512]{3,2,1,0:T(8,128)S(1)} %get-tuple-element.44.own_ref, ...), custom_call_target="tpu_custom_call" | custom-call | tf_op jit(solution)/shard_map/pallas_call | solution.py:670
  38.6 1.9 %collective-permute-start.8 = (f32[7,48,128]{2,1,0:T(8,128)S(1)}, f32[7,48,128]{2,1,0:T(8,128)S(1)}, u32[]{:S(2)}, u32[]{:S(2)}) collective-permute-start(f32[7,48,128]{2,1,0:T(8,128)S(1)} %get-tuple-element.64), channel_id=1, source_target_pairs={{16,32},{48,64},{80,96},{112,128},{144,160},{176,192},{208,224},{2... | collective-permute-start | bytes 516104 | tf_op jit(solution)/shard_map/ppermute | solution.py:683
  40.5 5.9 %collective-permute-start.9 = (f32[7,48,128]{2,1,0:T(8,128)S(1)}, f32[7,48,128]{2,1,0:T(8,128)S(1)}, u32[]{:S(2)}, u32[]{:S(2)}) collective-permute-start(f32[7,48,128]{2,1,0:T(8,128)S(1)} %get-tuple-element.65), channel_id=1, source_target_pairs={{0,16},{32,48},{64,80},{96,112},{128,144},{160,176},{192,208},{224... | collective-permute-start | bytes 516104 | tf_op jit(solution)/shard_map/ppermute | solution.py:683
  46.4 0.0 collective-permute-done.5.low3
  46.4 0.0 collective-permute-done.7.high3
  46.4 4.6 %shard_map.72 = (f32[8,48,512]{2,1,0:T(8,128)S(1)}, f32[6,48,512]{2,1,0:T(8,128)S(1)}, f32[6,48,512]{2,1,0:T(8,128)S(1)}, f32[6,48,512]{2,1,0:T(8,128)S(1)}, f32...) custom-call(s32[2]{0:T(128)S(1)} %copy-done, ...), custom_call_target="tpu_custom_call" | custom-call | tf_op jit(solution)/shard_map/pallas_call | solution.py:670
  51.1 0.0 collective-permute-done.8.low_ref
  51.1 0.0 collective-permute-done.9.high_ref
  51.1 4.2 %shard_map.73 = (f32[4,6,48,384]{3,2,1,0:T(8,128)}, f32[4,48,2,128]{3,2,1,0:T(2,128)}) custom-call(s32[2]{0:T(128)S(1)} %copy-done, f32[8,48,512]{2,1,0:T(8,128)S(1)} %get-tuple-element.55.u_rim, f32[6,48,512]{2,1,0:T(8,128)S(1)} %get-tuple-element.56.v_rim, f32[6,48,512]{2,1,0:T(8,128)S(1)} %get-tuple-element.57.w_rim, ...), custom_call_target="tpu_custom_call" | custom-call | tf_op jit(solution)/shard_map/pallas_call | solution.py:670
  (3 shorter events, 0.0 us)
Async XLA Ops:
  3.4 21.4 %copy-start.1 = (f32[48,48]{1,0:T(8,128)S(1)}, f32[48,48]{1,0:T(8,128)}, u32[]{:S(2)}) copy-start(f32[48,48]{1,0:T(8,128)} %param.8) | copy-start | bytes 27652
  3.4 24.3 %copy-start = (s32[2]{0:T(128)S(1)}, s32[2]{0:T(128)}, u32[]{:S(2)}) copy-start(s32[2]{0:T(128)} %off_ref.9) | copy-start | bytes 28
  3.4 21.4 %collective-permute-start.2 = (f32[9,48,384]{2,1,0:T(8,128)S(1)}, f32[9,48,384]{2,1,0:T(8,128)S(1)}, u32[]{:S(2)}, u32[]{:S(2)}) collective-permute-start(f32[9,48,384]{2,1,0:T(8,128)S(1)} %get-tuple-element.42), channel_id=1, source_target_pairs={{16,32},{48,64},{80,96},{112,128},{144,160},{176,192},{208,224},{2... | collective-permute-start | bytes 1990664 | tf_op jit(solution)/shard_map/ppermute | solution.py:683
  5.9 21.8 %collective-permute-start.3 = (f32[9,48,384]{2,1,0:T(8,128)S(1)}, f32[9,48,384]{2,1,0:T(8,128)S(1)}, u32[]{:S(2)}, u32[]{:S(2)}) collective-permute-start(f32[9,48,384]{2,1,0:T(8,128)S(1)} %get-tuple-element.43), channel_id=1, source_target_pairs={{0,16},{32,48},{64,80},{96,112},{128,144},{160,176},{192,208},{224... | collective-permute-start | bytes 1990664 | tf_op jit(solution)/shard_map/ppermute | solution.py:683
  12.0 5.7 %collective-permute-start = (f32[48,384]{1,0:T(8,128)S(1)}, f32[48,384]{1,0:T(8,128)S(1)}, u32[]{:S(2)}, u32[]{:S(2)}) collective-permute-start(f32[48,384]{1,0:T(8,128)S(1)} %get-tuple-element.39), channel_id=1, source_target_pairs={{1,2},{3,4},{5,6},{7,8},{9,10},{11,12},{13,14},{2,1},{4,3},{6,5},{... | collective-permute-start | bytes 221192 | tf_op jit(solution)/shard_map/ppermute | solution.py:683
  14.1 3.5 %collective-permute-start.1 = (f32[48,384]{1,0:T(8,128)S(1)}, f32[48,384]{1,0:T(8,128)S(1)}, u32[]{:S(2)}, u32[]{:S(2)}) collective-permute-start(f32[48,384]{1,0:T(8,128)S(1)} %get-tuple-element.40), channel_id=1, source_target_pairs={{0,1},{2,3},{4,5},{6,7},{8,9},{10,11},{12,13},{14,15},{1,0},{3,2},... | collective-permute-start | bytes 221192 | tf_op jit(solution)/shard_map/ppermute | solution.py:683
  18.0 18.3 %collective-permute-start.4 = (f32[5,48,384]{2,1,0:T(8,128)S(1)}, f32[5,48,384]{2,1,0:T(8,128)S(1)}, u32[]{:S(2)}, u32[]{:S(2)}) collective-permute-start(f32[5,48,384]{2,1,0:T(8,128)S(1)} %get-tuple-element.47), channel_id=1, source_target_pairs={{16,32},{48,64},{80,96},{112,128},{144,160},{176,192},{208,224},{2... | collective-permute-start | bytes 1105928 | tf_op jit(solution)/shard_map/ppermute | solution.py:683
  19.9 16.3 %collective-permute-start.6 = (f32[5,48,384]{2,1,0:T(8,128)S(1)}, f32[5,48,384]{2,1,0:T(8,128)S(1)}, u32[]{:S(2)}, u32[]{:S(2)}) collective-permute-start(f32[5,48,384]{2,1,0:T(8,128)S(1)} %get-tuple-element.49), channel_id=1, source_target_pairs={{0,16},{32,48},{64,80},{96,112},{128,144},{160,176},{192,208},{224... | collective-permute-start | bytes 1105928 | tf_op jit(solution)/shard_map/ppermute | solution.py:683
  28.9 17.5 %collective-permute-start.5 = (f32[6,48,384]{2,1,0:T(8,128)S(1)}, f32[6,48,384]{2,1,0:T(8,128)S(1)}, u32[]{:S(2)}, u32[]{:S(2)}) collective-permute-start(f32[6,48,384]{2,1,0:T(8,128)S(1)} %get-tuple-element.48), channel_id=1, source_target_pairs={{16,32},{48,64},{80,96},{112,128},{144,160},{176,192},{208,224},{2... | collective-permute-start | bytes 1327112 | tf_op jit(solution)/shard_map/ppermute | solution.py:683
  30.8 15.6 %collective-permute-start.7 = (f32[6,48,384]{2,1,0:T(8,128)S(1)}, f32[6,48,384]{2,1,0:T(8,128)S(1)}, u32[]{:S(2)}, u32[]{:S(2)}) collective-permute-start(f32[6,48,384]{2,1,0:T(8,128)S(1)} %get-tuple-element.50), channel_id=1, source_target_pairs={{0,16},{32,48},{64,80},{96,112},{128,144},{160,176},{192,208},{224... | collective-permute-start | bytes 1327112 | tf_op jit(solution)/shard_map/ppermute | solution.py:683
  38.6 12.5 %collective-permute-start.8 = (f32[7,48,128]{2,1,0:T(8,128)S(1)}, f32[7,48,128]{2,1,0:T(8,128)S(1)}, u32[]{:S(2)}, u32[]{:S(2)}) collective-permute-start(f32[7,48,128]{2,1,0:T(8,128)S(1)} %get-tuple-element.64), channel_id=1, source_target_pairs={{16,32},{48,64},{80,96},{112,128},{144,160},{176,192},{208,224},{2... | collective-permute-start | bytes 516104 | tf_op jit(solution)/shard_map/ppermute | solution.py:683
  40.5 10.6 %collective-permute-start.9 = (f32[7,48,128]{2,1,0:T(8,128)S(1)}, f32[7,48,128]{2,1,0:T(8,128)S(1)}, u32[]{:S(2)}, u32[]{:S(2)}) collective-permute-start(f32[7,48,128]{2,1,0:T(8,128)S(1)} %get-tuple-element.65), channel_id=1, source_target_pairs={{0,16},{32,48},{64,80},{96,112},{128,144},{160,176},{192,208},{224... | collective-permute-start | bytes 516104 | tf_op jit(solution)/shard_map/ppermute | solution.py:683

commit v7 on v6

--- a/solution.py
+++ b/solution.py
@@ -594,9 +594,17 @@
         def _(step=step, kept=kept):
             for field, window, deep in windows:
                 if not wait:
-                    for row in kept:
-                        moved = pltpu.roll(window[row + deep + RATIO * step], move_y, 1)
-                        new_win[field, row] = moved[:, :COLS]
+                    @pl.when(at.off_y == 0)
+                    def _(field=field, window=window, deep=deep):
+                        for row in kept:
+                            new_win[field, row] = window[row + deep + RATIO * step, :, :COLS]
+
+                    @pl.when(at.off_y != 0)
+                    def _(field=field, window=window, deep=deep):
+                        for row in kept:
+                            moved = pltpu.roll(window[row + deep + RATIO * step], move_y, 1)
+                            new_win[field, row] = moved[:, :COLS]
+
                 part = pl.ds(kept[0], len(kept))
                 copy = pltpu.make_async_copy(
                     new_win.at[field, part], new_hbm.at[field, part], sems.at[field + (0 if ready else 4)]

time: 55.8 us -> 56 us (level)
  no operation moved by 1% of the time
where the time goes in v7:
time: 56 us; the launch traced here: 55.8 us
  starting transfers between devices  34.4 us (61%)
  Pallas kernels  15.9 us (28%)
  waiting for transfers between devices  4.46 us (8%)
  between operations  0.86 us (2%)
    ppermute x10, starting transfers between devices, swap(): return lax.ppermute(x, axis, pairs + [(high, low) for low, high in pairs])  34.4 us
    pallas_call x6, Pallas kernels, call(): pl.pallas_call(body, out_shape=[jax.ShapeDtypeStruct(shape, F32) for shap...  15.9 us
    ppermute x10, waiting for transfers between devices, swap(): return lax.ppermute(x, axis, pairs + [(high, low) for low, high in pairs])  4.46 us
  transfers between devices with their start and end apart: 10, of which 2 were waited for; matrix products, arithmetic and copies ran while one was open for 0% of the time, Pallas kernels for 15%

profile of v7, /device:TPU:252, one launch (start us, length us, event | category | flops | bytes accessed | tf_op | source)
XLA Modules:
  0.0 55.8 jit_solution(14991605757386266197)
XLA Ops:
  0.6 2.8 %shard_map.68 = (f32[4,6,48,384]{3,2,1,0:T(8,128)S(1)}, f32[6,48,384]{2,1,0:T(8,128)S(1)}, f32[4,2,48,128]{3,2,1,0:T(8,128)S(1)}, f32[48,384]{1,0:T(8,128)S(1)},...) custom-call(s32[2]{0:T(128)} %off_ref.9, ...), custom_call_target="tpu_custom_call" | custom-call | tf_op jit(solution)/shard_map/pallas_call | solution.py:678
  3.4 0.0 copy-start.1
  3.4 0.0 copy-start
  3.4 2.4 %collective-permute-start.2 = (f32[9,48,384]{2,1,0:T(8,128)S(1)}, f32[9,48,384]{2,1,0:T(8,128)S(1)}, u32[]{:S(2)}, u32[]{:S(2)}) collective-permute-start(f32[9,48,384]{2,1,0:T(8,128)S(1)} %get-tuple-element.42), channel_id=1, source_target_pairs={{16,32},{48,64},{80,96},{112,128},{144,160},{176,192},{208,224},{2... | collective-permute-start | bytes 1990664 | tf_op jit(solution)/shard_map/ppermute | solution.py:691
  5.9 6.1 %collective-permute-start.3 = (f32[9,48,384]{2,1,0:T(8,128)S(1)}, f32[9,48,384]{2,1,0:T(8,128)S(1)}, u32[]{:S(2)}, u32[]{:S(2)}) collective-permute-start(f32[9,48,384]{2,1,0:T(8,128)S(1)} %get-tuple-element.43), channel_id=1, source_target_pairs={{0,16},{32,48},{64,80},{96,112},{128,144},{160,176},{192,208},{224... | collective-permute-start | bytes 1990664 | tf_op jit(solution)/shard_map/ppermute | solution.py:691
  12.0 2.1 %collective-permute-start = (f32[48,384]{1,0:T(8,128)S(1)}, f32[48,384]{1,0:T(8,128)S(1)}, u32[]{:S(2)}, u32[]{:S(2)}) collective-permute-start(f32[48,384]{1,0:T(8,128)S(1)} %get-tuple-element.39), channel_id=1, source_target_pairs={{1,2},{3,4},{5,6},{7,8},{9,10},{11,12},{13,14},{2,1},{4,3},{6,5},{... | collective-permute-start | bytes 221192 | tf_op jit(solution)/shard_map/ppermute | solution.py:691
  14.1 1.9 %collective-permute-start.1 = (f32[48,384]{1,0:T(8,128)S(1)}, f32[48,384]{1,0:T(8,128)S(1)}, u32[]{:S(2)}, u32[]{:S(2)}) collective-permute-start(f32[48,384]{1,0:T(8,128)S(1)} %get-tuple-element.40), channel_id=1, source_target_pairs={{0,1},{2,3},{4,5},{6,7},{8,9},{10,11},{12,13},{14,15},{1,0},{3,2},... | collective-permute-start | bytes 221192 | tf_op jit(solution)/shard_map/ppermute | solution.py:691
  16.0 1.6 %collective-permute-done.left_ref = f32[48,384]{1,0:T(8,128)S(1)} collective-permute-done((f32[48,384]{1,0:T(8,128)S(1)}, f32[48,384]{1,0:T(8,128)S(1)}, u32[]{:S(2)}, u32[]{:S(2)}) %collective-permute-start) | collective-permute-done | bytes 73760 | tf_op jit(solution)/shard_map/ppermute | solution.py:691
  17.6 0.0 collective-permute-done.1.right_ref
  17.6 0.4 shard_map.69
  18.0 1.9 %collective-permute-start.4 = (f32[5,48,384]{2,1,0:T(8,128)S(1)}, f32[5,48,384]{2,1,0:T(8,128)S(1)}, u32[]{:S(2)}, u32[]{:S(2)}) collective-permute-start(f32[5,48,384]{2,1,0:T(8,128)S(1)} %get-tuple-element.47), channel_id=1, source_target_pairs={{16,32},{48,64},{80,96},{112,128},{144,160},{176,192},{208,224},{2... | collective-permute-start | bytes 1105928 | tf_op jit(solution)/shard_map/ppermute | solution.py:691
  19.9 4.9 %collective-permute-start.6 = (f32[5,48,384]{2,1,0:T(8,128)S(1)}, f32[5,48,384]{2,1,0:T(8,128)S(1)}, u32[]{:S(2)}, u32[]{:S(2)}) collective-permute-start(f32[5,48,384]{2,1,0:T(8,128)S(1)} %get-tuple-element.49), channel_id=1, source_target_pairs={{0,16},{32,48},{64,80},{96,112},{128,144},{160,176},{192,208},{224... | collective-permute-start | bytes 1105928 | tf_op jit(solution)/shard_map/ppermute | solution.py:691
  24.8 0.0 copy-done.1
  24.8 0.0 collective-permute-done.2.low1
  24.8 2.8 %collective-permute-done.3.high1 = f32[9,48,384]{2,1,0:T(8,128)S(1)} collective-permute-done((f32[9,48,384]{2,1,0:T(8,128)S(1)}, f32[9,48,384]{2,1,0:T(8,128)S(1)}, u32[]{:S(2)}, u32[]{:S(2)}) %collective-permute-start.3) | collective-permute-done | bytes 663584 | tf_op jit(solution)/shard_map/ppermute | solution.py:691
  27.7 0.0 copy-done
  27.7 1.2 %shard_map.70 = (f32[6,48,384]{2,1,0:T(8,128)S(1)}, f32[6,48,384]{2,1,0:T(8,128)S(1)}, f32[4,6,48,512]{3,2,1,0:T(8,128)S(1)}, f32[6,48,512]{2,1,0:T(8,128)S(1)}, f32[4,48,512]{2,1,0:T(8,128)S(1)}) custom-call(s32[2]{0:T(128)S(1)} %copy-done, f32[4,6,48,384]{3,2,1,0:T(8,128)S(1)} %get-tuple-element.35.cur_ref, f32[6,48,384]{2,1,0:T(8,128)S(1)} %get-tuple-element.36.stiff_ref, ...), custom_call_target="tpu_custom_call" | custom-call | tf_op jit(solution)/shard_map/pallas_call | solution.py:678
  28.9 1.9 %collective-permute-start.5 = (f32[6,48,384]{2,1,0:T(8,128)S(1)}, f32[6,48,384]{2,1,0:T(8,128)S(1)}, u32[]{:S(2)}, u32[]{:S(2)}) collective-permute-start(f32[6,48,384]{2,1,0:T(8,128)S(1)} %get-tuple-element.48), channel_id=1, source_target_pairs={{16,32},{48,64},{80,96},{112,128},{144,160},{176,192},{208,224},{2... | collective-permute-start | bytes 1327112 | tf_op jit(solution)/shard_map/ppermute | solution.py:691
  30.8 5.3 %collective-permute-start.7 = (f32[6,48,384]{2,1,0:T(8,128)S(1)}, f32[6,48,384]{2,1,0:T(8,128)S(1)}, u32[]{:S(2)}, u32[]{:S(2)}) collective-permute-start(f32[6,48,384]{2,1,0:T(8,128)S(1)} %get-tuple-element.50), channel_id=1, source_target_pairs={{0,16},{32,48},{64,80},{96,112},{128,144},{160,176},{192,208},{224... | collective-permute-start | bytes 1327112 | tf_op jit(solution)/shard_map/ppermute | solution.py:691
  36.1 0.1 pad_maximum_fusion.1.table_ref
  36.3 0.0 collective-permute-done.4.low2
  36.3 0.0 collective-permute-done.6.high2
  36.3 2.3 %shard_map.71 = (f32[8,48,512]{2,1,0:T(8,128)S(1)}, f32[6,48,512]{2,1,0:T(8,128)S(1)}, f32[6,48,512]{2,1,0:T(8,128)S(1)}, f32[6,48,512]{2,1,0:T(8,128)S(1)}, f32...) custom-call(s32[2]{0:T(128)S(1)} %copy-done, f32[4,6,48,512]{3,2,1,0:T(8,128)S(1)} %get-tuple-element.44.own_ref, ...), custom_call_target="tpu_custom_call" | custom-call | tf_op jit(solution)/shard_map/pallas_call | solution.py:678
  38.6 1.9 %collective-permute-start.8 = (f32[7,48,128]{2,1,0:T(8,128)S(1)}, f32[7,48,128]{2,1,0:T(8,128)S(1)}, u32[]{:S(2)}, u32[]{:S(2)}) collective-permute-start(f32[7,48,128]{2,1,0:T(8,128)S(1)} %get-tuple-element.64), channel_id=1, source_target_pairs={{16,32},{48,64},{80,96},{112,128},{144,160},{176,192},{208,224},{2... | collective-permute-start | bytes 516104 | tf_op jit(solution)/shard_map/ppermute | solution.py:691
  40.5 5.9 %collective-permute-start.9 = (f32[7,48,128]{2,1,0:T(8,128)S(1)}, f32[7,48,128]{2,1,0:T(8,128)S(1)}, u32[]{:S(2)}, u32[]{:S(2)}) collective-permute-start(f32[7,48,128]{2,1,0:T(8,128)S(1)} %get-tuple-element.65), channel_id=1, source_target_pairs={{0,16},{32,48},{64,80},{96,112},{128,144},{160,176},{192,208},{224... | collective-permute-start | bytes 516104 | tf_op jit(solution)/shard_map/ppermute | solution.py:691
  46.4 0.0 collective-permute-done.5.low3
  46.4 0.0 collective-permute-done.7.high3
  46.4 4.6 %shard_map.72 = (f32[8,48,512]{2,1,0:T(8,128)S(1)}, f32[6,48,512]{2,1,0:T(8,128)S(1)}, f32[6,48,512]{2,1,0:T(8,128)S(1)}, f32[6,48,512]{2,1,0:T(8,128)S(1)}, f32...) custom-call(s32[2]{0:T(128)S(1)} %copy-done, ...), custom_call_target="tpu_custom_call" | custom-call | tf_op jit(solution)/shard_map/pallas_call | solution.py:678
  51.1 0.0 collective-permute-done.8.low_ref
  51.1 0.0 collective-permute-done.9.high_ref
  51.1 4.7 %shard_map.73 = (f32[4,6,48,384]{3,2,1,0:T(8,128)}, f32[4,48,2,128]{3,2,1,0:T(2,128)}) custom-call(s32[2]{0:T(128)S(1)} %copy-done, f32[8,48,512]{2,1,0:T(8,128)S(1)} %get-tuple-element.55.u_rim, f32[6,48,512]{2,1,0:T(8,128)S(1)} %get-tuple-element.56.v_rim, f32[6,48,512]{2,1,0:T(8,128)S(1)} %get-tuple-element.57.w_rim, ...), custom_call_target="tpu_custom_call" | custom-call | tf_op jit(solution)/shard_map/pallas_call | solution.py:678
  (3 shorter events, 0.0 us)
Async XLA Ops:
  3.4 21.4 %copy-start.1 = (f32[48,48]{1,0:T(8,128)S(1)}, f32[48,48]{1,0:T(8,128)}, u32[]{:S(2)}) copy-start(f32[48,48]{1,0:T(8,128)} %param.8) | copy-start | bytes 27652
  3.4 24.3 %copy-start = (s32[2]{0:T(128)S(1)}, s32[2]{0:T(128)}, u32[]{:S(2)}) copy-start(s32[2]{0:T(128)} %off_ref.9) | copy-start | bytes 28
  3.4 21.4 %collective-permute-start.2 = (f32[9,48,384]{2,1,0:T(8,128)S(1)}, f32[9,48,384]{2,1,0:T(8,128)S(1)}, u32[]{:S(2)}, u32[]{:S(2)}) collective-permute-start(f32[9,48,384]{2,1,0:T(8,128)S(1)} %get-tuple-element.42), channel_id=1, source_target_pairs={{16,32},{48,64},{80,96},{112,128},{144,160},{176,192},{208,224},{2... | collective-permute-start | bytes 1990664 | tf_op jit(solution)/shard_map/ppermute | solution.py:691
  5.9 21.8 %collective-permute-start.3 = (f32[9,48,384]{2,1,0:T(8,128)S(1)}, f32[9,48,384]{2,1,0:T(8,128)S(1)}, u32[]{:S(2)}, u32[]{:S(2)}) collective-permute-start(f32[9,48,384]{2,1,0:T(8,128)S(1)} %get-tuple-element.43), channel_id=1, source_target_pairs={{0,16},{32,48},{64,80},{96,112},{128,144},{160,176},{192,208},{224... | collective-permute-start | bytes 1990664 | tf_op jit(solution)/shard_map/ppermute | solution.py:691
  12.0 5.7 %collective-permute-start = (f32[48,384]{1,0:T(8,128)S(1)}, f32[48,384]{1,0:T(8,128)S(1)}, u32[]{:S(2)}, u32[]{:S(2)}) collective-permute-start(f32[48,384]{1,0:T(8,128)S(1)} %get-tuple-element.39), channel_id=1, source_target_pairs={{1,2},{3,4},{5,6},{7,8},{9,10},{11,12},{13,14},{2,1},{4,3},{6,5},{... | collective-permute-start | bytes 221192 | tf_op jit(solution)/shard_map/ppermute | solution.py:691
  14.1 3.5 %collective-permute-start.1 = (f32[48,384]{1,0:T(8,128)S(1)}, f32[48,384]{1,0:T(8,128)S(1)}, u32[]{:S(2)}, u32[]{:S(2)}) collective-permute-start(f32[48,384]{1,0:T(8,128)S(1)} %get-tuple-element.40), channel_id=1, source_target_pairs={{0,1},{2,3},{4,5},{6,7},{8,9},{10,11},{12,13},{14,15},{1,0},{3,2},... | collective-permute-start | bytes 221192 | tf_op jit(solution)/shard_map/ppermute | solution.py:691
  18.0 18.3 %collective-permute-start.4 = (f32[5,48,384]{2,1,0:T(8,128)S(1)}, f32[5,48,384]{2,1,0:T(8,128)S(1)}, u32[]{:S(2)}, u32[]{:S(2)}) collective-permute-start(f32[5,48,384]{2,1,0:T(8,128)S(1)} %get-tuple-element.47), channel_id=1, source_target_pairs={{16,32},{48,64},{80,96},{112,128},{144,160},{176,192},{208,224},{2... | collective-permute-start | bytes 1105928 | tf_op jit(solution)/shard_map/ppermute | solution.py:691
  19.9 16.3 %collective-permute-start.6 = (f32[5,48,384]{2,1,0:T(8,128)S(1)}, f32[5,48,384]{2,1,0:T(8,128)S(1)}, u32[]{:S(2)}, u32[]{:S(2)}) collective-permute-start(f32[5,48,384]{2,1,0:T(8,128)S(1)} %get-tuple-element.49), channel_id=1, source_target_pairs={{0,16},{32,48},{64,80},{96,112},{128,144},{160,176},{192,208},{224... | collective-permute-start | bytes 1105928 | tf_op jit(solution)/shard_map/ppermute | solution.py:691
  28.9 17.5 %collective-permute-start.5 = (f32[6,48,384]{2,1,0:T(8,128)S(1)}, f32[6,48,384]{2,1,0:T(8,128)S(1)}, u32[]{:S(2)}, u32[]{:S(2)}) collective-permute-start(f32[6,48,384]{2,1,0:T(8,128)S(1)} %get-tuple-element.48), channel_id=1, source_target_pairs={{16,32},{48,64},{80,96},{112,128},{144,160},{176,192},{208,224},{2... | collective-permute-start | bytes 1327112 | tf_op jit(solution)/shard_map/ppermute | solution.py:691
  30.8 15.6 %collective-permute-start.7 = (f32[6,48,384]{2,1,0:T(8,128)S(1)}, f32[6,48,384]{2,1,0:T(8,128)S(1)}, u32[]{:S(2)}, u32[]{:S(2)}) collective-permute-start(f32[6,48,384]{2,1,0:T(8,128)S(1)} %get-tuple-element.50), channel_id=1, source_target_pairs={{0,16},{32,48},{64,80},{96,112},{128,144},{160,176},{192,208},{224... | collective-permute-start | bytes 1327112 | tf_op jit(solution)/shard_map/ppermute | solution.py:691
  38.6 12.5 %collective-permute-start.8 = (f32[7,48,128]{2,1,0:T(8,128)S(1)}, f32[7,48,128]{2,1,0:T(8,128)S(1)}, u32[]{:S(2)}, u32[]{:S(2)}) collective-permute-start(f32[7,48,128]{2,1,0:T(8,128)S(1)} %get-tuple-element.64), channel_id=1, source_target_pairs={{16,32},{48,64},{80,96},{112,128},{144,160},{176,192},{208,224},{2... | collective-permute-start | bytes 516104 | tf_op jit(solution)/shard_map/ppermute | solution.py:691
  40.5 10.6 %collective-permute-start.9 = (f32[7,48,128]{2,1,0:T(8,128)S(1)}, f32[7,48,128]{2,1,0:T(8,128)S(1)}, u32[]{:S(2)}, u32[]{:S(2)}) collective-permute-start(f32[7,48,128]{2,1,0:T(8,128)S(1)} %get-tuple-element.65), channel_id=1, source_target_pairs={{0,16},{32,48},{64,80},{96,112},{128,144},{160,176},{192,208},{224... | collective-permute-start | bytes 516104 | tf_op jit(solution)/shard_map/ppermute | solution.py:691
